TPU v7x, 256 devices: a whole 4x4x8 slice. The times are simulated.
256 devices in a mesh: grp: 4 (over x), row: 16 (over y, z_hi), col: 4 (over z_lo, core).
Axes of the slice: x: 4, y: 4, z: 8 (z_hi: 4, z_lo: 2; z = z_hi * 2 + z_lo), core: 2. Of those that a mesh axis runs over, the one named last changes fastest.
Arguments:
- fields: float32 [5, 384, 64, 512], P(None, 'col', 'row', 'grp'), may hold values from -6 to 6
- lift_weight: float32 [32, 5], replicated, may hold values from -5 to 5
- mix_weight: float32 [32, 32], replicated, may hold values from -1 to 1
- project_weight: float32 [5, 32], replicated, may hold values from -1 to 1
- spectral_weight: bfloat16 [2, 64, 32, 32, 1024], P(None, 'grp', 'col', 'row'), may hold values from -1 to 1
Outputs:
- new_fields: float32 [5, 384, 64, 512], P(None, 'col', 'row', 'grp')
- weight_grad: bfloat16 [2, 64, 32, 32, 1024], P(None, 'grp', 'col', 'row')
All inputs are finite; a program needn't handle non-finite values.
Results may differ from a plain program's by a relative error of at most 0.006.
Values may be sent and summed in bfloat16 or wider, within the bound.
No kernel may reach another device: no remote copies, remote signals or barrier semaphores. Data moves between devices by JAX's collectives and lax.ppermute only.
A program may use at most 128 MiB of HBM per device.

v0:
```python
import math

import jax
import jax.numpy as jnp
from jax import lax
from jax.sharding import PartitionSpec as P

MODES = 32


ADVECT_RATE = 0.1
DIFFUSE_RATE = 0.12
FULL_PRECISION = lax.Precision.HIGHEST


def with_halo(x, sides, width):
    for axis, dim in sides:
        peers, length = (lax.axis_size(axis), x.shape[dim])
        up = [(i, (i + 1) % peers) for i in range(peers)]
        down = [(j, i) for i, j in up]
        last = lax.slice_in_dim(x, length - width, length, axis=dim)
        leading = lax.slice_in_dim(x, 0, width, axis=dim)
        before = lax.ppermute(last, axis, up)
        after = lax.ppermute(leading, axis, down)
        x = jnp.concatenate([before, x, after], axis=dim)
    return x


def from_behind(block, axis, distance):
    devices = range(lax.axis_size(axis))
    route = [(i - distance, i) for i in devices if i - distance in devices]
    return lax.ppermute(block, axis, route)


def advance(padded):
    center = padded[:, 1:-1, 1:-1, 1:-1]
    zplus = padded[:, 2:, 1:-1, 1:-1]
    zminus = padded[:, :-2, 1:-1, 1:-1]
    yplus = padded[:, 1:-1, 2:, 1:-1]
    yminus = padded[:, 1:-1, :-2, 1:-1]
    xplus = padded[:, 1:-1, 1:-1, 2:]
    xminus = padded[:, 1:-1, 1:-1, :-2]
    carried = (
        center[0:1] * (xplus - xminus)
        + center[1:2] * (yplus - yminus)
        + center[2:3] * (zplus - zminus)
    )
    spread = xplus + xminus + yplus + yminus + zplus + zminus - 6.0 * center
    return center - ADVECT_RATE * carried + DIFFUSE_RATE * spread


def close_walls(padded, group_index):
    columns = lax.broadcasted_iota(jnp.int32, (1, 1, 1, padded.shape[3]), 3)
    low_rim = jnp.logical_and(group_index == 0, columns < 1)
    high_rim = jnp.logical_and(group_index == 2, columns >= padded.shape[3] - 1)
    return jnp.where(jnp.logical_or(low_rim, high_rim), 0.0, padded)


def one_step(current, group_index):
    padded = with_halo(
        current.astype(jnp.bfloat16), (("grp", 3), ("row", 2), ("col", 1)), 1
    ).astype(current.dtype)
    return advance(close_walls(padded, group_index))


def coarsen(current):
    count_f, extent_z, extent_y, extent_x = current.shape
    blocks = current.reshape(count_f, extent_z // 2, 2, extent_y // 2, 2, extent_x // 2, 2)
    return jnp.mean(blocks, axis=(2, 4, 6))


def spectral_bins(kept, extent):
    positions = lax.broadcasted_iota(jnp.int32, (kept,), 0)
    return jnp.where(positions < kept // 2, positions, positions + extent - kept)


def phase(extent, frequency):
    positions = lax.broadcasted_iota(jnp.int32, (extent, frequency.shape[0]), 0)
    products = positions * frequency[None, :] % extent
    return 2.0 * math.pi / extent * products.astype(jnp.float32)


def real_table(extent, scaling):
    angles = phase(extent, lax.broadcasted_iota(jnp.int32, (scaling.shape[0],), 0))
    return jnp.stack([jnp.cos(angles) * scaling, -jnp.sin(angles) * scaling])


def forward_table(extent, kept):
    angles = phase(extent, spectral_bins(kept, extent))
    cosine = jnp.cos(angles)
    sine_part = jnp.sin(angles)
    return jnp.stack([jnp.stack([cosine, -sine_part], 1), jnp.stack([sine_part, cosine], 1)])


def inverse_table(extent, kept):
    angles = phase(extent, spectral_bins(kept, extent)).T
    cosine = jnp.cos(angles)
    sine_part = jnp.sin(angles)
    return jnp.stack([jnp.stack([cosine, sine_part], 1), jnp.stack([-sine_part, cosine], 1)])


def to_modes(cells_in, scaling):
    along_x = jnp.einsum(
        "czyx,pxk->pckyz",
        cells_in,
        real_table(cells_in.shape[3], scaling),
        precision=FULL_PRECISION,
    )
    gathered_y = lax.all_to_all(along_x, "row", split_axis=2, concat_axis=3, tiled=True)
    extent_y = gathered_y.shape[3]
    kept_y = min(2 * MODES, extent_y)
    along_y = jnp.einsum(
        "pcqyz,pyoj->ocqjz", gathered_y, forward_table(extent_y, kept_y), precision=FULL_PRECISION
    )
    gathered_z = lax.all_to_all(along_y, "col", split_axis=3, concat_axis=4, tiled=True)
    extent_z = gathered_z.shape[4]
    return jnp.einsum(
        "pcqjz,pzok->okjqc",
        gathered_z,
        forward_table(extent_z, 2 * MODES),
        precision=FULL_PRECISION,
    )


def to_cells(spectrum, scaling, extent_x, extent_y, extent_z):
    along_z = jnp.einsum(
        "pkjqc,pkoz->ocqjz", spectrum, inverse_table(extent_z, 2 * MODES), precision=FULL_PRECISION
    )
    spread_z = lax.all_to_all(along_z, "col", split_axis=4, concat_axis=3, tiled=True)
    kept_y = min(2 * MODES, extent_y)
    along_y = jnp.einsum(
        "pcqjz,pjoy->ocqyz", spread_z, inverse_table(extent_y, kept_y), precision=FULL_PRECISION
    )
    spread_y = lax.all_to_all(along_y, "row", split_axis=3, concat_axis=2, tiled=True)
    return jnp.einsum(
        "pckyz,pxk->czyx", spread_y, real_table(extent_x, scaling), precision=FULL_PRECISION
    )


def mix_modes(spectrum, weights, channels):
    weight_dims = weights.shape
    real_part = (
        weights[0]
        .reshape(weight_dims[1], weight_dims[2], weight_dims[3], channels, channels)
        .astype(jnp.float32)
    )
    imag_part = (
        weights[1]
        .reshape(weight_dims[1], weight_dims[2], weight_dims[3], channels, channels)
        .astype(jnp.float32)
    )
    out_real = jnp.einsum(
        "zyxi,zyxio->zyxo", spectrum[0], real_part, precision=FULL_PRECISION
    ) - jnp.einsum("zyxi,zyxio->zyxo", spectrum[1], imag_part, precision=FULL_PRECISION)
    out_imag = jnp.einsum(
        "zyxi,zyxio->zyxo", spectrum[0], imag_part, precision=FULL_PRECISION
    ) + jnp.einsum("zyxi,zyxio->zyxo", spectrum[1], real_part, precision=FULL_PRECISION)
    return jnp.stack([out_real, out_imag])


def gradient_terms(spectrum, back_modes):
    grad_real = jnp.einsum(
        "zyxi,zyxo->zyxio", spectrum[0], back_modes[0], precision=FULL_PRECISION
    ) + jnp.einsum("zyxi,zyxo->zyxio", spectrum[1], back_modes[1], precision=FULL_PRECISION)
    grad_imag = jnp.einsum(
        "zyxi,zyxo->zyxio", spectrum[0], back_modes[1], precision=FULL_PRECISION
    ) - jnp.einsum("zyxi,zyxo->zyxio", spectrum[1], back_modes[0], precision=FULL_PRECISION)
    return jnp.stack([grad_real, grad_imag])


def shards(fields, lift_weight, mix_weight, project_weight, spectral_weight):
    group_index = lax.axis_index("grp")
    stepped = one_step(one_step(fields, group_index), group_index)
    new_fields = jnp.where(group_index == 3, fields, stepped)
    start_snap = coarsen(fields)
    final_snap = coarsen(stepped)
    input_blocks = []
    target_blocks = []
    for offset in range(3, 0, -1):
        got_input, got_target = from_behind((start_snap, final_snap), "grp", offset)
        input_blocks.append(got_input)
        target_blocks.append(got_target)
    inputs = jnp.concatenate(input_blocks, axis=3)
    targets = jnp.concatenate(target_blocks, axis=3)
    extent_x = inputs.shape[3]
    extent_y = inputs.shape[2] * lax.axis_size("row")
    extent_z = inputs.shape[1] * lax.axis_size("col")
    cell_count = float(extent_x * extent_y * extent_z)
    frequency = lax.broadcasted_iota(jnp.int32, (MODES,), 0)
    plain_scale = jnp.full((MODES,), 1.0 / math.sqrt(cell_count), jnp.float32)
    doubled_scale = jnp.where(frequency == 0, 1.0, 2.0).astype(jnp.float32) / math.sqrt(cell_count)
    channels = lift_weight.shape[0]
    lifted = jnp.einsum("cf,fzyx->czyx", lift_weight, inputs, precision=FULL_PRECISION)
    spectrum = to_modes(lifted, plain_scale)
    weights = lax.all_gather(spectral_weight, "grp", axis=1, tiled=True)
    mixed_modes = mix_modes(spectrum, weights, channels)
    carried = to_cells(mixed_modes, doubled_scale, extent_x, extent_y, extent_z)
    preact = jnp.einsum("oc,czyx->ozyx", mix_weight, lifted, precision=FULL_PRECISION) + carried
    activated, gelu_back = jax.vjp(jax.nn.gelu, preact)
    predicted = inputs + jnp.einsum(
        "fc,czyx->fzyx", project_weight, activated, precision=FULL_PRECISION
    )
    misfit = predicted - targets
    back_act = jnp.einsum("fc,fzyx->czyx", project_weight, misfit, precision=FULL_PRECISION)
    back_preact = gelu_back(back_act)[0]
    back_modes = to_modes(back_preact, doubled_scale)
    term = gradient_terms(spectrum, back_modes).reshape(weights.shape)
    owned_term = jnp.where(group_index == 3, term, 0.0)
    weight_grad = lax.psum_scatter(
        owned_term.astype(jnp.bfloat16), "grp", scatter_dimension=1, tiled=True
    )
    return (new_fields, weight_grad)


def solution(mesh):
    placed = (P(None, "col", "row", "grp"), P(), P(), P(), P(None, "grp", "col", "row", None))
    return jax.shard_map(
        shards,
        mesh=mesh,
        in_specs=placed,
        out_specs=(P(None, "col", "row", "grp"), P(None, "grp", "col", "row", None)),
        check_vma=False,
    )
```

profile of v0, /device:TPU:1, one launch (start us, length us, event | category | flops | bytes accessed | tf_op | source)
XLA Modules:
  0.0 533.4 jit_solution(15918191539948757043)
XLA Ops:
  9.8 12.1 %copy.205 = f32[5,96,4,128]{0,3,2,1:T(8,128)} copy(f32[5,96,4,128]{3,2,1,0:T(4,128)S(1)} %copy-done.10) | data formatting | bytes 1966080 | tf_op args[0]
  22.0 16.8 %reduce_sum.18 = f32[5,48,2,64]{0,3,2,1:T(8,128)S(1)} reduce(f32[5,48,2,2,2,64,2]{0,6,5,4,3,2,1:T(2,128)} %bitcast.245, f32[]{:T(128)} %constant.95.clone.1), dimensions={2,4,6}, to_apply=%region_0.1 | reduce | flops 215040 | bytes 1105924 | tf_op jit(solution)/shard_map/reduce_sum | solution.py:69
  50.2 10.9 %collective-permute-done.14 = f32[5,48,2,64]{3,0,2,1:T(8,128)S(1)} collective-permute-done((f32[5,48,2,64]{3,0,2,1:T(8,128)S(1)}, f32[5,48,2,64]{3,0,2,1:T(8,128)S(1)}, u32[]{:S(2)}, u32[]{:S(2)}) %collective-permute-start.14) | collective-permute-done | bytes 122912 | tf_op jit(solution)/shard_map/ppermute | solution.py:32
  61.0 16.5 %collective-permute-done.13 = f32[5,48,2,64]{3,0,2,1:T(8,128)S(1)} collective-permute-done((f32[5,48,2,64]{3,0,2,1:T(8,128)S(1)}, f32[5,48,2,64]{3,0,2,1:T(8,128)S(1)}, u32[]{:S(2)}, u32[]{:S(2)}) %collective-permute-start.13) | collective-permute-done | bytes 122912 | tf_op jit(solution)/shard_map/ppermute | solution.py:32
  82.7 7.0 %fusion.30 = f32[2,32,32,2,48]{4,2,3,1,0:T(8,128)S(1)} fusion(f32[32,48,2,192]{3,0,2,1:T(8,128)S(1)} %convolution_bitcast_fusion, f32[1,192,32]{1,2,0:T(8,128)S(1)} %get-tuple-element.67, f32[1,192,32]{1,2,0:T(8,128)S(1)} %get-tuple-element.66), kind=kOutput, calls=%fused_computation.44 | convolution fusion | flops 452997120 | bytes 3194880 | tf_op jit(solution)/shard_map/czyx,pxk->pckyz/dot_general | solution.py:103
  96.1 10.0 %all-to-all-start = ((f32[16,1,12288]{2,1,0:T(1,128)}), f32[16,1,12288]{2,1,0:T(1,128)}, u32[]{:S(2)}, u32[]{:S(2)}) async-start(f32[16,1,12288]{2,1,0:T(1,128)} %reshape.561), calls=%async_computation | async-start | bytes 1572864 | tf_op jit(solution)/shard_map/all_to_all | solution.py:109
  113.7 5.5 %collective-permute-start.3 = (bf16[5,96,1,130]{1,3,2,0:T(8,128)(2,1)}, bf16[5,96,1,130]{1,3,2,0:T(8,128)(2,1)S(1)}, u32[]{:S(2)}, u32[]{:S(2)}) collective-permute-start(bf16[5,96,1,130]{1,3,2,0:T(8,128)(2,1)} %get-tuple-element.39), channel_id=1, source_target_pairs={{4,0},{8,4},{12,8},{16,12},{20,16},{24,20},{28,24},{32,28},{36,32}... | collective-permute-start | bytes 374408 | tf_op jit(solution)/shard_map/ppermute | solution.py:24
  119.3 11.3 %all-to-all-done = f32[16,1,12288]{2,1,0:T(1,128)} async-done(((f32[16,1,12288]{2,1,0:T(1,128)}), f32[16,1,12288]{2,1,0:T(1,128)}, u32[]{:S(2)}, u32[]{:S(2)}) %all-to-all-start) | async-done | bytes 786464 | tf_op jit(solution)/shard_map/all_to_all | solution.py:109
  147.2 5.5 %reshape.563 = f32[4,1,49152]{2,1,0:T(1,128)} reshape(f32[32,2,32,2,48]{4,3,2,1,0:T(2,128)} %bitcast.256) | data formatting | bytes 1572864
  152.8 7.4 %all-to-all-start.1 = ((f32[4,1,49152]{2,1,0:T(1,128)}), f32[4,1,49152]{2,1,0:T(1,128)S(1)}, u32[]{:S(2)}, u32[]{:S(2)}) async-start(f32[4,1,49152]{2,1,0:T(1,128)} %reshape.563), calls=%async_computation.1 | async-start | bytes 1572864 | tf_op jit(solution)/shard_map/all_to_all | solution.py:115
  182.3 5.9 %reshape.564 = f32[32,2,32,2,48]{4,3,2,1,0:T(2,128)} reshape(f32[4,49152]{1,0:T(4,128)} %reduce.9) | data formatting | bytes 1572864
  211.9 6.3 %fusion = (f32[64,8,2,32]{0,3,2,1:T(8,128)S(1)}, f32[64,8,2,32]{0,3,2,1:T(8,128)S(1)}, f32[64,8,2,32]{0,3,2,1:T(8,128)S(1)}, f32[64,8,2,32]{0,3,2,1:T(8,128)S(1)}) fusion(bf16[64,8,2,32,32]{0,4,3,2,1:T(8,128)(2,1)} %bitcast.246, bf16[64,8,2,32,32]{0,4,3,2,1:T(8,128)(2,1)} %bitcast.247, f32[64,8,2,32]{0,3,1,2:T(8,128)S(1)} %get-tuple-element.46, ...), kind=kLoop, calls=%fused_computation.4 | loop fusion | flops 10354688 | bytes 4980736 | tf_op jit(solution)/shard_map/zyxi,zyxio->zyxo/dot_general | solution.py:152
  223.1 5.5 %reshape.565 = f32[4,1,49152]{2,1,0:T(1,128)} reshape(f32[192,2,8,2,32]{4,3,2,1,0:T(2,128)} %bitcast.251) | data formatting | bytes 1572864
  246.2 5.8 %collective-permute-done.9 = bf16[5,96,1,130]{1,3,2,0:T(8,128)(2,1)S(1)} collective-permute-done((bf16[5,96,1,130]{1,3,2,0:T(8,128)(2,1)S(1)}, bf16[5,96,1,130]{1,3,2,0:T(8,128)(2,1)S(1)}, u32[]{:S(2)}, u32[]{:S(2)}) %collective-permute-start.9) | collective-permute-done | bytes 124832 | tf_op jit(solution)/shard_map/ppermute | solution.py:24
  281.0 6.1 %reshape.567 = f32[16,1,12288]{2,1,0:T(1,128)} reshape(f32[32,2,32,2,48]{4,3,2,1,0:T(2,128)} %bitcast.259) | data formatting | bytes 1572864
  303.5 14.3 %copy.224 = f32[5,96,4,128]{0,3,2,1:T(8,128)} copy(f32[5,96,4,128]{1,3,2,0:T(8,128)S(1)} %get-tuple-element.21) | data formatting | bytes 1966080 | tf_op jit(solution)/shard_map/add | solution.py:49
  317.8 16.8 %reduce_sum.19 = f32[5,48,2,64]{0,3,2,1:T(8,128)S(1)} reduce(f32[5,48,2,2,2,64,2]{0,6,5,4,3,2,1:T(2,128)} %bitcast.244, f32[]{:T(128)} %constant.95.clone.1), dimensions={2,4,6}, to_apply=%region_1.2 | reduce | flops 215040 | bytes 1105924 | tf_op jit(solution)/shard_map/reduce_sum | solution.py:69
  338.8 5.3 %collective-permute-start.16 = (f32[5,48,2,64]{3,0,2,1:T(8,128)}, f32[5,48,2,64]{3,0,2,1:T(8,128)}, u32[]{:S(2)}, u32[]{:S(2)}) collective-permute-start(f32[5,48,2,64]{3,0,2,1:T(8,128)} %broadcast_multiply_fusion), channel_id=1, source_target_pairs={{0,128},{64,192},{1,129},{65,193},{2,130},{66,194},{3,131},{67,195... | collective-permute-start | bytes 368648 | tf_op jit(solution)/shard_map/ppermute | solution.py:32
  355.1 5.5 %copy.223 = f32[2,32,32,2,48]{2,1,0,3,4:T(8,128)} copy(f32[2,32,32,2,48]{4,1,3,2,0:T(8,128)} %bitcast.262) | data formatting | bytes 1572864 | tf_op jit(solution)/shard_map/all_to_all | solution.py:134
  374.4 7.2 %fusion.33 = f32[2,32,32,2,48]{4,2,3,1,0:T(8,128)S(1)} fusion(f32[32,48,2,192]{3,0,2,1:T(8,128)S(1)} %fusion.10, f32[1,192,32]{1,2,0:T(8,128)S(1)} %copy-done.39, f32[1,192,32]{1,2,0:T(8,128)S(1)} %copy-done.38), kind=kOutput, calls=%fused_computation.45 | convolution fusion | flops 452997120 | bytes 3194880 | tf_op jit(solution)/shard_map/czyx,pxk->pckyz/dot_general | solution.py:103
  386.6 32.6 %all_to_all.108 = f32[16,1,12288]{2,1,0:T(1,128)S(1)} all-to-all(f32[16,1,12288]{2,1,0:T(1,128)S(1)} %reshape.569), channel_id=1, replica_groups=mesh['grp'=4,'row'=16,'col'=4] {'row'}, dimensions={0} | all-to-all | bytes 1572864 | tf_op jit(solution)/shard_map/all_to_all | solution.py:109
  433.5 14.7 %all_to_all.109 = f32[4,1,49152]{2,1,0:T(1,128)S(1)} all-to-all(f32[4,1,49152]{2,1,0:T(1,128)S(1)} %reshape.571), channel_id=1, replica_groups=mesh['grp'=4,'row'=16,'col'=4] {'col'}, dimensions={0} | all-to-all | bytes 1572864 | tf_op jit(solution)/shard_map/all_to_all | solution.py:115
  469.9 5.7 %copy.234 = bf16[1,64,8,2,1024]{4,2,3,1,0:T(8,128)(2,1)} copy(bf16[1,64,8,2,1024]{1,4,3,2,0:T(8,128)(2,1)} %bitcast.248) | data formatting | bytes 4194304 | tf_op jit(solution)/shard_map/stack | solution.py:168
  483.0 40.0 %reduce-scatter.2.cloned.1.call-done = bf16[2,16,8,2,1024]{4,2,3,0,1:T(8,128)(2,1)} async-done(((bf16[2,64,8,2,1024]{4,2,3,0,1:T(8,128)(2,1)}), bf16[2,16,8,2,1024]{4,2,3,0,1:T(8,128)(2,1)}) %reduce-scatter.2.cloned.1.call-update) | async-done | bytes 1048592 | tf_op jit(solution)/shard_map/reduce_scatter | solution.py:209
  (234 shorter events, 243.1 us)
Async XLA Ops:
  7.2 189.0 %all-gather.2.cloned.1.call-start = ((), (), s32[]{:S(2)}) async-start(), calls=%async_computation.7 | async-start | bytes 5242880 | tf_op jit(solution)/shard_map/all_gather | solution.py:195
  40.2 20.9 %collective-permute-start.14 = (f32[5,48,2,64]{3,0,2,1:T(8,128)S(1)}, f32[5,48,2,64]{3,0,2,1:T(8,128)S(1)}, u32[]{:S(2)}, u32[]{:S(2)}) collective-permute-start(f32[5,48,2,64]{3,0,2,1:T(8,128)S(1)} %broadcast_multiply_fusion.1), channel_id=1, source_target_pairs={{0,64},{64,128},{128,192},{1,65},{65,129},{129,193},{2,66},{66,130... | collective-permute-start | bytes 368648 | tf_op jit(solution)/shard_map/ppermute | solution.py:32
  44.1 33.4 %collective-permute-start.13 = (f32[5,48,2,64]{3,0,2,1:T(8,128)S(1)}, f32[5,48,2,64]{3,0,2,1:T(8,128)S(1)}, u32[]{:S(2)}, u32[]{:S(2)}) collective-permute-start(f32[5,48,2,64]{3,0,2,1:T(8,128)S(1)} %broadcast_multiply_fusion.1), channel_id=1, source_target_pairs={{0,128},{64,192},{1,129},{65,193},{2,130},{66,194},{3,131},{67,195... | collective-permute-start | bytes 368648 | tf_op jit(solution)/shard_map/ppermute | solution.py:32
  48.5 29.1 %collective-permute-start.12 = (f32[5,48,2,64]{3,0,2,1:T(8,128)S(1)}, f32[5,48,2,64]{3,0,2,1:T(8,128)S(1)}, u32[]{:S(2)}, u32[]{:S(2)}) collective-permute-start(f32[5,48,2,64]{3,0,2,1:T(8,128)S(1)} %broadcast_multiply_fusion.1), channel_id=1, source_target_pairs={{0,192},{1,193},{2,194},{3,195},{4,196},{5,197},{6,198},{7,199},{8... | collective-permute-start | bytes 368648 | tf_op jit(solution)/shard_map/ppermute | solution.py:32
  96.1 34.5 %all-to-all-start = ((f32[16,1,12288]{2,1,0:T(1,128)}), f32[16,1,12288]{2,1,0:T(1,128)}, u32[]{:S(2)}, u32[]{:S(2)}) async-start(f32[16,1,12288]{2,1,0:T(1,128)} %reshape.561), calls=%async_computation | async-start | bytes 1572864 | tf_op jit(solution)/shard_map/all_to_all | solution.py:109
  107.3 3.8 collective-permute-start.1
  108.4 4.5 collective-permute-start
  113.7 47.2 %collective-permute-start.3 = (bf16[5,96,1,130]{1,3,2,0:T(8,128)(2,1)}, bf16[5,96,1,130]{1,3,2,0:T(8,128)(2,1)S(1)}, u32[]{:S(2)}, u32[]{:S(2)}) collective-permute-start(bf16[5,96,1,130]{1,3,2,0:T(8,128)(2,1)} %get-tuple-element.39), channel_id=1, source_target_pairs={{4,0},{8,4},{12,8},{16,12},{20,16},{24,20},{28,24},{32,28},{36,32}... | collective-permute-start | bytes 374408 | tf_op jit(solution)/shard_map/ppermute | solution.py:24
  119.3 41.6 %collective-permute-start.2 = (bf16[5,96,1,130]{1,3,2,0:T(8,128)(2,1)}, bf16[5,96,1,130]{1,3,2,0:T(8,128)(2,1)S(1)}, u32[]{:S(2)}, u32[]{:S(2)}) collective-permute-start(bf16[5,96,1,130]{1,3,2,0:T(8,128)(2,1)} %get-tuple-element.38), channel_id=1, source_target_pairs={{0,4},{4,8},{8,12},{12,16},{16,20},{20,24},{24,28},{28,32},{32,36}... | collective-permute-start | bytes 374408 | tf_op jit(solution)/shard_map/ppermute | solution.py:23
  152.8 25.8 %all-to-all-start.1 = ((f32[4,1,49152]{2,1,0:T(1,128)}), f32[4,1,49152]{2,1,0:T(1,128)S(1)}, u32[]{:S(2)}, u32[]{:S(2)}) async-start(f32[4,1,49152]{2,1,0:T(1,128)} %reshape.563), calls=%async_computation.1 | async-start | bytes 1572864 | tf_op jit(solution)/shard_map/all_to_all | solution.py:115
  164.5 7.2 %collective-permute-start.5 = (bf16[5,1,6,130]{3,2,1,0:T(8,128)(2,1)}, bf16[5,1,6,130]{3,2,1,0:T(8,128)(2,1)S(1)}, u32[]{:S(2)}, u32[]{:S(2)}) collective-permute-start(bf16[5,1,6,130]{3,2,1,0:T(8,128)(2,1)} %copy.195), channel_id=1, source_target_pairs={{1,0},{2,1},{3,2},{0,3},{5,4},{6,5},{7,6},{4,7},{9,8},{10,9},{11,1... | collective-permute-start | bytes 23408 | tf_op jit(solution)/shard_map/ppermute | solution.py:24
  165.5 7.6 %collective-permute-start.4 = (bf16[5,1,6,130]{3,2,1,0:T(8,128)(2,1)S(1)}, bf16[5,1,6,130]{3,2,1,0:T(8,128)(2,1)S(1)}, u32[]{:S(2)}, u32[]{:S(2)}) collective-permute-start(bf16[5,1,6,130]{3,2,1,0:T(8,128)(2,1)S(1)} %copy.194), channel_id=1, source_target_pairs={{0,1},{1,2},{2,3},{3,0},{4,5},{5,6},{6,7},{7,4},{8,9},{9,10},{10,1... | collective-permute-start | bytes 23408 | tf_op jit(solution)/shard_map/ppermute | solution.py:23
  228.5 33.8 %all-to-all-start.2 = ((f32[4,1,49152]{2,1,0:T(1,128)}), f32[4,1,49152]{2,1,0:T(1,128)S(1)}, u32[]{:S(2)}, u32[]{:S(2)}) async-start(f32[4,1,49152]{2,1,0:T(1,128)} %reshape.565), calls=%async_computation.2 | async-start | bytes 1572864 | tf_op jit(solution)/shard_map/all_to_all | solution.py:129
  235.3 2.9 collective-permute-start.7
  235.4 7.1 %collective-permute-start.6 = (bf16[5,96,4,1]{1,3,2,0:T(2,128)(2,1)S(1)}, bf16[5,96,4,1]{1,3,2,0:T(2,128)(2,1)S(1)}, u32[]{:S(2)}, u32[]{:S(2)}) collective-permute-start(bf16[5,96,4,1]{1,3,2,0:T(2,128)(2,1)S(1)} %get-tuple-element.40), channel_id=1, source_target_pairs={{0,64},{64,128},{128,192},{192,0},{1,65},{65,129},{129,193},{193,1... | collective-permute-start | bytes 11528 | tf_op jit(solution)/shard_map/ppermute | solution.py:23
  242.6 9.5 %collective-permute-start.9 = (bf16[5,96,1,130]{1,3,2,0:T(8,128)(2,1)S(1)}, bf16[5,96,1,130]{1,3,2,0:T(8,128)(2,1)S(1)}, u32[]{:S(2)}, u32[]{:S(2)}) collective-permute-start(bf16[5,96,1,130]{1,3,2,0:T(8,128)(2,1)S(1)} %get-tuple-element.37), channel_id=1, source_target_pairs={{4,0},{8,4},{12,8},{16,12},{20,16},{24,20},{28,24},{32,28},{36,32}... | collective-permute-start | bytes 374408 | tf_op jit(solution)/shard_map/ppermute | solution.py:24
  243.1 13.0 %collective-permute-start.8 = (bf16[5,96,1,130]{1,3,2,0:T(8,128)(2,1)S(1)}, bf16[5,96,1,130]{1,3,2,0:T(8,128)(2,1)S(1)}, u32[]{:S(2)}, u32[]{:S(2)}) collective-permute-start(bf16[5,96,1,130]{1,3,2,0:T(8,128)(2,1)S(1)} %get-tuple-element.36), channel_id=1, source_target_pairs={{0,4},{4,8},{8,12},{12,16},{16,20},{20,24},{24,28},{28,32},{32,36}... | collective-permute-start | bytes 374408 | tf_op jit(solution)/shard_map/ppermute | solution.py:23
  259.0 37.1 %collective-permute-start.11 = (bf16[5,1,6,130]{3,2,1,0:T(8,128)(2,1)}, bf16[5,1,6,130]{3,2,1,0:T(8,128)(2,1)}, u32[]{:S(2)}, u32[]{:S(2)}) collective-permute-start(bf16[5,1,6,130]{3,2,1,0:T(8,128)(2,1)} %copy.199), channel_id=1, source_target_pairs={{1,0},{2,1},{3,2},{0,3},{5,4},{6,5},{7,6},{4,7},{9,8},{10,9},{11,1... | collective-permute-start | bytes 23408 | tf_op jit(solution)/shard_map/ppermute | solution.py:24
  260.9 36.6 %collective-permute-start.10 = (bf16[5,1,6,130]{3,2,1,0:T(8,128)(2,1)}, bf16[5,1,6,130]{3,2,1,0:T(8,128)(2,1)}, u32[]{:S(2)}, u32[]{:S(2)}) collective-permute-start(bf16[5,1,6,130]{3,2,1,0:T(8,128)(2,1)} %copy.198), channel_id=1, source_target_pairs={{0,1},{1,2},{2,3},{3,0},{4,5},{5,6},{6,7},{7,4},{8,9},{9,10},{10,1... | collective-permute-start | bytes 23408 | tf_op jit(solution)/shard_map/ppermute | solution.py:23
  287.1 59.1 %all-to-all-start.3 = ((f32[16,1,12288]{2,1,0:T(1,128)}), f32[16,1,12288]{2,1,0:T(1,128)}, u32[]{:S(2)}, u32[]{:S(2)}) async-start(f32[16,1,12288]{2,1,0:T(1,128)} %reshape.567), calls=%async_computation.3 | async-start | bytes 1572864 | tf_op jit(solution)/shard_map/all_to_all | solution.py:134
  291.4 231.6 %reduce-scatter.2.cloned.1.call-start = ((), (), s32[]{:S(2)}) async-start(), calls=%async_computation.8 | async-start | bytes 5242880 | tf_op jit(solution)/shard_map/reduce_scatter | solution.py:209
  336.8 28.9 %collective-permute-start.17 = (f32[5,48,2,64]{3,0,2,1:T(8,128)}, f32[5,48,2,64]{3,0,2,1:T(8,128)}, u32[]{:S(2)}, u32[]{:S(2)}) collective-permute-start(f32[5,48,2,64]{3,0,2,1:T(8,128)} %broadcast_multiply_fusion), channel_id=1, source_target_pairs={{0,64},{64,128},{128,192},{1,65},{65,129},{129,193},{2,66},{66,130... | collective-permute-start | bytes 368648 | tf_op jit(solution)/shard_map/ppermute | solution.py:32
  338.8 26.8 %collective-permute-start.16 = (f32[5,48,2,64]{3,0,2,1:T(8,128)}, f32[5,48,2,64]{3,0,2,1:T(8,128)}, u32[]{:S(2)}, u32[]{:S(2)}) collective-permute-start(f32[5,48,2,64]{3,0,2,1:T(8,128)} %broadcast_multiply_fusion), channel_id=1, source_target_pairs={{0,128},{64,192},{1,129},{65,193},{2,130},{66,194},{3,131},{67,195... | collective-permute-start | bytes 368648 | tf_op jit(solution)/shard_map/ppermute | solution.py:32
  344.2 21.5 %collective-permute-start.15 = (f32[5,48,2,64]{3,0,2,1:T(8,128)}, f32[5,48,2,64]{3,0,2,1:T(8,128)}, u32[]{:S(2)}, u32[]{:S(2)}) collective-permute-start(f32[5,48,2,64]{3,0,2,1:T(8,128)} %broadcast_multiply_fusion), channel_id=1, source_target_pairs={{0,192},{1,193},{2,194},{3,195},{4,196},{5,197},{6,198},{7,199},{8... | collective-permute-start | bytes 368648 | tf_op jit(solution)/shard_map/ppermute | solution.py:32
  (49 other events, 755.2 us)
Sparse Core Ops, SparseCore 0:
  10.4 67.8 all-gather.1
  480.4 42.5 reduce-scatter.1
where the time goes:
time: 538 us; the launch traced here: 533 us
  local copies, waits for them, and re-layouts  180 us (33%)
  waiting for transfers between devices  100 us (19%)
  other arithmetic  83.9 us (16%)
  starting transfers between devices  60 us (11%)
  blocking collectives  47.3 us (9%)
  matrix products  46 us (9%)
  between operations  15.3 us (3%)
    unnamed x117, local copies, waits for them, and re-layouts  89.4 us
    reduce_scatter x1, waiting for transfers between devices, shards(): lax.psum_scatter(owned_term.astype(jnp.bfloat16), 'grp', scatter_dimensio...  40 us
    reduce_sum x2, other arithmetic, coarsen(): return jnp.mean(blocks, axis=(2, 4, 6))  33.7 us
    all_to_all x1, blocking collectives, to_modes(): lax.all_to_all(along_x, 'row', split_axis=2, concat_axis=3, tiled=True)  32.6 us
    ppermute x6, waiting for transfers between devices, from_behind(): return lax.ppermute(block, axis, route)  27.4 us
    ppermute x6, starting transfers between devices, from_behind(): return lax.ppermute(block, axis, route)  19.3 us
    all_to_all x1, blocking collectives, to_modes(): lax.all_to_all(along_y, 'col', split_axis=3, concat_axis=4, tiled=True)  14.7 us
    add x1, local copies, waits for them, and re-layouts, advance(): return center - ADVECT_RATE * carried + DIFFUSE_RATE * spread  14.3 us
  transfers between devices with their start and end apart: 24, of which 10 were waited for; matrix products, arithmetic and copies ran while one was open for 38% of the time, Pallas kernels for 0%

commit v1 on v0

v1 whole, which is shorter than its diff:
```python
import functools
import math

import jax
import jax.numpy as jnp
import ml_dtypes
import numpy as np
from jax import lax
from jax.experimental import pallas as pl
from jax.experimental.pallas import tpu as pltpu
from jax.sharding import PartitionSpec as P

GX, GY, GZ = 192, 32, 192
KX, KY, KZ = 32, 32, 64
F, C = 5, 32
ADVECT_RATE = 0.1
DIFFUSE_RATE = 0.12
NORM = 1.0 / math.sqrt(GX * GY * GZ)
BF, F32 = jnp.bfloat16, jnp.float32
VMEM_LIMIT = 40 * 1024 * 1024


def freq(kept, extent):
    j = np.arange(kept)
    return np.where(j < kept // 2, j, j - kept)


FZ, FY = freq(KZ, GZ), freq(KY, GY)


def hilo(table):
    table = np.asarray(table, np.float32)
    high = table.astype(ml_dtypes.bfloat16)
    low = (table - high.astype(np.float32)).astype(ml_dtypes.bfloat16)
    return np.stack([high, low])


@functools.lru_cache(None)
def table_x_partial():
    out = np.zeros((4, 16, 2, 2, 2, 2, 128))
    x = np.arange(128) // 2
    for g in range(3):
        for kx in range(KX):
            angle = 2 * np.pi * ((kx * (64 * g + x)) % GX) / GX
            for y in range(2):
                out[g, kx // 2, y, kx % 2, 0, y] = np.cos(angle) * NORM / 8
                out[g, kx // 2, y, kx % 2, 1, y] = -np.sin(angle) * NORM / 8
    return np.moveaxis(hilo(out.reshape(4, 128, 256)), 0, 1)


def y_forward(rows, columns):
    p, kx, ky = (np.asarray(v)[:, None] for v in rows)
    q, jx, y = (np.asarray(v)[None, :] for v in columns)
    angle = 2 * np.pi * ((FY[ky] * y) % GY) / GY
    part = np.where(p == q, np.cos(angle), np.where(p == 0, np.sin(angle), -np.sin(angle)))
    return hilo(np.where(kx == jx, part, 0.0))


def index_of(*sizes):
    return [v.reshape(-1) for v in np.meshgrid(*[np.arange(s) for s in sizes], indexing="ij")]


@functools.lru_cache(None)
def table_y_first():
    p, ky, kx = index_of(2, 32, 2)
    r, y, jx, q = index_of(16, 2, 2, 2)
    return y_forward((p, kx, ky), (q, jx, 2 * r + y))


@functools.lru_cache(None)
def table_y_back():
    p, kx, ky = index_of(2, 2, 32)
    r, jx, q, y = index_of(16, 2, 2, 2)
    return y_forward((p, kx, ky), (q, jx, 2 * r + y))


@functools.lru_cache(None)
def table_z_first():
    out = np.zeros((2, 256, 4, 256))
    z = np.arange(48)
    for kz in range(KZ):
        angle = 2 * np.pi * ((FZ[kz] * z) % GZ) / GZ
        for f in range(F):
            lane = f * 32 + (kz % 16) * 2
            rows = slice(f * 48, f * 48 + 48)
            out[0, rows, kz // 16, lane] = np.cos(angle)
            out[0, rows, kz // 16, lane + 1] = -np.sin(angle)
            out[1, rows, kz // 16, lane] = np.sin(angle)
            out[1, rows, kz // 16, lane + 1] = np.cos(angle)
    return np.moveaxis(hilo(out.reshape(2, 256, 1024)), 0, 1)


@functools.lru_cache(None)
def table_select():
    out = np.zeros((4, 256, 2, 256), np.float32)
    for c in range(4):
        for kz in range(16):
            turn = (kz * c) % 4
            re = ((0, 1.0), (1, 1.0), (0, -1.0), (1, -1.0))[turn]
            im = ((1, 1.0), (0, -1.0), (1, -1.0), (0, 1.0))[turn]
            for f in range(F):
                row = f * 32 + kz * 2
                out[c, row + re[0], 0, f * 32 : f * 32 + 32] = re[1]
                out[c, row + im[0], 1, f * 32 : f * 32 + 32] = im[1]
    return out.reshape(1024, 512).astype(ml_dtypes.bfloat16)


@functools.lru_cache(None)
def table_sum_fields():
    out = np.zeros((2, 8, 32, 2, 2, 32), np.float32)
    for o in range(C):
        for p in range(2):
            out[p, :F, o, p, :, o] = 1.0
    return out.reshape(512, 128).astype(ml_dtypes.bfloat16)


@functools.lru_cache(None)
def table_z_inverse():
    g2, c2, zi = index_of(4, 4, 12)
    z = 48 * c2 + 12 * g2 + zi
    out = np.zeros((4, 192, 32))
    for g in range(4):
        for k in range(16):
            angle = 2 * np.pi * ((FZ[16 * g + k] * z) % GZ) / GZ
            out[g, :, k] = np.cos(angle)
            out[g, :, 16 + k] = np.sin(angle)
    return np.moveaxis(hilo(out), 0, 1)


@functools.lru_cache(None)
def table_lanes():
    out = np.zeros((4, 4, 32, 4, 4, 32), np.float32)
    for a in range(4):
        for b in range(4):
            for o in range(C):
                out[a, b, o, b, a, o] = 1.0
    return out.reshape(512, 512).astype(ml_dtypes.bfloat16)


@functools.lru_cache(None)
def table_y_inverse():
    r, kx, p, y = (v[:, None] for v in index_of(16, 2, 2, 2))
    q, jx, _, ky = (v[None, :] for v in index_of(2, 2, 4, 32))
    angle = 2 * np.pi * ((FY[ky] * (2 * r + y)) % GY) / GY
    part = np.where(p == q, np.cos(angle), np.where(p == 0, -np.sin(angle), np.sin(angle)))
    return hilo(np.where(kx == jx, part, 0.0))


@functools.lru_cache(None)
def table_x_inverse():
    g, y, x = (v[:, None] for v in index_of(3, 2, 64))
    r, kx, p, yy = (v[None, :] for v in index_of(16, 2, 2, 2))
    k = 2 * r + kx
    angle = 2 * np.pi * ((k * (64 * g + x)) % GX) / GX
    part = np.where(p == 0, np.cos(angle), -np.sin(angle)) * np.where(k == 0, 1.0, 2.0) * NORM
    return hilo(np.where(y == yy, part, 0.0))


@functools.lru_cache(None)
def table_x_back():
    return np.ascontiguousarray(np.swapaxes(table_x_inverse(), 1, 2))


@functools.lru_cache(None)
def table_z_back():
    out = np.zeros((4, 4, KZ, 2, 16))
    zi = np.arange(12)
    for c in range(4):
        for g in range(4):
            z = 48 * c + 12 * g + zi
            angle = 2 * np.pi * ((FZ[:, None] * z[None, :]) % GZ) / GZ
            out[c, g, :, 0, :12] = np.cos(angle)
            out[c, g, :, 1, :12] = np.sin(angle)
    return np.moveaxis(hilo(out.reshape(16, KZ, 32)), 0, 1)


@functools.lru_cache(None)
def table_pool_x():
    out = np.zeros((2, 64, 2, 128), np.float32)
    for x in range(128):
        for y in range(2):
            out[y, x // 2, y, x] = 0.125
    return out.reshape(128, 256).astype(ml_dtypes.bfloat16)


@functools.lru_cache(None)
def table_expand():
    out = np.zeros((2, 2, 2, 32, 2, 32, 32), np.float32)
    for o in range(C):
        for p in range(2):
            out[:, p, :, o, p, :, o] = 1.0
    return out.reshape(256, 2048).astype(ml_dtypes.bfloat16)


def dot(a, b, dims=((1,), (0,))):
    return lax.dot_general(a, b, (dims, ((), ())), preferred_element_type=F32)


def exact_dot(a, b, dims=((1,), (0,))):
    return lax.dot_general(
        a, b, (dims, ((), ())), preferred_element_type=F32, precision=lax.Precision.HIGHEST
    )


def split(x):
    high = x.astype(BF)
    return high, (x - high.astype(F32)).astype(BF)


def table_dot(table, x):
    return dot(table[0], x) + dot(table[1], x)


def table_dot3(table, x, dims=((1,), (0,))):
    high, low = split(x)
    return dot(table[0], high, dims) + dot(table[0], low, dims) + dot(table[1], high, dims)


def dot3(x, y):
    xh, xl = split(x)
    yh, yl = split(y)
    return dot(xh, yh) + dot(xl, yh) + dot(xh, yl)


def iota(shape, dim):
    return lax.broadcasted_iota(jnp.int32, shape, dim)


def call(body, outs, *args, scratch=(), cost=(0, 0)):
    single = not isinstance(outs, (list, tuple))
    shapes = [outs] if single else list(outs)
    vmem = pl.BlockSpec(memory_space=pltpu.VMEM)
    result = pl.pallas_call(
        body,
        out_shape=shapes,
        in_specs=[vmem] * len(args),
        out_specs=[vmem] * len(shapes),
        scratch_shapes=list(scratch),
        compiler_params=pltpu.CompilerParams(vmem_limit_bytes=VMEM_LIMIT),
    )(*args)
    return result[0] if single else result


def shape(dims, dtype):
    return jax.ShapeDtypeStruct(dims, dtype)


def pooled_rows(ref, f):
    rows = [ref[f, pl.ds(j, 48, stride=8), :] for j in range(8)]
    low = (rows[0] + rows[1]) + (rows[4] + rows[5])
    high = (rows[2] + rows[3]) + (rows[6] + rows[7])
    return low, high


def first_x_kernel(fields, table, out, rows):
    g = lax.axis_index("grp")
    rows[240:256, :] = jnp.zeros((16, 256), F32)
    for f in range(F):
        low, high = pooled_rows(fields, f)
        rows[f * 48 : f * 48 + 48, 0:128] = low
        rows[f * 48 : f * 48 + 48, 128:256] = high
    picked = table[g]
    result = table_dot3(picked, rows[...], ((1,), (1,)))
    out[...] = result.reshape(16, 8, 256)


def first_yz_kernel(got, ty, tz, out):
    both = table_dot3(ty, got[...].reshape(128, 256))
    result = dot3_table(both[:64], tz[0]) + dot3_table(both[64:], tz[1])
    for g in range(4):
        for c in range(4):
            out[g * 4 + c] = result[c * 16 : c * 16 + 16, g * 256 : g * 256 + 256]


def dot3_table(x, table):
    high, low = split(x)
    return dot(high, table[0]) + dot(low, table[0]) + dot(high, table[1])


def mix_kernel(got, weights, select, sum_fields, tz, out, spread_out, cells):
    g = lax.axis_index("grp")
    blocks = []
    for c in range(4):
        total = got[c]
        for src in range(1, 4):
            total = total + got[src * 4 + c]
        blocks.append(total)
    wide = jnp.concatenate(blocks, axis=1)
    wide = jnp.broadcast_to(wide[None], (16, 16, 1024)).reshape(256, 1024)
    own = iota((256, 1024), 0) // 16 == (iota((256, 1024), 1) // 2) % 16
    wide = jnp.where(own, wide, 0.0)
    high, low = split(wide)
    spread = dot(high, select[...]) + dot(low, select[...])
    spread_out[...] = spread
    sr, si = spread[:, :256], spread[:, 256:]
    wr, wi = weights[0], weights[1]
    mixed = jnp.concatenate([sr * wr - si * wi, sr * wi + si * wr], axis=1)
    high, low = split(mixed)
    modes = dot(high, sum_fields[...]) + dot(low, sum_fields[...])
    sign = jnp.where(iota((256, 128), 1) < 64, -1.0, 1.0)
    turned = pltpu.roll(modes, 64, 1) * sign
    cells[0:256, :] = modes
    cells[256:512, :] = turned
    first = (iota((16, 128), 1) // 32) % 2 == 0
    columns = []
    for ky in range(8):
        parts = []
        for part in range(2):
            a = cells[pl.ds(256 * part + 2 * ky, 16, stride=16), :]
            b = cells[pl.ds(256 * part + 2 * ky + 1, 16, stride=16), :]
            parts.append(jnp.where(first, a, b))
        columns.append(jnp.concatenate(parts, axis=0))
    stacked = jnp.concatenate(columns, axis=1)
    result = table_dot3(tz[g], stacked)
    for ky in range(8):
        cells[pl.ds(ky, 192, stride=8), :] = result[:, ky * 128 : ky * 128 + 128]
    out[...] = cells[...].reshape(16, 96, 128).astype(BF)


def inverse_y_kernel(got, lanes, ty, out):
    rows = got[...].astype(F32)
    thirds = []
    for z3 in range(3):
        wide = jnp.concatenate(
            [rows[:, z * 8 : z * 8 + 8, :].reshape(128, 128) for z in range(4 * z3, 4 * z3 + 4)], axis=1
        ).astype(BF)
        moved = dot(wide, lanes[...])
        thirds.append(jnp.concatenate([moved[:, k * 128 : k * 128 + 128] for k in range(4)], axis=0))
    stacked = jnp.concatenate(thirds, axis=1).astype(BF)
    out[...] = table_dot(ty, stacked).reshape(16, 8, 384).astype(BF)


def cell_kernel(got, snaps, tx, txb, lift_mix, project, project_t, out):
    rows = got[...].astype(F32).reshape(128, 384).astype(BF)
    carried = table_dot(tx, rows)
    snap = snaps[0:3].astype(F32).reshape(384, 128)
    preact = dot3(snap, lift_mix[...]) + carried
    rate = math.sqrt(2.0 / math.pi)
    square = preact * preact
    bend = jnp.tanh(rate * preact * (1.0 + 0.044715 * square))
    activated = 0.5 * preact * (1.0 + bend)
    slope = 0.5 * (1.0 + bend) + 0.5 * preact * (1.0 - bend * bend) * rate * (1.0 + 3 * 0.044715 * square)
    lane = iota((384, 128), 1)
    gap = jnp.where(lane < 64, snap - pltpu.roll(snap, 64, 1), 0.0)
    misfit = dot3(activated, project[...]) + gap
    back = dot3(misfit, project_t[...]) * slope
    out[...] = table_dot3(txb, back).reshape(16, 8, 384).astype(BF)


def back_yz_kernel(got, ty, lanes, tz, out, cells):
    g, c = lax.axis_index("grp"), lax.axis_index("col")
    rows = got[...].astype(F32).reshape(128, 384).astype(BF)
    modes = table_dot(ty, rows)
    for z3 in range(3):
        wide = jnp.concatenate(
            [modes[k * 32 : k * 32 + 32, z3 * 128 : z3 * 128 + 128] for k in range(4)], axis=1
        )
        high, low = split(wide)
        moved = dot(high, lanes[...]) + dot(low, lanes[...])
        for z4 in range(4):
            z = z3 * 4 + z4
            cells[z * 32 : z * 32 + 32, :] = moved[:, z4 * 128 : z4 * 128 + 128]
    cells[384:512, :] = jnp.zeros((128, 128), F32)
    sign = jnp.where(iota((16, 128), 1) < 64, 1.0, -1.0)
    columns = []
    for n in range(32):
        a = cells[pl.ds(n, 16, stride=32), :]
        columns.append(jnp.concatenate([a, pltpu.roll(a, 64, 1) * sign], axis=0))
    stacked = jnp.concatenate(columns, axis=1)
    result = table_dot3(tz[c * 4 + g], stacked)
    for g2 in range(4):
        for c2 in range(4):
            part = result[g2 * 16 : g2 * 16 + 16, c2 * 1024 : c2 * 1024 + 1024]
            high = part.astype(BF)
            out[g2 * 4 + c2, :, 0:1024] = high
            out[g2 * 4 + c2, :, 1024:1152] = (part[:, :128] - high[:, :128].astype(F32)).astype(BF)


def grad_kernel(got, spectrum, expand, out, cells):
    total = got[0].astype(F32)
    for src in range(1, 16):
        total = total + got[src].astype(F32)
    for ky in range(8):
        piece = total[:, ky * 128 : ky * 128 + 128]
        if ky == 0:
            piece = piece + total[:, 1024:1152]
        for kx in range(2):
            cells[pl.ds(2 * ky + kx, 16, stride=16), :] = piece
    own = (iota((256, 128), 1) // 32) % 2 == iota((256, 128), 0) % 2
    high, low = split(jnp.where(own, cells[...], 0.0))
    spread = dot(jnp.concatenate([high, low], axis=1), expand[...])
    br, bi = spread[:, :1024], spread[:, 1024:]
    sr, si = spectrum[0], spectrum[1]
    out[0] = (sr * br + si * bi).astype(BF)
    out[1] = (sr * bi - si * br).astype(BF)


def one_hot(dims, condition):
    a, b = iota(dims, 0), iota(dims, 1)
    return jnp.where(condition(a, b), 1.0, 0.0)


def prepare_kernel(weights, lift, mix, project, mixer, lift_mix, proj, proj_t, spread_lift):
    lift_v = lift[...]
    by_row = exact_dot(one_hot((1024, 32), lambda a, b: a // 32 == b), lift_v)
    table = exact_dot(by_row, one_hot((5, 256), lambda a, b: b // 32 == a))
    keep = iota((1024, 256), 0) % 32 == iota((1024, 256), 1) % 32
    high, low = split(jnp.where(keep, table, 0.0))
    for q in range(2):
        mixer[q] = dot(weights[q], high) + dot(weights[q], low)
    both = exact_dot(mix[...], lift_v)
    row_field = lambda a, b: (a // 12 == b) & (a < 60)
    rows = exact_dot(one_hot((128, 5), row_field), both, ((1,), (1,)))
    cols = exact_dot(rows, one_hot((32, 384), lambda a, b: b % 32 == a))
    same = iota((128, 384), 0) % 12 == iota((128, 384), 1) // 32
    lift_mix[...] = jnp.where(same, cols, 0.0)
    rows = exact_dot(one_hot((128, 5), row_field), project[...])
    cols = exact_dot(rows, one_hot((32, 384), lambda a, b: b % 32 == a))
    proj_t[...] = jnp.where(same, cols, 0.0)
    rows = exact_dot(one_hot((384, 32), lambda a, b: a % 32 == b), project[...], ((1,), (1,)))
    cols = exact_dot(rows, one_hot((5, 128), lambda a, b: (b // 12 == a) & (b < 60)))
    same = iota((384, 128), 1) % 12 == iota((384, 128), 0) // 32
    proj[...] = jnp.where(same, cols, 0.0)
    rows = exact_dot(
        one_hot((256, 5), lambda a, b: (a // 32 == b) & (a % 32 == 0)), lift_v, ((1,), (1,))
    )
    spread_lift[...] = exact_dot(rows, one_hot((32, 1024), lambda a, b: b // 32 == a))


def spectrum_kernel(spread, spread_lift, out):
    for q in range(2):
        out[q] = dot3(spread[:, q * 256 : q * 256 + 256], spread_lift[...])


def emit_faces(get, ylo, yhi, zlo, zhi, xlo, xhi):
    zlo[...] = jnp.zeros((32, 128), BF)
    zhi[...] = jnp.zeros((32, 128), BF)
    low_rows, high_rows = jnp.zeros((16, 384), F32), jnp.zeros((16, 384), F32)
    low_edges, high_edges = [], []
    for f in range(F):
        slabs = [get(f, y) for y in range(4)]
        ylo[f * 96 : f * 96 + 96, :] = slabs[0].astype(BF)
        yhi[f * 96 : f * 96 + 96, :] = slabs[3].astype(BF)
        low_edges += [s[0:1] for s in slabs]
        high_edges += [s[95:96] for s in slabs]
        cells = jnp.concatenate(slabs, axis=0).astype(BF)
        pick = lambda lane: one_hot((16, 128), lambda a, b: (a == f) & (b == lane)).astype(BF)
        low_rows = low_rows + dot(pick(0), cells, ((1,), (1,)))
        high_rows = high_rows + dot(pick(127), cells, ((1,), (1,)))
    pad = [jnp.zeros((12, 128), F32)]
    zlo[...] = jnp.concatenate(low_edges + pad, axis=0).astype(BF)
    zhi[...] = jnp.concatenate(high_edges + pad, axis=0).astype(BF)
    xlo[...] = low_rows.astype(BF)
    xhi[...] = high_rows.astype(BF)


FACES = [
    shape((480, 128), BF),
    shape((480, 128), BF),
    shape((32, 128), BF),
    shape((32, 128), BF),
    shape((16, 384), BF),
    shape((16, 384), BF),
]


def faces_kernel(fields, state, *faces):
    def get(f, y):
        cells = fields[f, pl.ds(y, 96, stride=4), :]
        state[f, y] = cells
        return cells

    emit_faces(get, *faces)


def advance(state, below, above, before, after, left, right, put):
    lane = iota((96, 128), 1)
    row = iota((96, 128), 0)
    before_v, after_v = before[...].astype(F32), after[...].astype(F32)
    for f in range(F):
        pick = lambda lane_of: one_hot((16, 128), lambda a, b: (a == f) & (b == lane_of)).astype(BF)
        low_x = dot(left[...], pick(0), ((0,), (0,)))
        high_x = dot(right[...], pick(127), ((0,), (0,)))
        slabs = [below[f * 96 : f * 96 + 96, :].astype(F32)]
        slabs += [state[f, y] for y in range(4)]
        slabs += [above[f * 96 : f * 96 + 96, :].astype(F32)]
        for y in range(4):
            q = slabs[y + 1]
            yminus, yplus = slabs[y], slabs[y + 2]
            xminus = jnp.where(lane == 0, low_x[y * 96 : y * 96 + 96], pltpu.roll(q, 1, 1))
            xplus = jnp.where(lane == 127, high_x[y * 96 : y * 96 + 96], pltpu.roll(q, 127, 1))
            k = f * 4 + y
            zminus = jnp.where(row == 0, before_v[k : k + 1], pltpu.roll(q, 1, 0))
            zplus = jnp.where(row == 95, after_v[k : k + 1], pltpu.roll(q, 95, 0))
            carried = (
                state[0, y] * (xplus - xminus)
                + state[1, y] * (yplus - yminus)
                + state[2, y] * (zplus - zminus)
            )
            around = xplus + xminus + yplus + yminus + zplus + zminus - 6.0 * q
            put(f, y, q - ADVECT_RATE * carried + DIFFUSE_RATE * around)


def step_kernel(state, below, above, before, after, left, right, new, *faces):
    def put(f, y, value):
        new[f, y] = value

    advance(state, below, above, before, after, left, right, put)
    emit_faces(lambda f, y: new[f, y], *faces)


def last_step_kernel(
    start, state, below, above, before, after, left, right, pool, new, snaps, stepped, rows
):
    outside = lax.axis_index("grp") == 3

    def put(f, y, value):
        stepped[f, pl.ds(y, 96, stride=4), :] = value
        new[f, pl.ds(y, 96, stride=4), :] = jnp.where(outside, start[f, y], value)

    advance(state, below, above, before, after, left, right, put)
    rows[...] = jnp.zeros((512, 256), F32)
    for f in range(F):
        pooled = []
        for y in range(2):
            both = start[f, 2 * y] + start[f, 2 * y + 1]
            stepped[F, 0:96, :] = both
            pooled.append(stepped[F, pl.ds(0, 48, stride=2), :] + stepped[F, pl.ds(1, 48, stride=2), :])
        for base, (low, high) in ((0, pooled), (64, pooled_rows(stepped, f))):
            for g in range(4):
                at = g * 128 + base + f * 12
                rows[at : at + 12, 0:128] = low[g * 12 : g * 12 + 12]
                rows[at : at + 12, 128:256] = high[g * 12 : g * 12 + 12]
    for g in range(4):
        high, low = split(rows[g * 128 : g * 128 + 128, :])
        snaps[g] = (dot(pool[...], high, ((1,), (1,))) + dot(pool[...], low, ((1,), (1,)))).astype(BF)


def swap(x, axes):
    return lax.all_to_all(x, axes, 0, 0, tiled=True)


def shift(x, axis, step, wrap=True):
    size = lax.axis_size(axis)
    peers = range(size) if wrap else range(size - 1)
    route = [(i, (i + step) % size) for i in peers if wrap or 0 <= i + step < size - 1]
    return lax.ppermute(x, axis, route)


def exchange(faces):
    ylo, yhi, zlo, zhi, xlo, xhi = faces
    return (
        shift(yhi, "row", 1),
        shift(ylo, "row", -1),
        shift(zhi, "col", 1),
        shift(zlo, "col", -1),
        shift(xhi, "grp", 1, False),
        shift(xlo, "grp", -1, False),
    )


def shards(fields, lift_weight, mix_weight, project_weight, spectral_weight):
    flat = fields.reshape(F, 384, 128)
    owner = ("grp", "col")

    first = call(
        first_x_kernel, shape((16, 8, 256), F32), flat, table_x_partial(), scratch=[pltpu.VMEM((256, 256), F32)]
    )
    got = swap(first, "row")
    state, *faces = call(faces_kernel, [shape((F, 4, 96, 128), F32)] + FACES, flat)
    halos = exchange(faces)
    mixer, lift_mix, proj, proj_t, spread_lift = call(
        prepare_kernel,
        [
            shape((2, 256, 256), F32),
            shape((128, 384), F32),
            shape((384, 128), F32),
            shape((128, 384), F32),
            shape((256, 1024), F32),
        ],
        spectral_weight.reshape(2, 256, 1024),
        lift_weight,
        mix_weight,
        project_weight,
    )
    first = call(first_yz_kernel, shape((16, 16, 256), F32), got, table_y_first(), table_z_first())
    got = swap(first, owner)
    middle, *faces = call(step_kernel, [shape((F, 4, 96, 128), F32)] + FACES, state, *halos)
    halos = exchange(faces)
    modes, spread = call(
        mix_kernel,
        [shape((16, 96, 128), BF), shape((256, 512), F32)],
        got,
        mixer,
        table_select(),
        table_sum_fields(),
        table_z_inverse(),
        scratch=[pltpu.VMEM((1536, 128), F32)],
    )
    got = swap(modes, owner)
    new_fields, snaps = call(
        last_step_kernel,
        [shape((F, 384, 128), F32), shape((4, 128, 128), BF)],
        state,
        middle,
        *halos,
        table_pool_x(),
        scratch=[pltpu.VMEM((F + 1, 384, 128), F32), pltpu.VMEM((512, 256), F32)],
    )
    snaps = swap(snaps, "grp")
    spectrum = call(spectrum_kernel, shape((2, 256, 1024), F32), spread, spread_lift)
    planes = call(inverse_y_kernel, shape((16, 8, 384), BF), got, table_lanes(), table_y_inverse())
    got = swap(planes, "row")
    back = call(
        cell_kernel,
        shape((16, 8, 384), BF),
        got,
        snaps,
        table_x_inverse(),
        table_x_back(),
        lift_mix,
        proj,
        proj_t,
    )
    got = swap(back, "row")
    back = call(
        back_yz_kernel,
        shape((16, 16, 1152), BF),
        got,
        table_y_back(),
        np.ascontiguousarray(table_lanes().T),
        table_z_back(),
        scratch=[pltpu.VMEM((512, 128), F32)],
    )
    got = swap(back, owner)
    grad = call(
        grad_kernel,
        shape((2, 256, 1024), BF),
        got,
        spectrum,
        table_expand(),
        scratch=[pltpu.VMEM((256, 128), F32)],
    )
    return new_fields.reshape(fields.shape), grad.reshape(spectral_weight.shape)


def solution(mesh):
    placed = (P(None, "col", "row", "grp"), P(), P(), P(), P(None, "grp", "col", "row", None))
    return jax.shard_map(
        shards,
        mesh=mesh,
        in_specs=placed,
        out_specs=(P(None, "col", "row", "grp"), P(None, "grp", "col", "row", None)),
        check_vma=False,
    )
```

time: 538 us -> 158 us (0.29)
  local copies, waits for them, and re-layouts: 180 us -> 21 us
  other arithmetic: 83.9 us -> 0 us
  waiting for transfers between devices: 100 us -> 19.5 us
  matrix products: 46 us -> 0 us
  Pallas kernels: 0 us -> 20.3 us
  between operations: 15.3 us -> 0.9 us
  starting transfers between devices: 60 us -> 49.6 us
    unnamed x117 -> x63, local copies, waits for them, and re-layouts: 89.4 us -> 18.3 us
    dot_general x13 -> x0, matrix products: 46 us -> none  [the longest x2 14.2 us: to_modes(): jnp.einsum('czyx,pxk->pckyz', cells_in, real_table(cells_in.shape[3], sca...]
    ppermute x18 -> x12, waiting for transfers between devices: 49 us -> 6.15 us  [shift(): return lax.ppermute(x, axis, route)]
    reduce_scatter x1 -> x0, waiting for transfers between devices: 40 us -> none  [shards(): lax.psum_scatter(owned_term.astype(jnp.bfloat16), 'grp', scatter_dimensio...]
    reduce_sum x2 -> x0, other arithmetic: 33.7 us -> none  [coarsen(): return jnp.mean(blocks, axis=(2, 4, 6))]
    all_to_all x11 -> x0, local copies, waits for them, and re-layouts: 28.2 us -> none  [the longest x4 11.9 us: to_modes(): lax.all_to_all(along_y, 'col', split_axis=3, concat_axis=4, tiled=True)]
    pallas_call x0 -> x12, Pallas kernels: none -> 20.3 us  [call(): pl.pallas_call(body, out_shape=shapes, in_specs=[vmem] * len(args), out_s...]
    all_to_all x6 -> x0, other arithmetic: 20.3 us -> none  [the longest x2 6.68 us: to_modes(): lax.all_to_all(along_y, 'col', split_axis=3, concat_axis=4, tiled=True)]
  transfers between devices with their start and end apart: 24 -> 16, of which waited for: 10 -> 4; matrix products, arithmetic and copies ran while one was open for 38% -> 1% of each run, Pallas kernels for 0% -> 7%
where the time goes in v1:
time: 158 us; the launch traced here: 157 us
  starting transfers between devices  49.6 us (31%)
  blocking collectives  45.4 us (29%)
  local copies, waits for them, and re-layouts  21 us (13%)
  Pallas kernels  20.3 us (13%)
  waiting for transfers between devices  19.5 us (12%)
    all_to_all x3, blocking collectives, swap(): return lax.all_to_all(x, axes, 0, 0, tiled=True)  45.4 us
    all_to_all x4, starting transfers between devices, swap(): return lax.all_to_all(x, axes, 0, 0, tiled=True)  24.9 us
    ppermute x12, starting transfers between devices, shift(): return lax.ppermute(x, axis, route)  24.8 us
    pallas_call x12, Pallas kernels, call(): pl.pallas_call(body, out_shape=shapes, in_specs=[vmem] * len(args), out_s...  20.3 us
    unnamed x63, local copies, waits for them, and re-layouts  18.3 us
    all_to_all x4, waiting for transfers between devices, swap(): return lax.all_to_all(x, axes, 0, 0, tiled=True)  13.4 us
    ppermute x12, waiting for transfers between devices, shift(): return lax.ppermute(x, axis, route)  6.15 us
  transfers between devices with their start and end apart: 16, of which 4 were waited for; matrix products, arithmetic and copies ran while one was open for 1% of the time, Pallas kernels for 7%

profile of v1, /device:TPU:1, one launch (start us, length us, event | category | flops | bytes accessed | tf_op | source)
XLA Modules:
  0.0 156.8 jit_solution(13098480341917032033)
XLA Ops:
  3.2 21.1 %all_to_all.35.got = f32[16,8,256]{2,1,0:T(8,128)S(1)} all-to-all(f32[16,8,256]{2,1,0:T(8,128)S(1)} %shard_map.206), channel_id=1, replica_groups=mesh['grp'=4,'row'=16,'col'=4] {'row'}, dimensions={0} | all-to-all | bytes 262144 | tf_op jit(solution)/shard_map/all_to_all | solution.py:540
  24.3 1.6 %copy-done.5 = bf16[2,2,256,1024]{3,2,1,0:T(8,128)(2,1)S(1)} copy-done((bf16[2,2,256,1024]{3,2,1,0:T(8,128)(2,1)S(1)}, bf16[2,2,256,1024]{3,2,1,0:T(8,128)(2,1)}, u32[]{:S(2)}) %copy-start.5) | copy-done | bytes 2097176
  26.7 1.6 shard_map.207
  28.3 7.0 %all-to-all-start.1 = ((f32[16,16,256]{2,1,0:T(8,128)}), f32[16,16,256]{2,1,0:T(8,128)S(1)}, u32[]{:S(2)}, u32[]{:S(2)}) async-start(f32[16,16,256]{2,1,0:T(8,128)} %shard_map.207), calls=%async_computation.1 | async-start | bytes 524288 | tf_op jit(solution)/shard_map/all_to_all | solution.py:540
  38.3 5.0 %shard_map.208 = (f32[2,256,256]{2,1,0:T(8,128)S(1)}, f32[128,384]{1,0:T(8,128)S(1)}, f32[384,128]{1,0:T(8,128)S(1)}, f32[128,384]{1,0:T(8,128)S(1)}, f32[256,1024]{1,0:T(8,128)S(1)}) custom-call(bf16[2,256,1024]{2,1,0:T(8,128)(2,1)S(1)} %reshape.18.weights, f32[32,5]{1,0:T(8,128)S(1)} %copy.22.lift, f32[32,32]{1,0:T(8,128)S(1)} %copy-done.28, ...), custom_call_target="tpu_custom_call" | custom-call | tf_op jit(solution)/shard_map/pallas_call | solution.py:233
  49.3 2.3 %shard_map.209 = (bf16[16,96,128]{2,1,0:T(8,128)(2,1)}, f32[256,512]{1,0:T(8,128)S(1)}) custom-call(f32[16,16,256]{2,1,0:T(8,128)S(1)} %all-to-all-done.1.got, f32[2,256,256]{2,1,0:T(8,128)S(1)} %copy-done.15, bf16[1024,512]{1,0:T(8,128)(2,1)S(1)} %copy-done.8, bf16[512,128]{1,0:T(8,128)(2,1)S(1)} %copy-done.24, bf16[4,2,192,32]{3,2,1,0:T(8,128)(2,1)S(1)} %copy-done.16), custom_call_target="tpu_custom_call" | custom-call | tf_op jit(solution)/shard_map/pallas_call | solution.py:233
  52.4 5.9 %all-to-all-start.2 = ((bf16[16,96,128]{2,1,0:T(8,128)(2,1)}), bf16[16,96,128]{2,1,0:T(8,128)(2,1)S(1)}, u32[]{:S(2)}, u32[]{:S(2)}) async-start(bf16[16,96,128]{2,1,0:T(8,128)(2,1)} %get-tuple-element.41), calls=%async_computation.2 | async-start | bytes 786432 | tf_op jit(solution)/shard_map/all_to_all | solution.py:540
  59.2 5.3 %collective-permute-start.1 = (bf16[480,128]{1,0:T(8,128)(2,1)S(1)}, bf16[480,128]{1,0:T(8,128)(2,1)S(1)}, u32[]{:S(2)}, u32[]{:S(2)}) collective-permute-start(bf16[480,128]{1,0:T(8,128)(2,1)S(1)} %get-tuple-element.27), channel_id=1, source_target_pairs={{0,60},{4,0},{8,4},{12,8},{16,12},{20,16},{24,20},{28,24},{32,28},... | collective-permute-start | bytes 368648 | tf_op jit(solution)/shard_map/ppermute | solution.py:547
  64.6 2.2 %collective-permute-start.2 = (bf16[32,128]{1,0:T(8,128)(2,1)S(1)}, bf16[32,128]{1,0:T(8,128)(2,1)S(1)}, u32[]{:S(2)}, u32[]{:S(2)}) collective-permute-start(bf16[32,128]{1,0:T(8,128)(2,1)S(1)} %get-tuple-element.28), channel_id=1, source_target_pairs={{0,1},{1,2},{2,3},{3,0},{4,5},{5,6},{6,7},{7,4},{8,9},{9,10},{10,1... | collective-permute-start | bytes 24584 | tf_op jit(solution)/shard_map/ppermute | solution.py:547
  66.7 3.1 %collective-permute-start.4 = (bf16[16,384]{1,0:T(8,128)(2,1)S(1)}, bf16[16,384]{1,0:T(8,128)(2,1)S(1)}, u32[]{:S(2)}, u32[]{:S(2)}) collective-permute-start(bf16[16,384]{1,0:T(8,128)(2,1)S(1)} %get-tuple-element.30), channel_id=1, source_target_pairs={{0,64},{64,128},{1,65},{65,129},{2,66},{66,130},{3,67},{67,131},{4... | collective-permute-start | bytes 36872 | tf_op jit(solution)/shard_map/ppermute | solution.py:547
  71.2 3.1 %collective-permute-done.3.after = bf16[32,128]{1,0:T(8,128)(2,1)S(1)} collective-permute-done((bf16[32,128]{1,0:T(8,128)(2,1)S(1)}, bf16[32,128]{1,0:T(8,128)(2,1)S(1)}, u32[]{:S(2)}, u32[]{:S(2)}) %collective-permute-start.3) | collective-permute-done | bytes 8224 | tf_op jit(solution)/shard_map/ppermute | solution.py:547
  76.0 5.7 %collective-permute-start.7 = (bf16[480,128]{1,0:T(8,128)(2,1)S(1)}, bf16[480,128]{1,0:T(8,128)(2,1)S(1)}, u32[]{:S(2)}, u32[]{:S(2)}) collective-permute-start(bf16[480,128]{1,0:T(8,128)(2,1)S(1)} %get-tuple-element.34), channel_id=1, source_target_pairs={{0,60},{4,0},{8,4},{12,8},{16,12},{20,16},{24,20},{28,24},{32,28},... | collective-permute-start | bytes 368648 | tf_op jit(solution)/shard_map/ppermute | solution.py:547
  81.7 2.0 %collective-permute-start.8 = (bf16[32,128]{1,0:T(8,128)(2,1)S(1)}, bf16[32,128]{1,0:T(8,128)(2,1)S(1)}, u32[]{:S(2)}, u32[]{:S(2)}) collective-permute-start(bf16[32,128]{1,0:T(8,128)(2,1)S(1)} %get-tuple-element.35), channel_id=1, source_target_pairs={{0,1},{1,2},{2,3},{3,0},{4,5},{5,6},{6,7},{7,4},{8,9},{9,10},{10,1... | collective-permute-start | bytes 24584 | tf_op jit(solution)/shard_map/ppermute | solution.py:547
  83.7 3.1 %collective-permute-start.10 = (bf16[16,384]{1,0:T(8,128)(2,1)S(1)}, bf16[16,384]{1,0:T(8,128)(2,1)S(1)}, u32[]{:S(2)}, u32[]{:S(2)}) collective-permute-start(bf16[16,384]{1,0:T(8,128)(2,1)S(1)} %get-tuple-element.37), channel_id=1, source_target_pairs={{0,64},{64,128},{1,65},{65,129},{2,66},{66,130},{3,67},{67,131},{4... | collective-permute-start | bytes 36872 | tf_op jit(solution)/shard_map/ppermute | solution.py:547
  88.2 3.1 %collective-permute-done.9.after = bf16[32,128]{1,0:T(8,128)(2,1)S(1)} collective-permute-done((bf16[32,128]{1,0:T(8,128)(2,1)S(1)}, bf16[32,128]{1,0:T(8,128)(2,1)S(1)}, u32[]{:S(2)}, u32[]{:S(2)}) %collective-permute-start.9) | collective-permute-done | bytes 8224 | tf_op jit(solution)/shard_map/ppermute | solution.py:547
  91.2 2.7 %shard_map.205 = (f32[5,384,128]{2,1,0:T(8,128)}, bf16[4,128,128]{2,1,0:T(8,128)(2,1)}) custom-call(f32[5,4,96,128]{3,2,1,0:T(8,128)S(1)} %get-tuple-element.25.state.start, f32[5,4,96,128]{3,2,1,0:T(8,128)S(1)} %get-tuple-element.32.state, bf16[480,128]{1,0:T(8,128)(2,1)S(1)} %collective-permute-done.6.below, ...), custom_call_target="tpu_custom_call" | custom-call | tf_op jit(solution)/shard_map/pallas_call | solution.py:233
  93.9 4.5 %all-to-all-start.4 = ((bf16[4,128,128]{2,1,0:T(8,128)(2,1)}), bf16[4,128,128]{2,1,0:T(8,128)(2,1)S(1)}, u32[]{:S(2)}, u32[]{:S(2)}) async-start(bf16[4,128,128]{2,1,0:T(8,128)(2,1)} %get-tuple-element.42), calls=%async_computation.4 | async-start | bytes 262144 | tf_op jit(solution)/shard_map/all_to_all | solution.py:540
  99.1 5.0 %all-to-all-done.4.snaps = bf16[4,128,128]{2,1,0:T(8,128)(2,1)S(1)} async-done(((bf16[4,128,128]{2,1,0:T(8,128)(2,1)}), bf16[4,128,128]{2,1,0:T(8,128)(2,1)S(1)}, u32[]{:S(2)}, u32[]{:S(2)}) %all-to-all-start.4) | async-done | bytes 131104 | tf_op jit(solution)/shard_map/all_to_all | solution.py:540
  104.1 12.4 %all_to_all.36.got = bf16[16,8,384]{2,1,0:T(8,128)(2,1)S(1)} all-to-all(bf16[16,8,384]{2,1,0:T(8,128)(2,1)S(1)} %shard_map.210), channel_id=1, replica_groups=mesh['grp'=4,'row'=16,'col'=4] {'row'}, dimensions={0} | all-to-all | bytes 196608 | tf_op jit(solution)/shard_map/all_to_all | solution.py:540
  117.4 2.0 %shard_map.211 = bf16[16,8,384]{2,1,0:T(8,128)(2,1)S(1)} custom-call(bf16[16,8,384]{2,1,0:T(8,128)(2,1)S(1)} %all_to_all.36.got, bf16[4,128,128]{2,1,0:T(8,128)(2,1)S(1)} %all-to-all-done.4.snaps, bf16[2,384,128]{2,1,0:T(8,128)(2,1)S(1)} %copy-done.18, bf16[2,128,384]{2,1,0:T(8,128)(2,1)S(1)} %copy-done.19, f32[128,384]{1,0:T(8,128)S(1)} %get-tuple-element.43.lift_mix, ...), custom_call_target="tpu_custom_call" | custom-call | tf_op jit(solution)/shard_map/pallas_call | solution.py:233
  119.4 11.9 %all_to_all.37.got = bf16[16,8,384]{2,1,0:T(8,128)(2,1)S(1)} all-to-all(bf16[16,8,384]{2,1,0:T(8,128)(2,1)S(1)} %shard_map.211), channel_id=1, replica_groups=mesh['grp'=4,'row'=16,'col'=4] {'row'}, dimensions={0} | all-to-all | bytes 196608 | tf_op jit(solution)/shard_map/all_to_all | solution.py:540
  131.3 2.3 %shard_map.212 = bf16[16,16,1152]{2,1,0:T(8,128)(2,1)} custom-call(bf16[16,8,384]{2,1,0:T(8,128)(2,1)S(1)} %all_to_all.37.got, bf16[2,128,128]{2,1,0:T(8,128)(2,1)S(1)} %copy-done.25, bf16[512,512]{1,0:T(8,128)(2,1)S(1)} %copy-done.4, bf16[16,2,64,32]{3,2,1,0:T(8,128)(2,1)S(1)} %copy-done.10), custom_call_target="tpu_custom_call" | custom-call | tf_op jit(solution)/shard_map/pallas_call | solution.py:233
  133.6 7.5 %all-to-all-start.6 = ((bf16[16,16,1152]{2,1,0:T(8,128)(2,1)}), bf16[16,16,1152]{2,1,0:T(8,128)(2,1)S(1)}, u32[]{:S(2)}, u32[]{:S(2)}) async-start(bf16[16,16,1152]{2,1,0:T(8,128)(2,1)} %shard_map.212), calls=%async_computation.6 | async-start | bytes 1179648 | tf_op jit(solution)/shard_map/all_to_all | solution.py:540
  143.3 8.4 %all-to-all-done.6.got = bf16[16,16,1152]{2,1,0:T(8,128)(2,1)S(1)} async-done(((bf16[16,16,1152]{2,1,0:T(8,128)(2,1)}), bf16[16,16,1152]{2,1,0:T(8,128)(2,1)S(1)}, u32[]{:S(2)}, u32[]{:S(2)}) %all-to-all-start.6) | async-done | bytes 589856 | tf_op jit(solution)/shard_map/all_to_all | solution.py:540
  (88 shorter events, 27.5 us)
Async XLA Ops:
  28.3 18.1 %all-to-all-start.1 = ((f32[16,16,256]{2,1,0:T(8,128)}), f32[16,16,256]{2,1,0:T(8,128)S(1)}, u32[]{:S(2)}, u32[]{:S(2)}) async-start(f32[16,16,256]{2,1,0:T(8,128)} %shard_map.207), calls=%async_computation.1 | async-start | bytes 524288 | tf_op jit(solution)/shard_map/all_to_all | solution.py:540
  52.4 38.8 %copy-start.26 = (bf16[128,256]{1,0:T(8,128)(2,1)S(1)}, bf16[128,256]{1,0:T(8,128)(2,1)}, u32[]{:S(2)}) copy-start(bf16[128,256]{1,0:T(8,128)(2,1)} %constant.34.clone.pool) | copy-start | bytes 196612
  52.4 41.5 %all-to-all-start.2 = ((bf16[16,96,128]{2,1,0:T(8,128)(2,1)}), bf16[16,96,128]{2,1,0:T(8,128)(2,1)S(1)}, u32[]{:S(2)}, u32[]{:S(2)}) async-start(bf16[16,96,128]{2,1,0:T(8,128)(2,1)} %get-tuple-element.41), calls=%async_computation.2 | async-start | bytes 786432 | tf_op jit(solution)/shard_map/all_to_all | solution.py:540
  58.7 39.7 %copy-start.4 = (bf16[512,512]{1,0:T(8,128)(2,1)S(1)}, bf16[512,512]{1,0:T(8,128)(2,1)}, u32[]{:S(2)}) copy-start(bf16[512,512]{1,0:T(8,128)(2,1)} %constant.35.clone.lanes) | copy-start | bytes 1572868
  58.8 39.7 %copy-start.17 = (bf16[2,128,512]{2,1,0:T(8,128)(2,1)S(1)}, bf16[2,128,512]{2,1,0:T(8,128)(2,1)}, u32[]{:S(2)}) copy-start(bf16[2,128,512]{2,1,0:T(8,128)(2,1)} %constant.36.clone.ty) | copy-start | bytes 786436
  58.8 15.5 %collective-permute-start = (bf16[480,128]{1,0:T(8,128)(2,1)S(1)}, bf16[480,128]{1,0:T(8,128)(2,1)S(1)}, u32[]{:S(2)}, u32[]{:S(2)}) collective-permute-start(bf16[480,128]{1,0:T(8,128)(2,1)S(1)} %get-tuple-element.26), channel_id=1, source_target_pairs={{0,4},{4,8},{8,12},{12,16},{16,20},{20,24},{24,28},{28,32},{32,36}... | collective-permute-start | bytes 368648 | tf_op jit(solution)/shard_map/ppermute | solution.py:547
  59.2 15.1 %collective-permute-start.1 = (bf16[480,128]{1,0:T(8,128)(2,1)S(1)}, bf16[480,128]{1,0:T(8,128)(2,1)S(1)}, u32[]{:S(2)}, u32[]{:S(2)}) collective-permute-start(bf16[480,128]{1,0:T(8,128)(2,1)S(1)} %get-tuple-element.27), channel_id=1, source_target_pairs={{0,60},{4,0},{8,4},{12,8},{16,12},{20,16},{24,20},{28,24},{32,28},... | collective-permute-start | bytes 368648 | tf_op jit(solution)/shard_map/ppermute | solution.py:547
  64.6 6.6 %collective-permute-start.2 = (bf16[32,128]{1,0:T(8,128)(2,1)S(1)}, bf16[32,128]{1,0:T(8,128)(2,1)S(1)}, u32[]{:S(2)}, u32[]{:S(2)}) collective-permute-start(bf16[32,128]{1,0:T(8,128)(2,1)S(1)} %get-tuple-element.28), channel_id=1, source_target_pairs={{0,1},{1,2},{2,3},{3,0},{4,5},{5,6},{6,7},{7,4},{8,9},{9,10},{10,1... | collective-permute-start | bytes 24584 | tf_op jit(solution)/shard_map/ppermute | solution.py:547
  66.7 7.6 %collective-permute-start.4 = (bf16[16,384]{1,0:T(8,128)(2,1)S(1)}, bf16[16,384]{1,0:T(8,128)(2,1)S(1)}, u32[]{:S(2)}, u32[]{:S(2)}) collective-permute-start(bf16[16,384]{1,0:T(8,128)(2,1)S(1)} %get-tuple-element.30), channel_id=1, source_target_pairs={{0,64},{64,128},{1,65},{65,129},{2,66},{66,130},{3,67},{67,131},{4... | collective-permute-start | bytes 36872 | tf_op jit(solution)/shard_map/ppermute | solution.py:547
  69.8 4.5 %collective-permute-start.5 = (bf16[16,384]{1,0:T(8,128)(2,1)S(1)}, bf16[16,384]{1,0:T(8,128)(2,1)S(1)}, u32[]{:S(2)}, u32[]{:S(2)}) collective-permute-start(bf16[16,384]{1,0:T(8,128)(2,1)S(1)} %get-tuple-element.31), channel_id=1, source_target_pairs={{64,0},{128,64},{65,1},{129,65},{66,2},{130,66},{67,3},{131,67},{6... | collective-permute-start | bytes 36872 | tf_op jit(solution)/shard_map/ppermute | solution.py:547
  71.1 3.2 %collective-permute-start.3 = (bf16[32,128]{1,0:T(8,128)(2,1)S(1)}, bf16[32,128]{1,0:T(8,128)(2,1)S(1)}, u32[]{:S(2)}, u32[]{:S(2)}) collective-permute-start(bf16[32,128]{1,0:T(8,128)(2,1)S(1)} %get-tuple-element.29), channel_id=1, source_target_pairs={{0,3},{1,0},{2,1},{3,2},{4,7},{5,4},{6,5},{7,6},{8,11},{9,8},{10,9... | collective-permute-start | bytes 24584 | tf_op jit(solution)/shard_map/ppermute | solution.py:547
  75.7 40.8 %copy-start.18 = (bf16[2,384,128]{2,1,0:T(8,128)(2,1)S(1)}, bf16[2,384,128]{2,1,0:T(8,128)(2,1)}, u32[]{:S(2)}) copy-start(bf16[2,384,128]{2,1,0:T(8,128)(2,1)} %constant.37.clone.tx) | copy-start | bytes 589828
  75.7 40.8 %copy-start.19 = (bf16[2,128,384]{2,1,0:T(8,128)(2,1)S(1)}, bf16[2,128,384]{2,1,0:T(8,128)(2,1)}, u32[]{:S(2)}) copy-start(bf16[2,128,384]{2,1,0:T(8,128)(2,1)} %constant.38.clone.txb) | copy-start | bytes 589828
  75.7 40.8 %copy-start.21 = (f32[384,128]{1,0:T(8,128)S(1)}, f32[384,128]{1,0:T(8,128)}, u32[]{:S(2)}) copy-start(f32[384,128]{1,0:T(8,128)} %copy-done.20) | copy-start | bytes 589828
  75.7 15.5 %collective-permute-start.6 = (bf16[480,128]{1,0:T(8,128)(2,1)S(1)}, bf16[480,128]{1,0:T(8,128)(2,1)S(1)}, u32[]{:S(2)}, u32[]{:S(2)}) collective-permute-start(bf16[480,128]{1,0:T(8,128)(2,1)S(1)} %get-tuple-element.33), channel_id=1, source_target_pairs={{0,4},{4,8},{8,12},{12,16},{16,20},{20,24},{24,28},{28,32},{32,36}... | collective-permute-start | bytes 368648 | tf_op jit(solution)/shard_map/ppermute | solution.py:547
  76.0 15.2 %collective-permute-start.7 = (bf16[480,128]{1,0:T(8,128)(2,1)S(1)}, bf16[480,128]{1,0:T(8,128)(2,1)S(1)}, u32[]{:S(2)}, u32[]{:S(2)}) collective-permute-start(bf16[480,128]{1,0:T(8,128)(2,1)S(1)} %get-tuple-element.34), channel_id=1, source_target_pairs={{0,60},{4,0},{8,4},{12,8},{16,12},{20,16},{24,20},{28,24},{32,28},... | collective-permute-start | bytes 368648 | tf_op jit(solution)/shard_map/ppermute | solution.py:547
  81.7 6.4 %collective-permute-start.8 = (bf16[32,128]{1,0:T(8,128)(2,1)S(1)}, bf16[32,128]{1,0:T(8,128)(2,1)S(1)}, u32[]{:S(2)}, u32[]{:S(2)}) collective-permute-start(bf16[32,128]{1,0:T(8,128)(2,1)S(1)} %get-tuple-element.35), channel_id=1, source_target_pairs={{0,1},{1,2},{2,3},{3,0},{4,5},{5,6},{6,7},{7,4},{8,9},{9,10},{10,1... | collective-permute-start | bytes 24584 | tf_op jit(solution)/shard_map/ppermute | solution.py:547
  83.7 7.6 %collective-permute-start.10 = (bf16[16,384]{1,0:T(8,128)(2,1)S(1)}, bf16[16,384]{1,0:T(8,128)(2,1)S(1)}, u32[]{:S(2)}, u32[]{:S(2)}) collective-permute-start(bf16[16,384]{1,0:T(8,128)(2,1)S(1)} %get-tuple-element.37), channel_id=1, source_target_pairs={{0,64},{64,128},{1,65},{65,129},{2,66},{66,130},{3,67},{67,131},{4... | collective-permute-start | bytes 36872 | tf_op jit(solution)/shard_map/ppermute | solution.py:547
  86.7 4.5 %collective-permute-start.11 = (bf16[16,384]{1,0:T(8,128)(2,1)S(1)}, bf16[16,384]{1,0:T(8,128)(2,1)S(1)}, u32[]{:S(2)}, u32[]{:S(2)}) collective-permute-start(bf16[16,384]{1,0:T(8,128)(2,1)S(1)} %get-tuple-element.38), channel_id=1, source_target_pairs={{64,0},{128,64},{65,1},{129,65},{66,2},{130,66},{67,3},{131,67},{6... | collective-permute-start | bytes 36872 | tf_op jit(solution)/shard_map/ppermute | solution.py:547
  88.1 3.2 %collective-permute-start.9 = (bf16[32,128]{1,0:T(8,128)(2,1)S(1)}, bf16[32,128]{1,0:T(8,128)(2,1)S(1)}, u32[]{:S(2)}, u32[]{:S(2)}) collective-permute-start(bf16[32,128]{1,0:T(8,128)(2,1)S(1)} %get-tuple-element.36), channel_id=1, source_target_pairs={{0,3},{1,0},{2,1},{3,2},{4,7},{5,4},{6,5},{7,6},{8,11},{9,8},{10,9... | collective-permute-start | bytes 24584 | tf_op jit(solution)/shard_map/ppermute | solution.py:547
  93.9 37.4 %copy-start.10 = (bf16[16,2,64,32]{3,2,1,0:T(8,128)(2,1)S(1)}, bf16[16,2,64,32]{3,2,1,0:T(8,128)(2,1)}, u32[]{:S(2)}) copy-start(bf16[16,2,64,32]{3,2,1,0:T(8,128)(2,1)} %constant.40.clone.tz) | copy-start | bytes 393220
  93.9 37.4 %copy-start.25 = (bf16[2,128,128]{2,1,0:T(8,128)(2,1)S(1)}, bf16[2,128,128]{2,1,0:T(8,128)(2,1)}, u32[]{:S(2)}) copy-start(bf16[2,128,128]{2,1,0:T(8,128)(2,1)} %constant.39.clone.ty) | copy-start | bytes 196612
  93.9 10.2 %all-to-all-start.4 = ((bf16[4,128,128]{2,1,0:T(8,128)(2,1)}), bf16[4,128,128]{2,1,0:T(8,128)(2,1)S(1)}, u32[]{:S(2)}, u32[]{:S(2)}) async-start(bf16[4,128,128]{2,1,0:T(8,128)(2,1)} %get-tuple-element.42), calls=%async_computation.4 | async-start | bytes 262144 | tf_op jit(solution)/shard_map/all_to_all | solution.py:540
  133.6 18.1 %all-to-all-start.6 = ((bf16[16,16,1152]{2,1,0:T(8,128)(2,1)}), bf16[16,16,1152]{2,1,0:T(8,128)(2,1)S(1)}, u32[]{:S(2)}, u32[]{:S(2)}) async-start(bf16[16,16,1152]{2,1,0:T(8,128)(2,1)} %shard_map.212), calls=%async_computation.6 | async-start | bytes 1179648 | tf_op jit(solution)/shard_map/all_to_all | solution.py:540
  (23 other events, 90.0 us)

commit v2 on v1

v2 whole, which is shorter than its diff:
```python
import functools
import math

import jax
import jax.numpy as jnp
import ml_dtypes
import numpy as np
from jax import lax
from jax.experimental.layout import Layout, with_layout_constraint
from jax.experimental import pallas as pl
from jax.experimental.pallas import tpu as pltpu
from jax.sharding import PartitionSpec as P

GX, GY, GZ = 192, 32, 192
KX, KY, KZ = 32, 32, 64
F, C = 5, 32
ADVECT_RATE = 0.1
DIFFUSE_RATE = 0.12
NORM = 1.0 / math.sqrt(GX * GY * GZ)
BF, F32 = jnp.bfloat16, jnp.float32
VMEM_LIMIT = 14 * 1024 * 1024


def freq(kept, extent):
    j = np.arange(kept)
    return np.where(j < kept // 2, j, j - kept)


FZ, FY = freq(KZ, GZ), freq(KY, GY)


def hilo(table):
    table = np.asarray(table, np.float32)
    high = table.astype(ml_dtypes.bfloat16)
    low = (table - high.astype(np.float32)).astype(ml_dtypes.bfloat16)
    return np.stack([high, low])


@functools.lru_cache(None)
def table_x_partial():
    out = np.zeros((4, 16, 2, 2, 2, 2, 128))
    x = np.arange(128) // 2
    for g in range(3):
        for kx in range(KX):
            angle = 2 * np.pi * ((kx * (64 * g + x)) % GX) / GX
            for y in range(2):
                out[g, kx // 2, y, kx % 2, 0, y] = np.cos(angle) * NORM / 8
                out[g, kx // 2, y, kx % 2, 1, y] = -np.sin(angle) * NORM / 8
    return np.moveaxis(hilo(out.reshape(4, 128, 256)), 0, 1)


def y_forward(rows, columns):
    p, kx, ky = (np.asarray(v)[:, None] for v in rows)
    q, jx, y = (np.asarray(v)[None, :] for v in columns)
    angle = 2 * np.pi * ((FY[ky] * y) % GY) / GY
    part = np.where(p == q, np.cos(angle), np.where(p == 0, np.sin(angle), -np.sin(angle)))
    return hilo(np.where(kx == jx, part, 0.0))


def index_of(*sizes):
    return [v.reshape(-1) for v in np.meshgrid(*[np.arange(s) for s in sizes], indexing="ij")]


@functools.lru_cache(None)
def table_y_first():
    p, ky, kx = index_of(2, 32, 2)
    r, y, jx, q = index_of(16, 2, 2, 2)
    return y_forward((p, kx, ky), (q, jx, 2 * r + y))


@functools.lru_cache(None)
def table_y_back():
    p, kx, ky = index_of(2, 2, 32)
    r, jx, q, y = index_of(16, 2, 2, 2)
    return y_forward((p, kx, ky), (q, jx, 2 * r + y))


@functools.lru_cache(None)
def table_z_first():
    out = np.zeros((2, 256, 4, 128))
    z = np.arange(48)
    for kz in range(KZ):
        angle = 2 * np.pi * ((FZ[kz] * z) % GZ) / GZ
        for f in range(F):
            rows, lane = slice(f * 48, f * 48 + 48), f * 16 + kz % 16
            out[0, rows, kz // 16, lane] = np.cos(angle)
            out[1, rows, kz // 16, lane] = np.sin(angle)
    return hilo(out.reshape(2, 256, 512))


@functools.lru_cache(None)
def table_select():
    out = np.zeros((8, 16, 8, 32), np.float32)
    for f in range(F):
        out[f, :, f, :] = 1.0
    return out.reshape(128, 256).astype(ml_dtypes.bfloat16)


@functools.lru_cache(None)
def table_sum_fields():
    out = np.zeros((2, 8, 32, 2, 2, 32), np.float32)
    for o in range(C):
        for p in range(2):
            out[p, :F, o, p, :, o] = 1.0
    return out.reshape(512, 128).astype(ml_dtypes.bfloat16)


@functools.lru_cache(None)
def table_z_inverse():
    g2, c2, zi = index_of(4, 4, 12)
    z = 48 * c2 + 12 * g2 + zi
    out = np.zeros((4, 192, 32))
    for g in range(4):
        for k in range(16):
            angle = 2 * np.pi * ((FZ[16 * g + k] * z) % GZ) / GZ
            out[g, :, k] = np.cos(angle)
            out[g, :, 16 + k] = np.sin(angle)
    return np.moveaxis(hilo(out), 0, 1)


@functools.lru_cache(None)
def table_lanes():
    out = np.zeros((4, 4, 32, 4, 4, 32), np.float32)
    for a in range(4):
        for b in range(4):
            for o in range(C):
                out[a, b, o, b, a, o] = 1.0
    return out.reshape(512, 512).astype(ml_dtypes.bfloat16)


@functools.lru_cache(None)
def table_y_inverse():
    r, kx, p, y = (v[:, None] for v in index_of(16, 2, 2, 2))
    q, jx, _, ky = (v[None, :] for v in index_of(2, 2, 4, 32))
    angle = 2 * np.pi * ((FY[ky] * (2 * r + y)) % GY) / GY
    part = np.where(p == q, np.cos(angle), np.where(p == 0, -np.sin(angle), np.sin(angle)))
    return hilo(np.where(kx == jx, part, 0.0))


@functools.lru_cache(None)
def table_x_inverse():
    g, y, x = (v[:, None] for v in index_of(3, 2, 64))
    r, kx, p, yy = (v[None, :] for v in index_of(16, 2, 2, 2))
    k = 2 * r + kx
    angle = 2 * np.pi * ((k * (64 * g + x)) % GX) / GX
    part = np.where(p == 0, np.cos(angle), -np.sin(angle)) * np.where(k == 0, 1.0, 2.0) * NORM
    return hilo(np.where(y == yy, part, 0.0))


@functools.lru_cache(None)
def table_z_back():
    out = np.zeros((4, 4, KZ, 2, 16))
    zi = np.arange(12)
    for c in range(4):
        for g in range(4):
            z = 48 * c + 12 * g + zi
            angle = 2 * np.pi * ((FZ[:, None] * z[None, :]) % GZ) / GZ
            out[c, g, :, 0, :12] = np.cos(angle)
            out[c, g, :, 1, :12] = np.sin(angle)
    return np.moveaxis(hilo(out.reshape(16, KZ, 32)), 0, 1)


@functools.lru_cache(None)
def table_pool_x():
    out = np.zeros((2, 64, 2, 128), np.float32)
    for x in range(128):
        for y in range(2):
            out[y, x // 2, y, x] = 0.125
    return out.reshape(128, 256).astype(ml_dtypes.bfloat16)


@functools.lru_cache(None)
def table_expand():
    out = np.zeros((2, 2, 2, 32, 2, 4, 32), np.float32)
    for o in range(C):
        for p in range(2):
            out[:, p, :, o, p, :, o] = 1.0
    return out.reshape(256, 256).astype(ml_dtypes.bfloat16)


def dot(a, b, dims=((1,), (0,))):
    return lax.dot_general(a, b, (dims, ((), ())), preferred_element_type=F32)


def exact_dot(a, b, dims=((1,), (0,))):
    return lax.dot_general(
        a, b, (dims, ((), ())), preferred_element_type=F32, precision=lax.Precision.HIGHEST
    )


def split(x):
    high = x.astype(BF)
    return high, (x - high.astype(F32)).astype(BF)


def table_dot(table, x):
    return dot(table[0], x) + dot(table[1], x)


def table_dot3(table, x, dims=((1,), (0,))):
    high, low = split(x)
    return dot(table[0], high, dims) + dot(table[0], low, dims) + dot(table[1], high, dims)


def dot3(x, y):
    xh, xl = split(x)
    yh, yl = split(y)
    return dot(xh, yh) + dot(xl, yh) + dot(xh, yl)


def iota(shape, dim):
    return lax.broadcasted_iota(jnp.int32, shape, dim)


class Late:
    def __init__(self, copy, ref):
        self.copy, self.ref, self.there = copy, ref, False

    def get(self):
        if not self.there:
            self.copy.wait()
            self.there = True
        return self.ref


class Far:
    def __init__(self, out, ref, sems, pieces):
        self.out, self.ref, self.sems, self.pieces, self.sent = out, ref, sems, pieces, {}

    def push(self, piece):
        source = self.ref if self.pieces == 1 else self.ref.at[piece]
        target = self.out if self.pieces == 1 else self.out.at[piece]
        self.sent[piece] = pltpu.make_async_copy(source, target, self.sems.at[piece])
        self.sent[piece].start()

    def finish(self):
        for piece in range(self.pieces):
            if piece not in self.sent:
                self.push(piece)

    def wait(self):
        for copy in self.sent.values():
            copy.wait()


def call(body, outs, inputs, tables=(), scratch=(), far=None):
    far = far or {}
    single = not isinstance(outs, (list, tuple))
    shapes = [outs] if single else list(outs)
    n, t, m, w = len(inputs), len(tables), len(shapes), len(far)
    spaces = [
        pltpu.VMEM(a.shape if place is None else a.shape[1:], a.dtype) for a, place in tables
    ] + [pltpu.VMEM(shapes[k].shape, shapes[k].dtype) for k in far]
    sems = ([pltpu.SemaphoreType.DMA((t,))] if t else []) + [pltpu.SemaphoreType.DMA((p,)) for p in far.values()]

    def kernel(*refs):
        ins, sources, results, rest = refs[:n], refs[n : n + t], refs[n + t : n + t + m], refs[n + t + m :]
        held, marks, own = rest[: t + w], rest[t + w : t + w + len(sems)], rest[t + w + len(sems) :]
        late = []
        for k, (_, place) in enumerate(tables):
            source = sources[k] if place is None else sources[k].at[place()]
            copy = pltpu.make_async_copy(source, held[k], marks[0].at[k])
            copy.start()
            late.append(Late(copy, held[k]))
        near = list(results)
        for k, (index, pieces) in enumerate(far.items()):
            near[index] = Far(results[index], held[t + k], marks[k + (1 if t else 0)], pieces)
        body(*ins, *late, *near, *own)
        for index in far:
            near[index].finish()
        for index in far:
            near[index].wait()

    vmem, hbm = (pl.BlockSpec(memory_space=space) for space in (pltpu.VMEM, pltpu.HBM))
    result = pl.pallas_call(
        kernel,
        out_shape=[pltpu.HBM(o.shape, o.dtype) if k in far else o for k, o in enumerate(shapes)],
        in_specs=[vmem] * n + [hbm] * t,
        out_specs=[hbm if k in far else vmem for k in range(m)],
        scratch_shapes=spaces + sems + list(scratch),
        compiler_params=pltpu.CompilerParams(vmem_limit_bytes=VMEM_LIMIT),
    )(*inputs, *[pltpu.with_memory_space_constraint(a, pltpu.HBM) for a, _ in tables])
    return result[0] if single else result


def own_group():
    return lax.axis_index("grp")


def shape(dims, dtype):
    return jax.ShapeDtypeStruct(dims, dtype)


def first_kernel(*refs):
    fields, table, out = refs[:F], refs[F], refs[F + 1]
    faces, state, rows = refs[F + 2 : F + 8], refs[F + 8], refs[F + 9]
    rows[240:256, :] = jnp.zeros((16, 256), F32)
    for f in range(F):
        cells = fields[f].get()
        for y in range(4):
            state[f, y] = cells[pl.ds(y, 96, stride=4), :]
        for y in range(2):
            rows[f * 48 : f * 48 + 48, y * 128 : y * 128 + 128] = pair_sums(state, f, y)
    result = table_dot3(table.get(), rows[...], ((1,), (1,)))
    out[...] = result.reshape(16, 8, 256)
    emit_faces(state, *faces)


def load_rows(fields, state, f):
    for y in range(4):
        state[f, y] = fields[f, pl.ds(y, 96, stride=4), :]


def pair_sums(state, f, y):
    parts = [state[f, 2 * y + k, pl.ds(j, 48, stride=2), :] for k in range(2) for j in range(2)]
    return (parts[0] + parts[1]) + (parts[2] + parts[3])


def neighbours():
    g, c = own_group(), lax.axis_index("col")
    return (g * 4 + (c + 3) % 4, g * 4 + (c + 1) % 4, ((g + 3) % 4) * 4 + c, ((g + 1) % 4) * 4 + c)


def first_yz_kernel(got, ty, tz, zlo, zhi, xlo, xhi, out):
    both = table_dot3(ty, got[...].reshape(128, 256))
    high, low = split(both)
    parts = []
    for k in range(2):
        parts.append(dot(high, tz[0, k]) + dot(low, tz[0, k]) + dot(high, tz[1, k]))
    re = parts[0][:64] + parts[1][64:]
    im = parts[0][64:] - parts[1][:64]
    for k, part in enumerate((re, im)):
        lanes = slice(k * 128, k * 128 + 128)
        high, low = split(part)
        for g in range(4):
            for c in range(4):
                rows, cols = slice(c * 16, c * 16 + 16), slice(g * 128, g * 128 + 128)
                out[g * 4 + c, 0:16, lanes] = high[rows, cols]
                out[g * 4 + c, 16:32, lanes] = low[rows, cols]
                out[g * 4 + c, 32:48, lanes] = jnp.zeros((16, 128), BF)
    for dest, face in zip(neighbours(), (zlo, zhi, xlo, xhi)):
        out[dest, 32:48, 0:128] = face[0:16, :]
        out[dest, 32:48, 128:256] = face[16:32, :]


def dot3_table(x, table):
    high, low = split(x)
    return dot(high, table[0]) + dot(low, table[0]) + dot(high, table[1])


def mix_kernel(
    got, below, above, select, sum_fields, weights, fields, tz, out, spread_out, middle, ylo, yhi, cells, state
):
    kz = iota((16, 128), 1) % 16
    re_sum, im_sum = 0.0, 0.0
    for c in range(4):
        total = 0.0
        for src in range(4):
            block = got[src * 4 + c, 0:32, :].astype(F32)
            total = total + (block[:16] + block[16:])
        re, im = total[:, :128], total[:, 128:]
        turn = (kz * c) % 4
        re_sum += jnp.where(turn == 0, re, jnp.where(turn == 1, im, jnp.where(turn == 2, -re, -im)))
        im_sum += jnp.where(turn == 0, im, jnp.where(turn == 1, -re, jnp.where(turn == 2, -im, re)))
    own = iota((256, 128), 0) // 16 == iota((256, 128), 1) % 16
    wide = []
    for part in (re_sum, im_sum):
        part = jnp.broadcast_to(part[None], (16, 16, 128)).reshape(256, 128)
        wide.append(jnp.where(own, part, 0.0))
    high, low = split(jnp.concatenate(wide, axis=0))
    spread = dot(high, select[...]) + dot(low, select[...])
    for q in range(2):
        for half in range(2):
            spread_out.ref[q, half] = spread[q * 256 : q * 256 + 256, half * 128 : half * 128 + 128]
    spread_out.push(0)
    faces = []
    for source in neighbours():
        block = got[source, 32:48, :]
        faces.append(jnp.concatenate([block[:, :128], block[:, 128:]], axis=0).astype(F32))
    for f in range(F):
        load_rows(fields, state, f)

    def put(f, y, value):
        middle.ref[f, y] = value

    advance(state, below, above, *faces, put)
    middle.push(0)
    faces = emit_faces(middle.ref, ylo, yhi)
    sr, si = spread[:256], spread[256:]
    wr, wi = weights[0], weights[1]
    mixed = jnp.concatenate([sr * wr - si * wi, sr * wi + si * wr], axis=1)
    high, low = split(mixed)
    modes = dot(high, sum_fields[...]) + dot(low, sum_fields[...])
    sign = jnp.where(iota((256, 128), 1) < 64, -1.0, 1.0)
    turned = pltpu.roll(modes, 64, 1) * sign
    cells[0:256, :] = modes
    cells[256:512, :] = turned
    first = (iota((16, 128), 1) // 32) % 2 == 0
    columns = []
    for ky in range(8):
        parts = []
        for part in range(2):
            a = cells[pl.ds(256 * part + 2 * ky, 16, stride=16), :]
            b = cells[pl.ds(256 * part + 2 * ky + 1, 16, stride=16), :]
            parts.append(jnp.where(first, a, b))
        columns.append(jnp.concatenate(parts, axis=0))
    stacked = jnp.concatenate(columns, axis=1)
    result = table_dot3(tz.get(), stacked)
    for ky in range(8):
        cells[pl.ds(ky, 192, stride=8), :] = result[:, ky * 128 : ky * 128 + 128]
    out[:, 0:96, :] = cells[...].reshape(16, 96, 128).astype(BF)
    out[:, 96:128, :] = jnp.zeros((16, 32, 128), BF)
    for dest, face in zip(neighbours(), faces):
        out[dest, 96:128, :] = face


def inverse_y_kernel(got, lanes, ty, out):
    rows = got[:, 0:96, :].astype(F32)
    thirds = []
    for z3 in range(3):
        wide = jnp.concatenate(
            [rows[:, z * 8 : z * 8 + 8, :].reshape(128, 128) for z in range(4 * z3, 4 * z3 + 4)], axis=1
        ).astype(BF)
        moved = dot(wide, lanes[...])
        thirds.append(jnp.concatenate([moved[:, k * 128 : k * 128 + 128] for k in range(4)], axis=0))
    stacked = jnp.concatenate(thirds, axis=1).astype(BF)
    out[...] = table_dot(ty, stacked).reshape(16, 8, 384).astype(BF)


def cell_kernel(got, snap0, snap1, snap2, snap3, tx, lift_mix, project_t, out, kept):
    g = own_group()
    for d, snap in enumerate((snap0, snap1, snap2, snap3)):
        kept[(g + 4 - d) % 4] = snap[...].astype(F32)
    snap = kept[0:3].reshape(384, 128)
    high, low = split(snap)
    preact = dot(high, lift_mix[0]) + dot(low, lift_mix[0]) + dot(high, lift_mix[1])
    rows = got[...].astype(F32).reshape(128, 384).astype(BF)
    preact = preact + table_dot(tx, rows)
    rate = math.sqrt(2.0 / math.pi)
    square = preact * preact
    bend = jnp.tanh(rate * preact * (1.0 + 0.044715 * square))
    activated = 0.5 * preact * (1.0 + bend)
    slope = 0.5 * (1.0 + bend) + 0.5 * preact * (1.0 - bend * bend) * rate * (1.0 + 3 * 0.044715 * square)
    lane = iota((384, 128), 1)
    gap = jnp.where(lane < 64, snap - pltpu.roll(snap, 64, 1), 0.0)
    turned = ((1,), (1,))
    high, low = split(activated)
    misfit = dot(high, project_t[0], turned) + dot(low, project_t[0], turned) + dot(high, project_t[1], turned)
    misfit = misfit + gap
    back = dot3_table(misfit, project_t) * slope
    out[...] = table_dot3(tx, back, ((0,), (0,))).reshape(16, 8, 384).astype(BF)


def back_yz_kernel(got, ty, lanes, tz, out, cells):
    rows = got[...].astype(F32).reshape(128, 384).astype(BF)
    modes = table_dot(ty, rows)
    lanes_v = lanes[...]
    for z3 in range(3):
        wide = jnp.concatenate(
            [modes[k * 32 : k * 32 + 32, z3 * 128 : z3 * 128 + 128] for k in range(4)], axis=1
        )
        high, low = split(wide)
        moved = dot(high, lanes_v) + dot(low, lanes_v)
        for z4 in range(4):
            z = z3 * 4 + z4
            cells[z * 32 : z * 32 + 32, :] = moved[:, z4 * 128 : z4 * 128 + 128]
    cells[384:512, :] = jnp.zeros((128, 128), F32)
    sign = jnp.where(iota((16, 128), 1) < 64, 1.0, -1.0)
    columns = []
    for n in range(32):
        a = cells[pl.ds(n, 16, stride=32), :]
        columns.append(jnp.concatenate([a, pltpu.roll(a, 64, 1) * sign], axis=0))
    stacked = jnp.concatenate(columns, axis=1)
    result = table_dot3(tz.get(), stacked)
    for g2 in range(4):
        for c2 in range(4):
            part = result[g2 * 16 : g2 * 16 + 16, c2 * 1024 : c2 * 1024 + 1024]
            high = part.astype(BF)
            out[g2 * 4 + c2, :, 0:1024] = high
            out[g2 * 4 + c2, :, 1024:1152] = (part[:, :128] - high[:, :128].astype(F32)).astype(BF)


def grad_kernel(got, expand, spectrum, out, cells, wide):
    total = got[0].astype(F32)
    for src in range(1, 16):
        total = total + got[src].astype(F32)
    for ky in range(8):
        piece = total[:, ky * 128 : ky * 128 + 128]
        if ky == 0:
            piece = piece + total[:, 1024:1152]
        for kx in range(2):
            cells[pl.ds(128 * kx + ky, 16, stride=8), :] = piece
    own = (iota((256, 128), 1) // 32) % 2 == iota((256, 128), 0) // 128
    high, low = split(jnp.where(own, cells[...], 0.0))
    spread = dot(jnp.concatenate([high, low], axis=1), expand[...])
    for q in range(2):
        for kx in range(2):
            rows = slice(kx * 128, kx * 128 + 128)
            br, bi = spread[rows, :128], spread[rows, 128:]
            for i in range(8):
                lanes = slice(i * 128, i * 128 + 128)
                sr, si = spectrum[kx, :, lanes], spectrum[2 + kx, :, lanes]
                value = sr * br + si * bi if q == 0 else sr * bi - si * br
                wide[q, pl.ds(2 * i + kx, 128, stride=16), :] = value
        out.ref[q] = wide[q].astype(BF).reshape(128, 16, 128)
        out.push(q)


def one_hot(dims, condition):
    a, b = iota(dims, 0), iota(dims, 1)
    return jnp.where(condition(a, b), 1.0, 0.0)


def mixer_kernel(lift, weights, mixer):
    table = exact_dot(lift[...], one_hot((5, 256), lambda a, b: b // 32 == a))
    keep = iota((1024, 256), 0) % 32 == iota((1024, 256), 1) % 32
    parts = []
    for part in split(table):
        part = jnp.broadcast_to(part.astype(F32)[:, None, :], (32, 32, 256)).reshape(1024, 256)
        parts.append(jnp.where(keep, part, 0.0).astype(BF))
    weights_v = weights.get()
    for q in range(2):
        mixer[q] = dot(weights_v[q], parts[0]) + dot(weights_v[q], parts[1])


def cell_maps_kernel(lift, mix, project, lift_mix, proj_t):
    same = iota((128, 384), 0) % 12 == iota((128, 384), 1) // 32
    pick = one_hot((128, 8), lambda a, b: (a // 12 == b) & (a < 60)).astype(BF)
    spread = one_hot((32, 384), lambda a, b: b % 32 == a)
    both = exact_dot(lift[...], mix[...], ((0,), (1,)))
    for out, rows in ((lift_mix, both), (proj_t, project[...])):
        rows = jnp.concatenate([exact_dot(rows, spread), jnp.zeros((3, 384), F32)], axis=0)
        for k, part in enumerate(split(rows)):
            out[k] = jnp.where(same, dot(pick, part), 0.0).astype(BF)


def spectrum_kernel(lift, spread, out, table):
    wide = exact_dot(lift[...], one_hot((32, 1024), lambda a, b: b // 32 == a), ((0,), (0,)))
    table[...] = jnp.zeros((256, 1024), F32)
    for f in range(F):
        table[f * 32 : f * 32 + 1, :] = wide[f : f + 1]
    tables = split(table[...])
    spread_v = spread.get()
    for q in range(2):
        for kx in range(2):
            rows = jnp.concatenate([spread_v[q, half, pl.ds(kx, 128, stride=2), :] for half in range(2)], axis=1)
            out[2 * q + kx] = dot3_table(rows, tables)


def emit_faces(state, ylo, yhi, zlo=None, zhi=None, xlo=None, xhi=None):
    edges, sides = ([], []), [jnp.zeros((8, 384), F32)] * 2
    for f in range(F):
        slabs = [state[f, y] for y in range(4)]
        ylo[f * 96 : f * 96 + 96, :] = slabs[0].astype(BF)
        yhi[f * 96 : f * 96 + 96, :] = slabs[3].astype(BF)
        edges[0].extend(s[0:1] for s in slabs)
        edges[1].extend(s[95:96] for s in slabs)
        cells = jnp.concatenate(slabs, axis=0).astype(BF)
        for k in range(2):
            pick = one_hot((8, 128), lambda a, b: (a == f) & (b == 127 * k)).astype(BF)
            sides[k] = sides[k] + dot(pick, cells, ((1,), (1,)))
    pad = jnp.zeros((8, 128), F32)
    faces = [jnp.concatenate(rows + [pad, pad[:4]], axis=0).astype(BF) for rows in edges]
    for side in sides:
        faces.append(jnp.concatenate([side[:, j * 128 : j * 128 + 128] for j in range(3)] + [pad], axis=0).astype(BF))
    if zlo is not None:
        for ref, face in zip((zlo, zhi, xlo, xhi), faces):
            ref[...] = face
    return faces


Y_FACES = [shape((480, 128), BF)] * 2
FACES = Y_FACES + [shape((32, 128), BF)] * 4


def advance(state, below, above, before, after, left, right, put):
    g = own_group()
    lane = iota((96, 128), 1)
    row = iota((96, 128), 0)
    left, right = (
        jnp.concatenate([x[j * 8 : j * 8 + 8] for j in range(3)], axis=1).astype(BF) for x in (left, right)
    )
    for f in range(F):
        pick = lambda lane_of: one_hot((8, 128), lambda a, b: (a == f) & (b == lane_of)).astype(BF)
        low_x = jnp.where(g == 0, 0.0, dot(left, pick(0), ((0,), (0,))))
        high_x = jnp.where(g == 2, 0.0, dot(right, pick(127), ((0,), (0,))))
        slabs = [below[f * 96 : f * 96 + 96, :].astype(F32)]
        slabs += [state[f, y] for y in range(4)]
        slabs += [above[f * 96 : f * 96 + 96, :].astype(F32)]
        for y in range(4):
            q = slabs[y + 1]
            yminus, yplus = slabs[y], slabs[y + 2]
            xminus = jnp.where(lane == 0, low_x[y * 96 : y * 96 + 96], pltpu.roll(q, 1, 1))
            xplus = jnp.where(lane == 127, high_x[y * 96 : y * 96 + 96], pltpu.roll(q, 127, 1))
            k = f * 4 + y
            zminus = jnp.where(row == 0, before[k : k + 1], pltpu.roll(q, 1, 0))
            zplus = jnp.where(row == 95, after[k : k + 1], pltpu.roll(q, 95, 0))
            carried = (
                state[0, y] * (xplus - xminus)
                + state[1, y] * (yplus - yminus)
                + state[2, y] * (zplus - zminus)
            )
            around = xplus + xminus + yplus + yminus + zplus + zminus - 6.0 * q
            put(f, y, q - ADVECT_RATE * carried + DIFFUSE_RATE * around)


def last_step_kernel(got, below, above, pool, fields, middle, new, *refs):
    snaps, (start, stepped, rows) = refs[:4], refs[4:]
    g = own_group()
    outside = g == 3
    faces = [got[source, 96:128, :].astype(F32) for source in neighbours()]
    for f in range(F):
        load_rows(fields, start, f)

    def put(f, y, value):
        stepped[f, y] = value
        new.ref[f, pl.ds(y, 96, stride=4), :] = jnp.where(outside, start[f, y], value)
        if y == 3:
            new.push(f)

    advance(middle.get(), below, above, *faces, put)
    rows[...] = jnp.zeros((512, 256), F32)
    for f in range(F):
        for base, cells in ((0, start), (64, stepped)):
            for y in range(2):
                pooled = pair_sums(cells, f, y)
                for dest in range(4):
                    at = dest * 128 + base + f * 12
                    rows[at : at + 12, y * 128 : y * 128 + 128] = pooled[dest * 12 : dest * 12 + 12]
    for d in range(4):
        at = pl.multiple_of(((g + d) % 4) * 128, 128)
        high, low = split(rows[pl.ds(at, 128), :])
        snaps[d][...] = (dot(pool[...], high, ((1,), (1,))) + dot(pool[...], low, ((1,), (1,)))).astype(BF)


def swap(x, axes):
    return lax.all_to_all(x, axes, 0, 0, tiled=True)


def shift(x, axis, step):
    size = lax.axis_size(axis)
    return lax.ppermute(x, axis, [(i, (i + step) % size) for i in range(size)])


def tied(*values):
    return lax.optimization_barrier(values)


def shards(fields, lift_weight, mix_weight, project_weight, spectral_weight):
    flat = fields.reshape(F, 384, 128)
    by_field = [(flat, functools.partial(int, f)) for f in range(F)]
    owner = ("grp", "col")
    state_space = pltpu.VMEM((F, 4, 96, 128), F32)

    first, ylo, yhi, *faces = call(
        first_kernel,
        [shape((16, 8, 256), F32)] + FACES,
        [],
        by_field + [(table_x_partial(), own_group)],
        [state_space, pltpu.VMEM((256, 256), F32)],
    )
    got = swap(first, "row")
    maps = call(
        cell_maps_kernel,
        [shape((2, 128, 384), BF)] * 2,
        [lift_weight, mix_weight, project_weight],
    )
    mixer = call(
        mixer_kernel,
        shape((2, 256, 256), F32),
        [lift_weight],
        [(spectral_weight.reshape(2, 256, 1024), None)],
    )
    first = call(
        first_yz_kernel, shape((16, 48, 256), BF), [got, table_y_first(), table_z_first(), *faces]
    )
    below, above = shift(yhi, "row", 1), shift(ylo, "row", -1)
    first, below, above = tied(first, below, above)
    got = swap(first, owner)
    got, mixer = tied(got, mixer)
    modes, spread, middle, ylo, yhi = call(
        mix_kernel,
        [shape((16, 128, 128), BF), shape((2, 2, 256, 128), F32), shape((F, 4, 96, 128), F32)] + Y_FACES,
        [got, below, above, table_select(), table_sum_fields(), mixer, flat],
        [(table_z_inverse(), own_group)],
        [pltpu.VMEM((1536, 128), F32), state_space],
        far={1: 1, 2: 1},
    )
    got = swap(modes, owner)
    got, maps = tied(got, maps)
    below, above = shift(yhi, "row", 1), shift(ylo, "row", -1)
    planes = call(inverse_y_kernel, shape((16, 8, 384), BF), [got, table_lanes(), table_y_inverse()])
    planes, below, above = tied(planes, below, above)
    new_fields, *snaps = call(
        last_step_kernel,
        [shape((F, 384, 128), F32)] + [shape((128, 128), BF)] * 4,
        [got, below, above, table_pool_x(), flat],
        [(middle, None)],
        [state_space, state_space, pltpu.VMEM((512, 256), F32)],
        far={0: F},
    )
    got = swap(planes, "row")
    for d in range(1, 4):
        snaps[d] = shift(snaps[d], "grp", d)
    back = call(
        cell_kernel,
        shape((16, 8, 384), BF),
        [got, *snaps, table_x_inverse(), *maps],
        scratch=[pltpu.VMEM((4, 128, 128), F32)],
    )
    got = swap(back, "row")
    back = call(
        back_yz_kernel,
        shape((16, 16, 1152), BF),
        [got, table_y_back(), np.ascontiguousarray(table_lanes().T)],
        [(table_z_back(), lambda: lax.axis_index("col") * 4 + own_group())],
        [pltpu.VMEM((512, 128), F32)],
    )
    got = swap(back, owner)
    spectrum = call(
        spectrum_kernel,
        shape((4, 128, 1024), F32),
        [lift_weight],
        [(spread, None)],
        [pltpu.VMEM((256, 1024), F32)],
    )
    grad = call(
        grad_kernel,
        shape((2, 128, 16, 128), BF),
        [got, table_expand(), spectrum],
        [],
        [pltpu.VMEM((256, 128), F32), pltpu.VMEM((2, 2048, 128), F32)],
        far={0: 2},
    )
    grad = grad.reshape(2, 16, 8, 8, 2, 128).transpose(0, 1, 2, 4, 3, 5)
    grad = with_layout_constraint(grad, Layout(major_to_minor=(0, 1, 2, 4, 3, 5)))
    return new_fields.reshape(fields.shape), grad.reshape(spectral_weight.shape)


def solution(mesh):
    placed = (P(None, "col", "row", "grp"), P(), P(), P(), P(None, "grp", "col", "row", None))
    return jax.shard_map(
        shards,
        mesh=mesh,
        in_specs=placed,
        out_specs=(P(None, "col", "row", "grp"), P(None, "grp", "col", "row", None)),
        check_vma=False,
    )
```

time: 158 us -> 126 us (0.80)
  blocking collectives: 45.4 us -> 18.2 us
  local copies, waits for them, and re-layouts: 21 us -> 2.41 us
  waiting for transfers between devices: 19.5 us -> 25.6 us
  starting transfers between devices: 49.6 us -> 55.1 us
  Pallas kernels: 20.3 us -> 23.1 us
    all_to_all x3 -> x1, blocking collectives: 45.4 us -> 18.2 us  [swap(): return lax.all_to_all(x, axes, 0, 0, tiled=True)]
    unnamed x63 -> x29, local copies, waits for them, and re-layouts: 18.3 us -> 0.17 us
    all_to_all x4 -> x5, starting transfers between devices: 24.9 us -> 38.7 us  [swap(): return lax.all_to_all(x, axes, 0, 0, tiled=True)]
    all_to_all x4 -> x5, waiting for transfers between devices: 13.4 us -> 22.7 us  [swap(): return lax.all_to_all(x, axes, 0, 0, tiled=True)]
    ppermute x12 -> x7, starting transfers between devices: 24.8 us -> 16.3 us  [shift(): return lax.ppermute(x, axis, [(i, (i + step) % size) for i in range(size)])]
    ppermute x12 -> x7, waiting for transfers between devices: 6.15 us -> 2.86 us  [shift(): return lax.ppermute(x, axis, [(i, (i + step) % size) for i in range(size)])]
    pallas_call x12 -> x11, Pallas kernels: 20.3 us -> 23.1 us  [call(): pl.pallas_call(kernel, out_shape=[pltpu.HBM(o.shape, o.dtype) if k in far...]
  transfers between devices with their start and end apart: 16 -> 12, of which waited for: 4 -> 8; matrix products, arithmetic and copies ran while one was open for 1% -> 2% of each run, Pallas kernels for 7% -> 9%
where the time goes in v2:
time: 126 us; the launch traced here: 125 us
  starting transfers between devices  55.1 us (44%)
  waiting for transfers between devices  25.6 us (20%)
  Pallas kernels  23.1 us (18%)
  blocking collectives  18.2 us (14%)
  local copies, waits for them, and re-layouts  2.41 us (2%)
    all_to_all x5, starting transfers between devices, swap(): return lax.all_to_all(x, axes, 0, 0, tiled=True)  38.7 us
    pallas_call x11, Pallas kernels, call(): pl.pallas_call(kernel, out_shape=[pltpu.HBM(o.shape, o.dtype) if k in far...  23.1 us
    all_to_all x5, waiting for transfers between devices, swap(): return lax.all_to_all(x, axes, 0, 0, tiled=True)  22.7 us
    all_to_all x1, blocking collectives, swap(): return lax.all_to_all(x, axes, 0, 0, tiled=True)  18.2 us
    ppermute x7, starting transfers between devices, shift(): return lax.ppermute(x, axis, [(i, (i + step) % size) for i in range(size)])  16.3 us
    ppermute x7, waiting for transfers between devices, shift(): return lax.ppermute(x, axis, [(i, (i + step) % size) for i in range(size)])  2.86 us
  transfers between devices with their start and end apart: 12, of which 8 were waited for; matrix products, arithmetic and copies ran while one was open for 2% of the time, Pallas kernels for 9%

profile of v2, /device:TPU:1, one launch (start us, length us, event | category | flops | bytes accessed | tf_op | source)
XLA Modules:
  0.0 125.4 jit_solution(17108660910847256171)
XLA Ops:
  0.7 2.5 %shard_map.194 = (f32[16,8,256]{2,1,0:T(8,128)}, bf16[480,128]{1,0:T(8,128)(2,1)S(1)}, bf16[480,128]{1,0:T(8,128)(2,1)S(1)}, bf16[32,128]{1,0:T(8,128)(2,1)S(1)}...) custom-call(f32[5,384,128]{2,1,0:T(8,128)} %bitcast.7, ...), custom_call_target="tpu_custom_call" | custom-call | tf_op jit(solution)/shard_map/pallas_call | solution.py:275
  3.1 11.8 %all-to-all-start = ((f32[16,8,256]{2,1,0:T(8,128)}), f32[16,8,256]{2,1,0:T(8,128)S(1)}, u32[]{:S(2)}, u32[]{:S(2)}) async-start(f32[16,8,256]{2,1,0:T(8,128)} %get-tuple-element.32), calls=%async_computation | async-start | bytes 262144 | tf_op jit(solution)/shard_map/all_to_all | solution.py:637
  14.9 2.3 %collective-permute-start = (bf16[480,128]{1,0:T(8,128)(2,1)S(1)}, bf16[480,128]{1,0:T(8,128)(2,1)S(1)}, u32[]{:S(2)}, u32[]{:S(2)}) collective-permute-start(bf16[480,128]{1,0:T(8,128)(2,1)S(1)} %get-tuple-element.37), channel_id=1, source_target_pairs={{0,4},{4,8},{8,12},{12,16},{16,20},{20,24},{24,28},{28,32},{32,36}... | collective-permute-start | bytes 368648 | tf_op jit(solution)/shard_map/ppermute | solution.py:642
  17.2 3.5 %collective-permute-start.1 = (bf16[480,128]{1,0:T(8,128)(2,1)S(1)}, bf16[480,128]{1,0:T(8,128)(2,1)S(1)}, u32[]{:S(2)}, u32[]{:S(2)}) collective-permute-start(bf16[480,128]{1,0:T(8,128)(2,1)S(1)} %get-tuple-element.38), channel_id=1, source_target_pairs={{0,60},{4,0},{8,4},{12,8},{16,12},{20,16},{24,20},{28,24},{32,28},... | collective-permute-start | bytes 368648 | tf_op jit(solution)/shard_map/ppermute | solution.py:642
  20.7 3.9 %all-to-all-done.refs_0_ = f32[16,8,256]{2,1,0:T(8,128)S(1)} async-done(((f32[16,8,256]{2,1,0:T(8,128)}), f32[16,8,256]{2,1,0:T(8,128)S(1)}, u32[]{:S(2)}, u32[]{:S(2)}) %all-to-all-start) | async-done | bytes 131104 | tf_op jit(solution)/shard_map/all_to_all | solution.py:637
  24.6 1.4 %shard_map.195 = bf16[16,48,256]{2,1,0:T(8,128)(2,1)} custom-call(f32[16,8,256]{2,1,0:T(8,128)S(1)} %all-to-all-done.refs_0_, bf16[2,128,128]{2,1,0:T(8,128)(2,1)S(1)} %copy-done.10, bf16[2,2,256,512]{3,2,1,0:T(8,128)(2,1)S(1)} %copy-done.2, bf16[32,128]{1,0:T(8,128)(2,1)S(1)} %get-tuple-element.33.refs_3_, bf16[32,128]{1,0:T(8,128)(2,1)S(1)} %get-tuple-element.34.refs_4_, ...), custom_call_target="tpu_custom_call" | custom-call | tf_op jit(solution)/shard_map/pallas_call | solution.py:275
  26.5 8.7 %all-to-all-start.1 = ((bf16[16,48,256]{2,1,0:T(8,128)(2,1)}), bf16[16,48,256]{2,1,0:T(8,128)(2,1)S(1)}, u32[]{:S(2)}, u32[]{:S(2)}) async-start(bf16[16,48,256]{2,1,0:T(8,128)(2,1)} %shard_map.195), calls=%async_computation.1 | async-start | bytes 786432 | tf_op jit(solution)/shard_map/all_to_all | solution.py:637
  35.3 2.2 %reshape.20.refs_1_ = bf16[2,256,1024]{2,1,0:T(8,128)(2,1)} reshape(bf16[2,16,8,2,1024]{4,3,2,1,0:T(2,128)(2,1)} %param.23) | data formatting | bytes 2097152 | tf_op jit(solution)/shard_map/reshape | solution.py:672
  37.5 2.0 %shard_map.196.refs_5_ = f32[2,256,256]{2,1,0:T(8,128)S(1)} custom-call(f32[32,5]{1,0:T(8,128)S(1)} %copy.21.refs_0_, bf16[2,256,1024]{2,1,0:T(8,128)(2,1)} %reshape.20.refs_1_), custom_call_target="tpu_custom_call" | custom-call | tf_op jit(solution)/shard_map/pallas_call | solution.py:275
  39.6 4.0 %all-to-all-done.1.refs_0_ = bf16[16,48,256]{2,1,0:T(8,128)(2,1)S(1)} async-done(((bf16[16,48,256]{2,1,0:T(8,128)(2,1)}), bf16[16,48,256]{2,1,0:T(8,128)(2,1)S(1)}, u32[]{:S(2)}, u32[]{:S(2)}) %all-to-all-start.1) | async-done | bytes 393248 | tf_op jit(solution)/shard_map/all_to_all | solution.py:637
  43.6 3.7 %shard_map.197 = (bf16[16,128,128]{2,1,0:T(8,128)(2,1)}, f32[2,2,256,128]{3,2,1,0:T(8,128)}, f32[5,4,96,128]{3,2,1,0:T(8,128)}, bf16[480,128]{1,0:T(8,128)(2,1)S(1)}, bf16[480,128]{1,0:T(8,128)(2,1)}) custom-call(bf16[16,48,256]{2,1,0:T(8,128)(2,1)S(1)} %all-to-all-done.1.refs_0_, bf16[480,128]{1,0:T(8,128)(2,1)S(1)} %collective-permute-done.refs_1_, ...), custom_call_target="tpu_custom_call" | custom-call | tf_op jit(solution)/shard_map/pallas_call | solution.py:275
  47.3 4.5 %all-to-all-start.2 = ((bf16[16,128,128]{2,1,0:T(8,128)(2,1)}), bf16[16,128,128]{2,1,0:T(8,128)(2,1)S(1)}, u32[]{:S(2)}, u32[]{:S(2)}) async-start(bf16[16,128,128]{2,1,0:T(8,128)(2,1)} %get-tuple-element.44), calls=%async_computation.2 | async-start | bytes 1048576 | tf_op jit(solution)/shard_map/all_to_all | solution.py:637
  52.7 4.8 %collective-permute-start.3 = (bf16[480,128]{1,0:T(8,128)(2,1)S(1)}, bf16[480,128]{1,0:T(8,128)(2,1)S(1)}, u32[]{:S(2)}, u32[]{:S(2)}) collective-permute-start(bf16[480,128]{1,0:T(8,128)(2,1)S(1)} %get-tuple-element.49), channel_id=1, source_target_pairs={{0,60},{4,0},{8,4},{12,8},{16,12},{20,16},{24,20},{28,24},{32,28},... | collective-permute-start | bytes 368648 | tf_op jit(solution)/shard_map/ppermute | solution.py:642
  58.3 6.3 %all-to-all-done.2.refs_0_ = bf16[16,128,128]{2,1,0:T(8,128)(2,1)S(1)} async-done(((bf16[16,128,128]{2,1,0:T(8,128)(2,1)}), bf16[16,128,128]{2,1,0:T(8,128)(2,1)S(1)}, u32[]{:S(2)}, u32[]{:S(2)}) %all-to-all-start.2) | async-done | bytes 524320 | tf_op jit(solution)/shard_map/all_to_all | solution.py:637
  66.2 5.1 %all-to-all-start.3 = ((bf16[16,8,384]{2,1,0:T(8,128)(2,1)}), bf16[16,8,384]{2,1,0:T(8,128)(2,1)S(1)}, u32[]{:S(2)}, u32[]{:S(2)}) async-start(bf16[16,8,384]{2,1,0:T(8,128)(2,1)} %shard_map.199), calls=%async_computation.3 | async-start | bytes 196608 | tf_op jit(solution)/shard_map/all_to_all | solution.py:637
  71.4 3.3 %shard_map.200 = (f32[5,384,128]{2,1,0:T(8,128)}, bf16[128,128]{1,0:T(8,128)(2,1)S(1)}, bf16[128,128]{1,0:T(8,128)(2,1)S(1)}, bf16[128,128]{1,0:T(8,128)(2,1)S(1)}, bf16[128,128]{1,0:T(8,128)(2,1)S(1)}) custom-call(bf16[16,128,128]{2,1,0:T(8,128)(2,1)S(1)} %all-to-all-done.2.refs_0_, bf16[480,128]{1,0:T(8,128)(2,1)S(1)} %collective-permute-done.2.refs_1_, ...), custom_call_target="tpu_custom_call" | custom-call | tf_op jit(solution)/shard_map/pallas_call | solution.py:275
  76.0 2.4 %collective-permute-start.5 = (bf16[128,128]{1,0:T(8,128)(2,1)S(1)}, bf16[128,128]{1,0:T(8,128)(2,1)S(1)}, u32[]{:S(2)}, u32[]{:S(2)}) collective-permute-start(bf16[128,128]{1,0:T(8,128)(2,1)S(1)} %get-tuple-element.57), channel_id=1, source_target_pairs={{0,128},{64,192},{128,0},{192,64},{1,129},{65,193},{129,1},{193,65... | collective-permute-start | bytes 98312 | tf_op jit(solution)/shard_map/ppermute | solution.py:642
  81.7 2.0 %shard_map.201 = bf16[16,8,384]{2,1,0:T(8,128)(2,1)S(1)} custom-call(bf16[16,8,384]{2,1,0:T(8,128)(2,1)S(1)} %all-to-all-done.3.refs_0_, bf16[128,128]{1,0:T(8,128)(2,1)S(1)} %get-tuple-element.55.refs_1_, bf16[128,128]{1,0:T(8,128)(2,1)S(1)} %collective-permute-done.4.refs_2_, bf16[128,128]{1,0:T(8,128)(2,1)S(1)} %collective-permute-done.5.refs_3_, ...), custom_call_target="tpu_custom_call" | custom-call | tf_op jit(solution)/shard_map/pallas_call | solution.py:275
  83.6 18.2 %all_to_all.30.refs_0_ = bf16[16,8,384]{2,1,0:T(8,128)(2,1)S(1)} all-to-all(bf16[16,8,384]{2,1,0:T(8,128)(2,1)S(1)} %shard_map.201), channel_id=1, replica_groups=mesh['grp'=4,'row'=16,'col'=4] {'row'}, dimensions={0} | all-to-all | bytes 196608 | tf_op jit(solution)/shard_map/all_to_all | solution.py:637
  101.8 2.4 %shard_map.202 = bf16[16,16,1152]{2,1,0:T(8,128)(2,1)} custom-call(bf16[16,8,384]{2,1,0:T(8,128)(2,1)S(1)} %all_to_all.30.refs_0_, bf16[2,128,128]{2,1,0:T(8,128)(2,1)S(1)} %copy-done.7, bf16[512,512]{1,0:T(8,128)(2,1)S(1)} %copy-done.1, bf16[16,2,64,32]{3,2,1,0:T(8,128)(2,1)} %constant.36.clone.refs_3_), custom_call_target="tpu_custom_call" | custom-call | tf_op jit(solution)/shard_map/pallas_call | solution.py:275
  104.2 8.6 %all-to-all-start.5 = ((bf16[16,16,1152]{2,1,0:T(8,128)(2,1)}), bf16[16,16,1152]{2,1,0:T(8,128)(2,1)S(1)}, u32[]{:S(2)}, u32[]{:S(2)}) async-start(bf16[16,16,1152]{2,1,0:T(8,128)(2,1)} %shard_map.202), calls=%async_computation.5 | async-start | bytes 1179648 | tf_op jit(solution)/shard_map/all_to_all | solution.py:637
  112.8 2.0 %shard_map.203.refs_2_ = f32[4,128,1024]{2,1,0:T(8,128)S(1)} custom-call(f32[32,5]{1,0:T(8,128)S(1)} %copy.21.refs_0_, f32[2,2,256,128]{3,2,1,0:T(8,128)} %get-tuple-element.61.refs_1_), custom_call_target="tpu_custom_call" | custom-call | tf_op jit(solution)/shard_map/pallas_call | solution.py:275
  114.8 8.5 %all-to-all-done.5.refs_0_ = bf16[16,16,1152]{2,1,0:T(8,128)(2,1)S(1)} async-done(((bf16[16,16,1152]{2,1,0:T(8,128)(2,1)}), bf16[16,16,1152]{2,1,0:T(8,128)(2,1)S(1)}, u32[]{:S(2)}, u32[]{:S(2)}) %all-to-all-start.5) | async-done | bytes 589856 | tf_op jit(solution)/shard_map/all_to_all | solution.py:637
  123.3 1.9 %shard_map.204 = bf16[2,128,16,128]{3,2,1,0:T(8,128)(2,1)} custom-call(bf16[16,16,1152]{2,1,0:T(8,128)(2,1)S(1)} %all-to-all-done.5.refs_0_, bf16[256,256]{1,0:T(8,128)(2,1)S(1)} %copy-done.6, f32[4,128,1024]{2,1,0:T(8,128)S(1)} %shard_map.203.refs_2_), custom_call_target="tpu_custom_call" | custom-call | tf_op jit(solution)/shard_map/pallas_call | solution.py:275
  (42 shorter events, 8.4 us)
Async XLA Ops:
  0.6 24.0 %copy-start.2 = (bf16[2,2,256,512]{3,2,1,0:T(8,128)(2,1)S(1)}, bf16[2,2,256,512]{3,2,1,0:T(8,128)(2,1)}, u32[]{:S(2)}) copy-start(bf16[2,2,256,512]{3,2,1,0:T(8,128)(2,1)} %constant.28.clone.refs_2_) | copy-start | bytes 3145732
  0.6 24.0 %copy-start.10 = (bf16[2,128,128]{2,1,0:T(8,128)(2,1)S(1)}, bf16[2,128,128]{2,1,0:T(8,128)(2,1)}, u32[]{:S(2)}) copy-start(bf16[2,128,128]{2,1,0:T(8,128)(2,1)} %constant.27.clone.refs_1_) | copy-start | bytes 196612
  3.1 32.1 %copy-start.13 = (f32[32,5]{0,1:T(8,128)S(1)}, f32[32,5]{0,1:T(8,128)}, u32[]{:S(2)}) copy-start(f32[32,5]{0,1:T(8,128)} %param.20) | copy-start | bytes 1924
  3.1 21.5 %all-to-all-start = ((f32[16,8,256]{2,1,0:T(8,128)}), f32[16,8,256]{2,1,0:T(8,128)S(1)}, u32[]{:S(2)}, u32[]{:S(2)}) async-start(f32[16,8,256]{2,1,0:T(8,128)} %get-tuple-element.32), calls=%async_computation | async-start | bytes 262144 | tf_op jit(solution)/shard_map/all_to_all | solution.py:637
  14.9 11.1 %collective-permute-start = (bf16[480,128]{1,0:T(8,128)(2,1)S(1)}, bf16[480,128]{1,0:T(8,128)(2,1)S(1)}, u32[]{:S(2)}, u32[]{:S(2)}) collective-permute-start(bf16[480,128]{1,0:T(8,128)(2,1)S(1)} %get-tuple-element.37), channel_id=1, source_target_pairs={{0,4},{4,8},{8,12},{12,16},{16,20},{20,24},{24,28},{28,32},{32,36}... | collective-permute-start | bytes 368648 | tf_op jit(solution)/shard_map/ppermute | solution.py:642
  17.2 9.3 %collective-permute-start.1 = (bf16[480,128]{1,0:T(8,128)(2,1)S(1)}, bf16[480,128]{1,0:T(8,128)(2,1)S(1)}, u32[]{:S(2)}, u32[]{:S(2)}) collective-permute-start(bf16[480,128]{1,0:T(8,128)(2,1)S(1)} %get-tuple-element.38), channel_id=1, source_target_pairs={{0,60},{4,0},{8,4},{12,8},{16,12},{20,16},{24,20},{28,24},{32,28},... | collective-permute-start | bytes 368648 | tf_op jit(solution)/shard_map/ppermute | solution.py:642
  26.0 17.6 %copy-start.5 = (bf16[512,128]{1,0:T(8,128)(2,1)S(1)}, bf16[512,128]{1,0:T(8,128)(2,1)}, u32[]{:S(2)}) copy-start(bf16[512,128]{1,0:T(8,128)(2,1)} %constant.31.clone.refs_4_) | copy-start | bytes 393220
  26.0 17.6 %copy-start.9 = (bf16[128,256]{1,0:T(8,128)(2,1)S(1)}, bf16[128,256]{1,0:T(8,128)(2,1)}, u32[]{:S(2)}) copy-start(bf16[128,256]{1,0:T(8,128)(2,1)} %constant.30.clone.refs_3_) | copy-start | bytes 196612
  26.5 17.1 %all-to-all-start.1 = ((bf16[16,48,256]{2,1,0:T(8,128)(2,1)}), bf16[16,48,256]{2,1,0:T(8,128)(2,1)S(1)}, u32[]{:S(2)}, u32[]{:S(2)}) async-start(bf16[16,48,256]{2,1,0:T(8,128)(2,1)} %shard_map.195), calls=%async_computation.1 | async-start | bytes 786432 | tf_op jit(solution)/shard_map/all_to_all | solution.py:637
  39.6 18.0 %copy-start.11 = (f32[32,32]{1,0:T(8,128)S(1)}, f32[32,32]{1,0:T(8,128)}, u32[]{:S(2)}) copy-start(f32[32,32]{1,0:T(8,128)} %refs_1_.5) | copy-start | bytes 12292
  39.6 18.0 %copy-start.12 = (f32[5,32]{1,0:T(8,128)S(1)}, f32[5,32]{1,0:T(8,128)}, u32[]{:S(2)}) copy-start(f32[5,32]{1,0:T(8,128)} %refs_2_.4) | copy-start | bytes 1924
  39.6 25.1 %copy-start.1 = (bf16[512,512]{1,0:T(8,128)(2,1)S(1)}, bf16[512,512]{1,0:T(8,128)(2,1)}, u32[]{:S(2)}) copy-start(bf16[512,512]{1,0:T(8,128)(2,1)} %constant.32.clone.refs_1_.refs_2_) | copy-start | bytes 1572868
  39.6 25.1 %copy-start.3 = (bf16[2,128,512]{2,1,0:T(8,128)(2,1)S(1)}, bf16[2,128,512]{2,1,0:T(8,128)(2,1)}, u32[]{:S(2)}) copy-start(bf16[2,128,512]{2,1,0:T(8,128)(2,1)} %constant.33.clone.refs_2_) | copy-start | bytes 786436
  39.6 31.8 %copy-start.8 = (bf16[128,256]{1,0:T(8,128)(2,1)S(1)}, bf16[128,256]{1,0:T(8,128)(2,1)}, u32[]{:S(2)}) copy-start(bf16[128,256]{1,0:T(8,128)(2,1)} %constant.34.clone.refs_3_) | copy-start | bytes 196612
  47.3 17.4 %all-to-all-start.2 = ((bf16[16,128,128]{2,1,0:T(8,128)(2,1)}), bf16[16,128,128]{2,1,0:T(8,128)(2,1)S(1)}, u32[]{:S(2)}, u32[]{:S(2)}) async-start(bf16[16,128,128]{2,1,0:T(8,128)(2,1)} %get-tuple-element.44), calls=%async_computation.2 | async-start | bytes 1048576 | tf_op jit(solution)/shard_map/all_to_all | solution.py:637
  51.8 14.4 %collective-permute-start.2 = (bf16[480,128]{1,0:T(8,128)(2,1)}, bf16[480,128]{1,0:T(8,128)(2,1)S(1)}, u32[]{:S(2)}, u32[]{:S(2)}) collective-permute-start(bf16[480,128]{1,0:T(8,128)(2,1)} %get-tuple-element.48), channel_id=1, source_target_pairs={{0,4},{4,8},{8,12},{12,16},{16,20},{20,24},{24,28},{28,32},{32,36}... | collective-permute-start | bytes 368648 | tf_op jit(solution)/shard_map/ppermute | solution.py:642
  52.7 13.5 %collective-permute-start.3 = (bf16[480,128]{1,0:T(8,128)(2,1)S(1)}, bf16[480,128]{1,0:T(8,128)(2,1)S(1)}, u32[]{:S(2)}, u32[]{:S(2)}) collective-permute-start(bf16[480,128]{1,0:T(8,128)(2,1)S(1)} %get-tuple-element.49), channel_id=1, source_target_pairs={{0,60},{4,0},{8,4},{12,8},{16,12},{20,16},{24,20},{28,24},{32,28},... | collective-permute-start | bytes 368648 | tf_op jit(solution)/shard_map/ppermute | solution.py:642
  65.9 35.9 %copy-start.7 = (bf16[2,128,128]{2,1,0:T(8,128)(2,1)S(1)}, bf16[2,128,128]{2,1,0:T(8,128)(2,1)}, u32[]{:S(2)}) copy-start(bf16[2,128,128]{2,1,0:T(8,128)(2,1)} %constant.37.clone.refs_1_) | copy-start | bytes 196612
  66.2 15.4 %all-to-all-start.3 = ((bf16[16,8,384]{2,1,0:T(8,128)(2,1)}), bf16[16,8,384]{2,1,0:T(8,128)(2,1)S(1)}, u32[]{:S(2)}, u32[]{:S(2)}) async-start(bf16[16,8,384]{2,1,0:T(8,128)(2,1)} %shard_map.199), calls=%async_computation.3 | async-start | bytes 196608 | tf_op jit(solution)/shard_map/all_to_all | solution.py:637
  74.7 4.9 %collective-permute-start.4 = (bf16[128,128]{1,0:T(8,128)(2,1)S(1)}, bf16[128,128]{1,0:T(8,128)(2,1)S(1)}, u32[]{:S(2)}, u32[]{:S(2)}) collective-permute-start(bf16[128,128]{1,0:T(8,128)(2,1)S(1)} %get-tuple-element.56), channel_id=1, source_target_pairs={{0,64},{64,128},{128,192},{192,0},{1,65},{65,129},{129,193},{193,1... | collective-permute-start | bytes 98312 | tf_op jit(solution)/shard_map/ppermute | solution.py:642
  76.0 4.6 %collective-permute-start.5 = (bf16[128,128]{1,0:T(8,128)(2,1)S(1)}, bf16[128,128]{1,0:T(8,128)(2,1)S(1)}, u32[]{:S(2)}, u32[]{:S(2)}) collective-permute-start(bf16[128,128]{1,0:T(8,128)(2,1)S(1)} %get-tuple-element.57), channel_id=1, source_target_pairs={{0,128},{64,192},{128,0},{192,64},{1,129},{65,193},{129,1},{193,65... | collective-permute-start | bytes 98312 | tf_op jit(solution)/shard_map/ppermute | solution.py:642
  78.4 3.3 %collective-permute-start.6 = (bf16[128,128]{1,0:T(8,128)(2,1)S(1)}, bf16[128,128]{1,0:T(8,128)(2,1)S(1)}, u32[]{:S(2)}, u32[]{:S(2)}) collective-permute-start(bf16[128,128]{1,0:T(8,128)(2,1)S(1)} %get-tuple-element.58), channel_id=1, source_target_pairs={{0,192},{64,0},{128,64},{192,128},{1,193},{65,1},{129,65},{193,129... | collective-permute-start | bytes 98312 | tf_op jit(solution)/shard_map/ppermute | solution.py:642
  104.2 19.1 %copy-start.6 = (bf16[256,256]{1,0:T(8,128)(2,1)S(1)}, bf16[256,256]{1,0:T(8,128)(2,1)}, u32[]{:S(2)}) copy-start(bf16[256,256]{1,0:T(8,128)(2,1)} %constant.38.clone.refs_1_) | copy-start | bytes 393220
  104.2 19.1 %all-to-all-start.5 = ((bf16[16,16,1152]{2,1,0:T(8,128)(2,1)}), bf16[16,16,1152]{2,1,0:T(8,128)(2,1)S(1)}, u32[]{:S(2)}, u32[]{:S(2)}) async-start(bf16[16,16,1152]{2,1,0:T(8,128)(2,1)} %shard_map.202), calls=%async_computation.5 | async-start | bytes 1179648 | tf_op jit(solution)/shard_map/all_to_all | solution.py:637
  (2 other events, 34.6 us)

commit v3 on v2

--- a/solution.py
+++ b/solution.py
@@ -202,10 +202,10 @@
     return dot(table[0], high, dims) + dot(table[0], low, dims) + dot(table[1], high, dims)
 
 
-def dot3(x, y):
-    xh, xl = split(x)
-    yh, yl = split(y)
-    return dot(xh, yh) + dot(xl, yh) + dot(xh, yl)
+def stacked_dot3(table, x):
+    high, low = split(x)
+    left = jnp.concatenate([table[0], table[0], table[1]], axis=1)
+    return dot(left, jnp.concatenate([high, low, high], axis=0))
 
 
 def iota(shape, dim):
@@ -293,7 +293,7 @@
 
 def first_kernel(*refs):
     fields, table, out = refs[:F], refs[F], refs[F + 1]
-    faces, state, rows = refs[F + 2 : F + 8], refs[F + 8], refs[F + 9]
+    slabs, faces, (state, rows, face) = refs[F + 2 : F + 6], refs[F + 6 : F + 10], refs[F + 10 :]
     rows[240:256, :] = jnp.zeros((16, 256), F32)
     for f in range(F):
         cells = fields[f].get()
@@ -303,7 +303,7 @@
             rows[f * 48 : f * 48 + 48, y * 128 : y * 128 + 128] = pair_sums(state, f, y)
     result = table_dot3(table.get(), rows[...], ((1,), (1,)))
     out[...] = result.reshape(16, 8, 256)
-    emit_faces(state, *faces)
+    emit_faces(state, slabs, faces, face)
 
 
 def load_rows(fields, state, f):
@@ -316,12 +316,18 @@
     return (parts[0] + parts[1]) + (parts[2] + parts[3])
 
 
+def fine_sums(fields, f, y):
+    parts = [fields[f, pl.ds(2 * y + k, 48, stride=8), :] for k in (0, 1, 4, 5)]
+    return (parts[0] + parts[1]) + (parts[2] + parts[3])
+
+
 def neighbours():
     g, c = own_group(), lax.axis_index("col")
-    return (g * 4 + (c + 3) % 4, g * 4 + (c + 1) % 4, ((g + 3) % 4) * 4 + c, ((g + 1) % 4) * 4 + c)
-
-
-def first_yz_kernel(got, ty, tz, zlo, zhi, xlo, xhi, out):
+    steps = ((0, 3), (0, 1), (3, 0), (1, 0), (3, 3), (3, 1), (1, 3), (1, 1))
+    return [((g + a) % 4) * 4 + (c + b) % 4 for a, b in steps]
+
+
+def first_yz_kernel(got, ty, tz, out):
     both = table_dot3(ty, got[...].reshape(128, 256))
     high, low = split(both)
     parts = []
@@ -337,10 +343,42 @@
                 rows, cols = slice(c * 16, c * 16 + 16), slice(g * 128, g * 128 + 128)
                 out[g * 4 + c, 0:16, lanes] = high[rows, cols]
                 out[g * 4 + c, 16:32, lanes] = low[rows, cols]
-                out[g * 4 + c, 32:48, lanes] = jnp.zeros((16, 128), BF)
-    for dest, face in zip(neighbours(), (zlo, zhi, xlo, xhi)):
-        out[dest, 32:48, 0:128] = face[0:16, :]
-        out[dest, 32:48, 128:256] = face[16:32, :]
+
+
+def add_faces_kernel(modes, below, above, zlo, zhi, xlo, xhi, out, kept, face):
+    kept.ref[0] = below[...]
+    kept.ref[1] = above[...]
+    kept.push(0)
+    out[:, 0:32, :] = modes[...]
+    out[:, 32:64, :] = jnp.zeros((16, 32, 256), BF)
+    for k, ref in enumerate((zlo, zhi, xlo, xhi)):
+        face[k] = ref[...].astype(F32)
+    sides = [jnp.zeros((16, 96), F32)] * 2
+    for f in range(F):
+        for k, ref in enumerate((below, above)):
+            slab = ref[f * 96 : f * 96 + 96, :]
+            pick = one_hot((16, 128), lambda a, b: ((a == f) & (b == 0)) | ((a == 8 + f) & (b == 127)))
+            sides[k] = sides[k] + dot(pick.astype(BF), slab, ((1,), (1,)))
+            slab = slab.astype(F32)
+            face[0, f * 6 + 5 * k : f * 6 + 5 * k + 1, :] = slab[0:1]
+            face[1, f * 6 + 5 * k : f * 6 + 5 * k + 1, :] = slab[95:96]
+    for k, side in enumerate(sides):
+        face[2, 25 * k : 25 * k + 5, 0:96] = side[0:5]
+        face[3, 25 * k : 25 * k + 5, 0:96] = side[8:13]
+    before, after, left, right, *corners = neighbours()
+    zlo_v, zhi_v, xlo_v, xhi_v = (face[k].astype(BF) for k in range(4))
+    for dest, value in (
+        (before, zlo_v),
+        (after, zhi_v),
+        (left, xlo_v),
+        (right, xhi_v),
+        (corners[0], zlo_v),
+        (corners[1], zhi_v),
+        (corners[2], zlo_v),
+        (corners[3], zhi_v),
+    ):
+        out[dest, 32:64, 0:128] = value[0:32]
+        out[dest, 32:64, 128:256] = value[32:64]
 
 
 def dot3_table(x, table):
@@ -348,9 +386,7 @@
     return dot(high, table[0]) + dot(low, table[0]) + dot(high, table[1])
 
 
-def mix_kernel(
-    got, below, above, select, sum_fields, weights, fields, tz, out, spread_out, middle, ylo, yhi, cells, state
-):
+def mix_kernel(got, select, sum_fields, weights, tz, out, spread_out, near, cells):
     kz = iota((16, 128), 1) % 16
     re_sum, im_sum = 0.0, 0.0
     for c in range(4):
@@ -373,19 +409,11 @@
         for half in range(2):
             spread_out.ref[q, half] = spread[q * 256 : q * 256 + 256, half * 128 : half * 128 + 128]
     spread_out.push(0)
-    faces = []
-    for source in neighbours():
-        block = got[source, 32:48, :]
-        faces.append(jnp.concatenate([block[:, :128], block[:, 128:]], axis=0).astype(F32))
-    for f in range(F):
-        load_rows(fields, state, f)
-
-    def put(f, y, value):
-        middle.ref[f, y] = value
-
-    advance(state, below, above, *faces, put)
-    middle.push(0)
-    faces = emit_faces(middle.ref, ylo, yhi)
+    for k, source in enumerate(neighbours()):
+        block = got[source, 32:64, :]
+        near.ref[k, 0:32, :] = block[:, :128]
+        near.ref[k, 32:64, :] = block[:, 128:]
+    near.push(0)
     sr, si = spread[:256], spread[256:]
     wr, wi = weights[0], weights[1]
     mixed = jnp.concatenate([sr * wr - si * wi, sr * wi + si * wr], axis=1)
@@ -405,24 +433,23 @@
             parts.append(jnp.where(first, a, b))
         columns.append(jnp.concatenate(parts, axis=0))
     stacked = jnp.concatenate(columns, axis=1)
-    result = table_dot3(tz.get(), stacked)
+    result = stacked_dot3(tz.get(), stacked)
     for ky in range(8):
         cells[pl.ds(ky, 192, stride=8), :] = result[:, ky * 128 : ky * 128 + 128]
-    out[:, 0:96, :] = cells[...].reshape(16, 96, 128).astype(BF)
-    out[:, 96:128, :] = jnp.zeros((16, 32, 128), BF)
-    for dest, face in zip(neighbours(), faces):
-        out[dest, 96:128, :] = face
+    out[...] = cells[...].reshape(16, 96, 128).astype(BF)
 
 
 def inverse_y_kernel(got, lanes, ty, out):
-    rows = got[:, 0:96, :].astype(F32)
-    thirds = []
-    for z3 in range(3):
-        wide = jnp.concatenate(
-            [rows[:, z * 8 : z * 8 + 8, :].reshape(128, 128) for z in range(4 * z3, 4 * z3 + 4)], axis=1
-        ).astype(BF)
-        moved = dot(wide, lanes[...])
-        thirds.append(jnp.concatenate([moved[:, k * 128 : k * 128 + 128] for k in range(4)], axis=0))
+    rows = got[...].astype(F32)
+    wide = [
+        jnp.concatenate([rows[:, z * 8 : z * 8 + 8, :].reshape(128, 128) for z in range(z3, z3 + 4)], axis=1)
+        for z3 in (0, 4, 8)
+    ]
+    moved = dot(jnp.concatenate(wide, axis=0).astype(BF), lanes[...])
+    thirds = [
+        jnp.concatenate([moved[k : k + 128, n * 128 : n * 128 + 128] for n in range(4)], axis=0)
+        for k in (0, 128, 256)
+    ]
     stacked = jnp.concatenate(thirds, axis=1).astype(BF)
     out[...] = table_dot(ty, stacked).reshape(16, 8, 384).astype(BF)
 
@@ -454,16 +481,18 @@
 def back_yz_kernel(got, ty, lanes, tz, out, cells):
     rows = got[...].astype(F32).reshape(128, 384).astype(BF)
     modes = table_dot(ty, rows)
-    lanes_v = lanes[...]
-    for z3 in range(3):
-        wide = jnp.concatenate(
-            [modes[k * 32 : k * 32 + 32, z3 * 128 : z3 * 128 + 128] for k in range(4)], axis=1
-        )
-        high, low = split(wide)
-        moved = dot(high, lanes_v) + dot(low, lanes_v)
-        for z4 in range(4):
-            z = z3 * 4 + z4
-            cells[z * 32 : z * 32 + 32, :] = moved[:, z4 * 128 : z4 * 128 + 128]
+    wide = jnp.concatenate(
+        [
+            jnp.concatenate([modes[k * 32 : k * 32 + 32, z3 : z3 + 128] for k in range(4)], axis=1)
+            for z3 in (0, 128, 256)
+        ],
+        axis=0,
+    )
+    moved = dot(jnp.concatenate(split(wide), axis=0), lanes[...])
+    moved = moved[:96] + moved[96:]
+    for z in range(12):
+        rows, columns = (z // 4) * 32, (z % 4) * 128
+        cells[z * 32 : z * 32 + 32, :] = moved[rows : rows + 32, columns : columns + 128]
     cells[384:512, :] = jnp.zeros((128, 128), F32)
     sign = jnp.where(iota((16, 128), 1) < 64, 1.0, -1.0)
     columns = []
@@ -471,7 +500,7 @@
         a = cells[pl.ds(n, 16, stride=32), :]
         columns.append(jnp.concatenate([a, pltpu.roll(a, 64, 1) * sign], axis=0))
     stacked = jnp.concatenate(columns, axis=1)
-    result = table_dot3(tz.get(), stacked)
+    result = stacked_dot3(tz.get(), stacked)
     for g2 in range(4):
         for c2 in range(4):
             part = result[g2 * 16 : g2 * 16 + 16, c2 * 1024 : c2 * 1024 + 1024]
@@ -547,90 +576,175 @@
             out[2 * q + kx] = dot3_table(rows, tables)
 
 
-def emit_faces(state, ylo, yhi, zlo=None, zhi=None, xlo=None, xhi=None):
-    edges, sides = ([], []), [jnp.zeros((8, 384), F32)] * 2
+def emit_faces(state, slabs, faces, face):
+    face[...] = jnp.zeros((4, 64, 128), F32)
     for f in range(F):
-        slabs = [state[f, y] for y in range(4)]
-        ylo[f * 96 : f * 96 + 96, :] = slabs[0].astype(BF)
-        yhi[f * 96 : f * 96 + 96, :] = slabs[3].astype(BF)
-        edges[0].extend(s[0:1] for s in slabs)
-        edges[1].extend(s[95:96] for s in slabs)
-        cells = jnp.concatenate(slabs, axis=0).astype(BF)
+        for y in range(4):
+            slabs[y][f * 96 : f * 96 + 96, :] = state[f, y].astype(BF)
+        for y in range(4):
+            for k, z in enumerate((0, 95)):
+                face[k, f * 6 + 1 + y : f * 6 + 2 + y, :] = state[f, y, z : z + 1, :]
+            for k, z in enumerate((1, 94)):
+                face[k, 32 + f * 4 + y : 33 + f * 4 + y, :] = state[f, y, z : z + 1, :]
+    for y in range(4):
+        sides = jnp.zeros((32, 96), F32)
+        for f in range(F):
+            pick = one_hot(
+                (32, 128),
+                lambda a, b: (a % 8 == f) & (b == jnp.where(a < 8, 0, jnp.where(a < 16, 1, jnp.where(a < 24, 127, 126)))),
+            )
+            sides = sides + dot(pick.astype(BF), state[f, y].astype(BF), ((1,), (1,)))
         for k in range(2):
-            pick = one_hot((8, 128), lambda a, b: (a == f) & (b == 127 * k)).astype(BF)
-            sides[k] = sides[k] + dot(pick, cells, ((1,), (1,)))
-    pad = jnp.zeros((8, 128), F32)
-    faces = [jnp.concatenate(rows + [pad, pad[:4]], axis=0).astype(BF) for rows in edges]
-    for side in sides:
-        faces.append(jnp.concatenate([side[:, j * 128 : j * 128 + 128] for j in range(3)] + [pad], axis=0).astype(BF))
-    if zlo is not None:
-        for ref, face in zip((zlo, zhi, xlo, xhi), faces):
-            ref[...] = face
-    return faces
-
-
-Y_FACES = [shape((480, 128), BF)] * 2
-FACES = Y_FACES + [shape((32, 128), BF)] * 4
-
-
-def advance(state, below, above, before, after, left, right, put):
-    g = own_group()
-    lane = iota((96, 128), 1)
-    row = iota((96, 128), 0)
-    left, right = (
-        jnp.concatenate([x[j * 8 : j * 8 + 8] for j in range(3)], axis=1).astype(BF) for x in (left, right)
-    )
-    for f in range(F):
-        pick = lambda lane_of: one_hot((8, 128), lambda a, b: (a == f) & (b == lane_of)).astype(BF)
-        low_x = jnp.where(g == 0, 0.0, dot(left, pick(0), ((0,), (0,))))
-        high_x = jnp.where(g == 2, 0.0, dot(right, pick(127), ((0,), (0,))))
-        slabs = [below[f * 96 : f * 96 + 96, :].astype(F32)]
-        slabs += [state[f, y] for y in range(4)]
-        slabs += [above[f * 96 : f * 96 + 96, :].astype(F32)]
-        for y in range(4):
-            q = slabs[y + 1]
-            yminus, yplus = slabs[y], slabs[y + 2]
-            xminus = jnp.where(lane == 0, low_x[y * 96 : y * 96 + 96], pltpu.roll(q, 1, 1))
-            xplus = jnp.where(lane == 127, high_x[y * 96 : y * 96 + 96], pltpu.roll(q, 127, 1))
-            k = f * 4 + y
-            zminus = jnp.where(row == 0, before[k : k + 1], pltpu.roll(q, 1, 0))
-            zplus = jnp.where(row == 95, after[k : k + 1], pltpu.roll(q, 95, 0))
-            carried = (
-                state[0, y] * (xplus - xminus)
-                + state[1, y] * (yplus - yminus)
-                + state[2, y] * (zplus - zminus)
+            face[2 + k, y * 5 + 5 : y * 5 + 10, 0:96] = sides[16 * k : 16 * k + 5]
+            face[2 + k, y * 5 + 30 : y * 5 + 35, 0:96] = sides[16 * k + 8 : 16 * k + 13]
+    for k in range(4):
+        faces[k][...] = face[k].astype(BF)
+
+
+FACES = [shape((480, 128), BF)] * 4 + [shape((64, 128), BF)] * 4
+
+
+def update(q, velocity, xminus, xplus, yminus, yplus, zminus, zplus):
+    carried = (
+        velocity[0] * (xplus - xminus) + velocity[1] * (yplus - yminus) + velocity[2] * (zplus - zminus)
+    )
+    around = xplus + xminus + yplus + yminus + zplus + zminus - 6.0 * q
+    return q - ADVECT_RATE * carried + DIFFUSE_RATE * around
+
+
+def advance(get, rows, sides, ends, put):
+    lane, row = iota((96, 128), 1), iota((96, 128), 0)
+    for y in rows:
+        side_y = sides(y)
+        velocity = [get(f, y) for f in range(3)]
+        for f in range(F):
+            q, side = get(f, y), side_y[:96, f * 128 : f * 128 + 128]
+            before, after = ends(f, y)
+            value = update(
+                q,
+                velocity,
+                jnp.where(lane == 0, side, pltpu.roll(q, 1, 1)),
+                jnp.where(lane == 127, side, pltpu.roll(q, 127, 1)),
+                get(f, y - 1),
+                get(f, y + 1),
+                jnp.where(row == 0, before, pltpu.roll(q, 1, 0)),
+                jnp.where(row == 95, after, pltpu.roll(q, 95, 0)),
             )
-            around = xplus + xminus + yplus + yminus + zplus + zminus - 6.0 * q
-            put(f, y, q - ADVECT_RATE * carried + DIFFUSE_RATE * around)
-
-
-def last_step_kernel(got, below, above, pool, fields, middle, new, *refs):
-    snaps, (start, stepped, rows) = refs[:4], refs[4:]
+            put(f, y, value)
+
+
+def stand_up(left, right):
+    pad = jnp.zeros((3, 128), F32)
+    put_at = lambda a, b: ((a < 8) & (b == a * 128)) | ((a >= 8) & (b == (a - 8) * 128 + 127))
+    sides = jnp.concatenate([left, pad, right, pad], axis=0).astype(BF)
+    return dot(sides, one_hot((16, F * 128), put_at).astype(BF), ((0,), (0,)))
+
+
+def steps_kernel(xlo, xhi, pool, near, fields, below2, kept, above2, new, *refs):
+    snaps, (state, middle, stepped, around, rows) = refs[:4], refs[4:]
     g = own_group()
     outside = g == 3
-    faces = [got[source, 96:128, :].astype(F32) for source in neighbours()]
+    fields, near = fields.get(), near.get()
+    kept = kept.get()
+    slabs = ((0, below2.get()), (1, kept.at[0]), (6, kept.at[1]), (7, above2.get()))
     for f in range(F):
-        load_rows(fields, start, f)
+        for y in range(4):
+            state[f, y + 2] = fields[f, pl.ds(y, 96, stride=4), :]
+        for k, slab in slabs:
+            state[f, k] = slab[f * 96 : f * 96 + 96, :].astype(F32)
+    for k in range(8):
+        wall = {2: 0, 4: 0, 5: 0, 3: 2, 6: 2, 7: 2}.get(k)
+        value = near[k].astype(F32)
+        around[k] = value if wall is None else jnp.where(g == wall, 0.0, value)
+
+    def put_middle(f, y, value):
+        middle[f, y + 1] = value
+
+    advance(
+        lambda f, y: state[f, y + 2],
+        range(-1, 5),
+        lambda y: stand_up(*(around[k, y * 5 + 5 : y * 5 + 10, :] for k in (2, 3))),
+        lambda f, y: [around[k, f * 6 + y + 1 : f * 6 + y + 2, :] for k in (0, 1)],
+        put_middle,
+    )
+    lane = iota((8, 128), 1)
+
+    def both(k, l, first):
+        return jnp.concatenate([around[k, first : first + 4, :], around[l, first : first + 4, :]], axis=0)
+
+    ends, centers = [], [both(0, 1, f * 6 + 1) for f in range(F)]
+    for f in range(F):
+        q = centers[f]
+        own = [[state[f, y + 2, z : z + 1, :] for y in range(4)] for z in (0, 95)]
+        left, right = both(4, 5, f * 6 + 1), both(6, 7, f * 6 + 1)
+        ends.append(
+            update(
+                q,
+                centers[:3],
+                jnp.where(lane == 0, pltpu.roll(left, 1, 1), pltpu.roll(q, 1, 1)),
+                jnp.where(lane == 127, pltpu.roll(right, 127, 1), pltpu.roll(q, 127, 1)),
+                both(0, 1, f * 6),
+                both(0, 1, f * 6 + 2),
+                jnp.concatenate([around[0, 32 + f * 4 : 36 + f * 4, :]] + own[1], axis=0),
+                jnp.concatenate(own[0] + [around[1, 32 + f * 4 : 36 + f * 4, :]], axis=0),
+            )
+        )
+    lane = iota((5, 128), 1)
+    columns = []
+    for y in range(4):
+        pair = []
+        for side, own in enumerate((xlo, xhi)):
+            k = 2 + side
+            q = around[k, y * 5 + 5 : y * 5 + 10, :]
+            inner = own[...].astype(F32)[y * 5 + 5 : y * 5 + 10]
+            outer = around[k, y * 5 + 30 : y * 5 + 35, :]
+            corners = [around[4 + 2 * side + n, pl.ds(1 + y, 5, stride=6), :] for n in range(2)]
+            turns = (1, 96) if side == 0 else (0, 95)
+            first, last = (pltpu.roll(v, t, 1) if t else v for v, t in zip(corners, turns))
+            value = update(
+                q,
+                [q[n : n + 1] for n in range(3)],
+                outer if side == 0 else inner,
+                inner if side == 0 else outer,
+                around[k, y * 5 : y * 5 + 5, :],
+                around[k, y * 5 + 10 : y * 5 + 15, :],
+                jnp.where(lane == 0, first, pltpu.roll(q, 1, 1)),
+                jnp.where(lane == 95, last, pltpu.roll(q, 127, 1)),
+            )
+            pair.append(jnp.where(g == 2 * side, 0.0, value))
+        columns.append(pair)
 
     def put(f, y, value):
         stepped[f, y] = value
-        new.ref[f, pl.ds(y, 96, stride=4), :] = jnp.where(outside, start[f, y], value)
+        cells = pl.ds(y, 96, stride=4)
+        new.ref[f, cells, :] = jnp.where(outside, state[f, y + 2], value)
         if y == 3:
             new.push(f)
 
-    advance(middle.get(), below, above, *faces, put)
+    advance(
+        lambda f, y: middle[f, y + 1],
+        range(4),
+        lambda y: stand_up(*columns[y]),
+        lambda f, y: [ends[f][y + 4 * k : y + 4 * k + 1] for k in range(2)],
+        put,
+    )
     rows[...] = jnp.zeros((512, 256), F32)
     for f in range(F):
-        for base, cells in ((0, start), (64, stepped)):
+        for base in (0, 64):
             for y in range(2):
-                pooled = pair_sums(cells, f, y)
+                pooled = pair_sums(stepped, f, y) if base else fine_sums(fields, f, y)
                 for dest in range(4):
                     at = dest * 128 + base + f * 12
                     rows[at : at + 12, y * 128 : y * 128 + 128] = pooled[dest * 12 : dest * 12 + 12]
     for d in range(4):
         at = pl.multiple_of(((g + d) % 4) * 128, 128)
         high, low = split(rows[pl.ds(at, 128), :])
-        snaps[d][...] = (dot(pool[...], high, ((1,), (1,))) + dot(pool[...], low, ((1,), (1,)))).astype(BF)
+        value = (dot(pool[...], high, ((1,), (1,))) + dot(pool[...], low, ((1,), (1,)))).astype(BF)
+        if d:
+            snaps[d].ref[...] = value
+            snaps[d].push(0)
+        else:
+            snaps[d][...] = value
 
 
 def swap(x, axes):
@@ -652,53 +766,63 @@
     owner = ("grp", "col")
     state_space = pltpu.VMEM((F, 4, 96, 128), F32)
 
-    first, ylo, yhi, *faces = call(
+    first, y0, y1, y2, y3, *faces = call(
         first_kernel,
         [shape((16, 8, 256), F32)] + FACES,
         [],
         by_field + [(table_x_partial(), own_group)],
-        [state_space, pltpu.VMEM((256, 256), F32)],
+        [state_space, pltpu.VMEM((256, 256), F32), pltpu.VMEM((4, 64, 128), F32)],
     )
     got = swap(first, "row")
-    maps = call(
-        cell_maps_kernel,
-        [shape((2, 128, 384), BF)] * 2,
-        [lift_weight, mix_weight, project_weight],
-    )
+    below, above = shift(y3, "row", 1), shift(y0, "row", -1)
+    below2, above2 = shift(y2, "row", 1), shift(y1, "row", -1)
+    first = call(first_yz_kernel, shape((16, 32, 256), BF), [got, table_y_first(), table_z_first()])
+    first, kept = call(
+        add_faces_kernel,
+        [shape((16, 64, 256), BF), shape((2, 480, 128), BF)],
+        [first, below, above, *faces],
+        scratch=[pltpu.VMEM((4, 64, 128), F32)],
+        far={1: 1},
+    )
+    got = swap(first, owner)
     mixer = call(
         mixer_kernel,
         shape((2, 256, 256), F32),
         [lift_weight],
         [(spectral_weight.reshape(2, 256, 1024), None)],
     )
-    first = call(
-        first_yz_kernel, shape((16, 48, 256), BF), [got, table_y_first(), table_z_first(), *faces]
-    )
-    below, above = shift(yhi, "row", 1), shift(ylo, "row", -1)
-    first, below, above = tied(first, below, above)
-    got = swap(first, owner)
-    got, mixer = tied(got, mixer)
-    modes, spread, middle, ylo, yhi = call(
+    maps = call(
+        cell_maps_kernel,
+        [shape((2, 128, 384), BF)] * 2,
+        [lift_weight, mix_weight, project_weight],
+    )
+    got, mixer, maps = tied(got, mixer, maps)
+    modes, spread, near = call(
         mix_kernel,
-        [shape((16, 128, 128), BF), shape((2, 2, 256, 128), F32), shape((F, 4, 96, 128), F32)] + Y_FACES,
-        [got, below, above, table_select(), table_sum_fields(), mixer, flat],
+        [shape((16, 96, 128), BF), shape((2, 2, 256, 128), F32), shape((8, 64, 128), BF)],
+        [got, table_select(), table_sum_fields(), mixer],
         [(table_z_inverse(), own_group)],
-        [pltpu.VMEM((1536, 128), F32), state_space],
+        [pltpu.VMEM((1536, 128), F32)],
         far={1: 1, 2: 1},
     )
+    modes, below2, above2 = tied(modes, below2, above2)
     got = swap(modes, owner)
-    got, maps = tied(got, maps)
-    below, above = shift(yhi, "row", 1), shift(ylo, "row", -1)
+    new_fields, *snaps = call(
+        steps_kernel,
+        [shape((F, 384, 128), F32)] + [shape((128, 128), BF)] * 4,
+        [*faces[2:], table_pool_x()],
+        [(v, None) for v in (near, flat, below2, kept, above2)],
+        [
+            pltpu.VMEM((F, 8, 96, 128), F32),
+            pltpu.VMEM((F, 6, 96, 128), F32),
+            state_space,
+            pltpu.VMEM((8, 64, 128), F32),
+            pltpu.VMEM((512, 256), F32),
+        ],
+        far={0: F, 2: 1, 3: 1, 4: 1},
+    )
+    got, snaps[1:] = tied(got, snaps[1:])
     planes = call(inverse_y_kernel, shape((16, 8, 384), BF), [got, table_lanes(), table_y_inverse()])
-    planes, below, above = tied(planes, below, above)
-    new_fields, *snaps = call(
-        last_step_kernel,
-        [shape((F, 384, 128), F32)] + [shape((128, 128), BF)] * 4,
-        [got, below, above, table_pool_x(), flat],
-        [(middle, None)],
-        [state_space, state_space, pltpu.VMEM((512, 256), F32)],
-        far={0: F},
-    )
     got = swap(planes, "row")
     for d in range(1, 4):
         snaps[d] = shift(snaps[d], "grp", d)

time: 126 us -> 122 us (0.968)
  blocking collectives: 18.2 us -> 14 us
  Pallas kernels: 23.1 us -> 25.1 us
    all_to_all x1, blocking collectives: 18.2 us -> 14 us  [swap(): return lax.all_to_all(x, axes, 0, 0, tiled=True)]
    pallas_call x11 -> x12, Pallas kernels: 23.1 us -> 25.1 us  [call(): pl.pallas_call(kernel, out_shape=[pltpu.HBM(o.shape, o.dtype) if k in far...]
  transfers between devices with their start and end apart: 12 -> 12, of which waited for: 8 -> 10; matrix products, arithmetic and copies ran while one was open for 2% -> 1% of each run, Pallas kernels for 9% -> 11%
where the time goes in v3:
time: 122 us; the launch traced here: 121 us
  starting transfers between devices  54.2 us (44%)
  Pallas kernels  25.1 us (21%)
  waiting for transfers between devices  24.9 us (20%)
  blocking collectives  14 us (11%)
  local copies, waits for them, and re-layouts  1.38 us (1%)
    all_to_all x5, starting transfers between devices, swap(): return lax.all_to_all(x, axes, 0, 0, tiled=True)  39 us
    pallas_call x12, Pallas kernels, call(): pl.pallas_call(kernel, out_shape=[pltpu.HBM(o.shape, o.dtype) if k in far...  25.1 us
    all_to_all x5, waiting for transfers between devices, swap(): return lax.all_to_all(x, axes, 0, 0, tiled=True)  21.6 us
    ppermute x7, starting transfers between devices, shift(): return lax.ppermute(x, axis, [(i, (i + step) % size) for i in range(size)])  15.2 us
    all_to_all x1, blocking collectives, swap(): return lax.all_to_all(x, axes, 0, 0, tiled=True)  14 us
    ppermute x7, waiting for transfers between devices, shift(): return lax.ppermute(x, axis, [(i, (i + step) % size) for i in range(size)])  3.24 us
  transfers between devices with their start and end apart: 12, of which 10 were waited for; matrix products, arithmetic and copies ran while one was open for 1% of the time, Pallas kernels for 11%

profile of v3, /device:TPU:1, one launch (start us, length us, event | category | flops | bytes accessed | tf_op | source)
XLA Modules:
  0.0 120.7 jit_solution(4432227683429413229)
XLA Ops:
  0.7 2.5 %shard_map.194 = (f32[16,8,256]{2,1,0:T(8,128)}, bf16[480,128]{1,0:T(8,128)(2,1)S(1)}, bf16[480,128]{1,0:T(8,128)(2,1)S(1)}, bf16[480,128]{1,0:T(8,128)(2,1)S(1)...) custom-call(f32[5,384,128]{2,1,0:T(8,128)} %bitcast.7, ...), custom_call_target="tpu_custom_call" | custom-call | tf_op jit(solution)/shard_map/pallas_call | solution.py:275
  3.2 11.9 %all-to-all-start = ((f32[16,8,256]{2,1,0:T(8,128)}), f32[16,8,256]{2,1,0:T(8,128)S(1)}, u32[]{:S(2)}, u32[]{:S(2)}) async-start(f32[16,8,256]{2,1,0:T(8,128)} %get-tuple-element.36), calls=%async_computation | async-start | bytes 262144 | tf_op jit(solution)/shard_map/all_to_all | solution.py:751
  15.1 2.3 %collective-permute-start = (bf16[480,128]{1,0:T(8,128)(2,1)S(1)}, bf16[480,128]{1,0:T(8,128)(2,1)S(1)}, u32[]{:S(2)}, u32[]{:S(2)}) collective-permute-start(bf16[480,128]{1,0:T(8,128)(2,1)S(1)} %get-tuple-element.37), channel_id=1, source_target_pairs={{0,4},{4,8},{8,12},{12,16},{16,20},{20,24},{24,28},{28,32},{32,36}... | collective-permute-start | bytes 368648 | tf_op jit(solution)/shard_map/ppermute | solution.py:756
  17.3 3.5 %collective-permute-start.1 = (bf16[480,128]{1,0:T(8,128)(2,1)S(1)}, bf16[480,128]{1,0:T(8,128)(2,1)S(1)}, u32[]{:S(2)}, u32[]{:S(2)}) collective-permute-start(bf16[480,128]{1,0:T(8,128)(2,1)S(1)} %get-tuple-element.38), channel_id=1, source_target_pairs={{0,60},{4,0},{8,4},{12,8},{16,12},{20,16},{24,20},{28,24},{32,28},... | collective-permute-start | bytes 368648 | tf_op jit(solution)/shard_map/ppermute | solution.py:756
  20.8 3.9 %all-to-all-done.refs_0_ = f32[16,8,256]{2,1,0:T(8,128)S(1)} async-done(((f32[16,8,256]{2,1,0:T(8,128)}), f32[16,8,256]{2,1,0:T(8,128)S(1)}, u32[]{:S(2)}, u32[]{:S(2)}) %all-to-all-start) | async-done | bytes 131104 | tf_op jit(solution)/shard_map/all_to_all | solution.py:751
  28.2 8.7 %all-to-all-start.1 = ((bf16[16,64,256]{2,1,0:T(8,128)(2,1)}), bf16[16,64,256]{2,1,0:T(8,128)(2,1)S(1)}, u32[]{:S(2)}, u32[]{:S(2)}) async-start(bf16[16,64,256]{2,1,0:T(8,128)(2,1)} %get-tuple-element.41), calls=%async_computation.1 | async-start | bytes 1048576 | tf_op jit(solution)/shard_map/all_to_all | solution.py:751
  38.0 4.8 %collective-permute-start.3 = (bf16[480,128]{1,0:T(8,128)(2,1)S(1)}, bf16[480,128]{1,0:T(8,128)(2,1)}, u32[]{:S(2)}, u32[]{:S(2)}) collective-permute-start(bf16[480,128]{1,0:T(8,128)(2,1)S(1)} %get-tuple-element.49), channel_id=1, source_target_pairs={{0,60},{4,0},{8,4},{12,8},{16,12},{20,16},{24,20},{28,24},{32,28},... | collective-permute-start | bytes 368648 | tf_op jit(solution)/shard_map/ppermute | solution.py:756
  44.1 2.0 %shard_map.197.refs_3_ = f32[2,256,256]{2,1,0:T(8,128)S(1)} custom-call(f32[32,5]{1,0:T(8,128)S(1)} %copy.21.refs_0_, bf16[2,256,1024]{2,1,0:T(8,128)(2,1)} %reshape.20.refs_1_), custom_call_target="tpu_custom_call" | custom-call | tf_op jit(solution)/shard_map/pallas_call | solution.py:275
  47.0 2.7 %all-to-all-done.1.refs_0_ = bf16[16,64,256]{2,1,0:T(8,128)(2,1)S(1)} async-done(((bf16[16,64,256]{2,1,0:T(8,128)(2,1)}), bf16[16,64,256]{2,1,0:T(8,128)(2,1)S(1)}, u32[]{:S(2)}, u32[]{:S(2)}) %all-to-all-start.1) | async-done | bytes 524320 | tf_op jit(solution)/shard_map/all_to_all | solution.py:751
  49.7 2.6 %shard_map.199 = (bf16[16,96,128]{2,1,0:T(8,128)(2,1)}, f32[2,2,256,128]{3,2,1,0:T(8,128)}, bf16[8,64,128]{2,1,0:T(8,128)(2,1)}) custom-call(bf16[16,64,256]{2,1,0:T(8,128)(2,1)S(1)} %all-to-all-done.1.refs_0_, bf16[128,256]{1,0:T(8,128)(2,1)S(1)} %copy-done.7, bf16[512,128]{1,0:T(8,128)(2,1)S(1)} %copy-done.4, f32[2,256,256]{2,1,0:T(8,128)S(1)} %shard_map.197.refs_3_, ...), custom_call_target="tpu_custom_call" | custom-call | tf_op jit(solution)/shard_map/pallas_call | solution.py:275
  52.4 4.8 %all-to-all-start.2 = ((bf16[16,96,128]{2,1,0:T(8,128)(2,1)}), bf16[16,96,128]{2,1,0:T(8,128)(2,1)S(1)}, u32[]{:S(2)}, u32[]{:S(2)}) async-start(bf16[16,96,128]{2,1,0:T(8,128)(2,1)} %get-tuple-element.54), calls=%async_computation.2 | async-start | bytes 786432 | tf_op jit(solution)/shard_map/all_to_all | solution.py:751
  57.2 5.8 %shard_map.200 = (f32[5,384,128]{2,1,0:T(8,128)}, bf16[128,128]{1,0:T(8,128)(2,1)S(1)}, bf16[128,128]{1,0:T(8,128)(2,1)}, bf16[128,128]{1,0:T(8,128)(2,1)}, bf16[128,128]{1,0:T(8,128)(2,1)}) custom-call(bf16[64,128]{1,0:T(8,128)(2,1)S(1)} %get-tuple-element.34.refs_5_.refs_0_, bf16[64,128]{1,0:T(8,128)(2,1)S(1)} %get-tuple-element.35.refs_6_.refs_1_, ...), custom_call_target="tpu_custom_call" | custom-call | tf_op jit(solution)/shard_map/pallas_call | solution.py:275
  63.1 2.6 %all-to-all-done.2.refs_0_ = bf16[16,96,128]{2,1,0:T(8,128)(2,1)S(1)} async-done(((bf16[16,96,128]{2,1,0:T(8,128)(2,1)}), bf16[16,96,128]{2,1,0:T(8,128)(2,1)S(1)}, u32[]{:S(2)}, u32[]{:S(2)}) %all-to-all-start.2) | async-done | bytes 393248 | tf_op jit(solution)/shard_map/all_to_all | solution.py:751
  66.9 5.0 %all-to-all-start.3 = ((bf16[16,8,384]{2,1,0:T(8,128)(2,1)}), bf16[16,8,384]{2,1,0:T(8,128)(2,1)S(1)}, u32[]{:S(2)}, u32[]{:S(2)}) async-start(bf16[16,8,384]{2,1,0:T(8,128)(2,1)} %shard_map.201), calls=%async_computation.3 | async-start | bytes 196608 | tf_op jit(solution)/shard_map/all_to_all | solution.py:751
  72.2 1.7 %collective-permute-start.5 = (bf16[128,128]{1,0:T(8,128)(2,1)}, bf16[128,128]{1,0:T(8,128)(2,1)S(1)}, u32[]{:S(2)}, u32[]{:S(2)}) collective-permute-start(bf16[128,128]{1,0:T(8,128)(2,1)} %get-tuple-element.61), channel_id=1, source_target_pairs={{0,128},{64,192},{128,0},{192,64},{1,129},{65,193},{129,1},{193,65... | collective-permute-start | bytes 98312 | tf_op jit(solution)/shard_map/ppermute | solution.py:756
  73.9 1.7 %collective-permute-start.6 = (bf16[128,128]{1,0:T(8,128)(2,1)}, bf16[128,128]{1,0:T(8,128)(2,1)S(1)}, u32[]{:S(2)}, u32[]{:S(2)}) collective-permute-start(bf16[128,128]{1,0:T(8,128)(2,1)} %get-tuple-element.62), channel_id=1, source_target_pairs={{0,192},{64,0},{128,64},{192,128},{1,193},{65,1},{129,65},{193,129... | collective-permute-start | bytes 98312 | tf_op jit(solution)/shard_map/ppermute | solution.py:756
  77.6 3.9 %all-to-all-done.3.refs_0_ = bf16[16,8,384]{2,1,0:T(8,128)(2,1)S(1)} async-done(((bf16[16,8,384]{2,1,0:T(8,128)(2,1)}), bf16[16,8,384]{2,1,0:T(8,128)(2,1)S(1)}, u32[]{:S(2)}, u32[]{:S(2)}) %all-to-all-start.3) | async-done | bytes 98336 | tf_op jit(solution)/shard_map/all_to_all | solution.py:751
  81.4 2.0 %shard_map.202 = bf16[16,8,384]{2,1,0:T(8,128)(2,1)S(1)} custom-call(bf16[16,8,384]{2,1,0:T(8,128)(2,1)S(1)} %all-to-all-done.3.refs_0_, bf16[128,128]{1,0:T(8,128)(2,1)S(1)} %get-tuple-element.59.refs_1_, bf16[128,128]{1,0:T(8,128)(2,1)S(1)} %collective-permute-done.4.refs_2_, bf16[128,128]{1,0:T(8,128)(2,1)S(1)} %collective-permute-done.5.refs_3_, ...), custom_call_target="tpu_custom_call" | custom-call | tf_op jit(solution)/shard_map/pallas_call | solution.py:275
  83.4 14.0 %all_to_all.30.refs_0_ = bf16[16,8,384]{2,1,0:T(8,128)(2,1)S(1)} all-to-all(bf16[16,8,384]{2,1,0:T(8,128)(2,1)S(1)} %shard_map.202), channel_id=1, replica_groups=mesh['grp'=4,'row'=16,'col'=4] {'row'}, dimensions={0} | all-to-all | bytes 196608 | tf_op jit(solution)/shard_map/all_to_all | solution.py:751
  97.4 2.0 %shard_map.203 = bf16[16,16,1152]{2,1,0:T(8,128)(2,1)} custom-call(bf16[16,8,384]{2,1,0:T(8,128)(2,1)S(1)} %all_to_all.30.refs_0_, bf16[2,128,128]{2,1,0:T(8,128)(2,1)S(1)} %copy-done.6, bf16[512,512]{1,0:T(8,128)(2,1)S(1)} %copy-done, bf16[16,2,64,32]{3,2,1,0:T(8,128)(2,1)} %constant.36.clone.refs_3_), custom_call_target="tpu_custom_call" | custom-call | tf_op jit(solution)/shard_map/pallas_call | solution.py:275
  99.5 8.6 %all-to-all-start.5 = ((bf16[16,16,1152]{2,1,0:T(8,128)(2,1)}), bf16[16,16,1152]{2,1,0:T(8,128)(2,1)S(1)}, u32[]{:S(2)}, u32[]{:S(2)}) async-start(bf16[16,16,1152]{2,1,0:T(8,128)(2,1)} %shard_map.203), calls=%async_computation.5 | async-start | bytes 1179648 | tf_op jit(solution)/shard_map/all_to_all | solution.py:751
  108.1 2.0 %shard_map.204.refs_2_ = f32[4,128,1024]{2,1,0:T(8,128)S(1)} custom-call(f32[32,5]{1,0:T(8,128)S(1)} %copy.21.refs_0_, f32[2,2,256,128]{3,2,1,0:T(8,128)} %get-tuple-element.65.refs_1_), custom_call_target="tpu_custom_call" | custom-call | tf_op jit(solution)/shard_map/pallas_call | solution.py:275
  110.2 8.5 %all-to-all-done.5.refs_0_ = bf16[16,16,1152]{2,1,0:T(8,128)(2,1)S(1)} async-done(((bf16[16,16,1152]{2,1,0:T(8,128)(2,1)}), bf16[16,16,1152]{2,1,0:T(8,128)(2,1)S(1)}, u32[]{:S(2)}, u32[]{:S(2)}) %all-to-all-start.5) | async-done | bytes 589856 | tf_op jit(solution)/shard_map/all_to_all | solution.py:751
  118.6 1.9 %shard_map.205 = bf16[2,128,16,128]{3,2,1,0:T(8,128)(2,1)} custom-call(bf16[16,16,1152]{2,1,0:T(8,128)(2,1)S(1)} %all-to-all-done.5.refs_0_, bf16[256,256]{1,0:T(8,128)(2,1)S(1)} %copy-done.5, f32[4,128,1024]{2,1,0:T(8,128)S(1)} %shard_map.204.refs_2_), custom_call_target="tpu_custom_call" | custom-call | tf_op jit(solution)/shard_map/pallas_call | solution.py:275
  (45 shorter events, 10.1 us)
Async XLA Ops:
  0.6 24.1 %copy-start.1 = (bf16[2,2,256,512]{3,2,1,0:T(8,128)(2,1)S(1)}, bf16[2,2,256,512]{3,2,1,0:T(8,128)(2,1)}, u32[]{:S(2)}) copy-start(bf16[2,2,256,512]{3,2,1,0:T(8,128)(2,1)} %constant.28.clone.refs_2_) | copy-start | bytes 3145732
  0.6 24.1 %copy-start.8 = (bf16[2,128,128]{2,1,0:T(8,128)(2,1)S(1)}, bf16[2,128,128]{2,1,0:T(8,128)(2,1)}, u32[]{:S(2)}) copy-start(bf16[2,128,128]{2,1,0:T(8,128)(2,1)} %constant.27.clone.refs_1_) | copy-start | bytes 196612
  3.1 39.7 %copy-start.14 = (f32[32,5]{0,1:T(8,128)S(1)}, f32[32,5]{0,1:T(8,128)}, u32[]{:S(2)}) copy-start(f32[32,5]{0,1:T(8,128)} %param.20) | copy-start | bytes 1924
  3.2 39.7 %copy-start.12 = (bf16[2,16,8,2,1024]{4,3,2,1,0:T(2,128)(2,1)S(1)}, bf16[2,16,8,2,1024]{4,3,2,1,0:T(2,128)(2,1)}, u32[]{:S(2)}) copy-start(bf16[2,16,8,2,1024]{4,3,2,1,0:T(2,128)(2,1)} %param.23) | copy-start | bytes 3145732
  3.2 21.6 %all-to-all-start = ((f32[16,8,256]{2,1,0:T(8,128)}), f32[16,8,256]{2,1,0:T(8,128)S(1)}, u32[]{:S(2)}, u32[]{:S(2)}) async-start(f32[16,8,256]{2,1,0:T(8,128)} %get-tuple-element.36), calls=%async_computation | async-start | bytes 262144 | tf_op jit(solution)/shard_map/all_to_all | solution.py:751
  15.1 10.9 %collective-permute-start = (bf16[480,128]{1,0:T(8,128)(2,1)S(1)}, bf16[480,128]{1,0:T(8,128)(2,1)S(1)}, u32[]{:S(2)}, u32[]{:S(2)}) collective-permute-start(bf16[480,128]{1,0:T(8,128)(2,1)S(1)} %get-tuple-element.37), channel_id=1, source_target_pairs={{0,4},{4,8},{8,12},{12,16},{16,20},{20,24},{24,28},{28,32},{32,36}... | collective-permute-start | bytes 368648 | tf_op jit(solution)/shard_map/ppermute | solution.py:756
  17.3 9.3 %collective-permute-start.1 = (bf16[480,128]{1,0:T(8,128)(2,1)S(1)}, bf16[480,128]{1,0:T(8,128)(2,1)S(1)}, u32[]{:S(2)}, u32[]{:S(2)}) collective-permute-start(bf16[480,128]{1,0:T(8,128)(2,1)S(1)} %get-tuple-element.38), channel_id=1, source_target_pairs={{0,60},{4,0},{8,4},{12,8},{16,12},{20,16},{24,20},{28,24},{32,28},... | collective-permute-start | bytes 368648 | tf_op jit(solution)/shard_map/ppermute | solution.py:756
  28.2 21.5 %all-to-all-start.1 = ((bf16[16,64,256]{2,1,0:T(8,128)(2,1)}), bf16[16,64,256]{2,1,0:T(8,128)(2,1)S(1)}, u32[]{:S(2)}, u32[]{:S(2)}) async-start(bf16[16,64,256]{2,1,0:T(8,128)(2,1)} %get-tuple-element.41), calls=%async_computation.1 | async-start | bytes 1048576 | tf_op jit(solution)/shard_map/all_to_all | solution.py:751
  37.0 12.7 %copy-start.4 = (bf16[512,128]{1,0:T(8,128)(2,1)S(1)}, bf16[512,128]{1,0:T(8,128)(2,1)}, u32[]{:S(2)}) copy-start(bf16[512,128]{1,0:T(8,128)(2,1)} %constant.31.clone.refs_2_) | copy-start | bytes 393220
  37.0 12.7 %copy-start.7 = (bf16[128,256]{1,0:T(8,128)(2,1)S(1)}, bf16[128,256]{1,0:T(8,128)(2,1)}, u32[]{:S(2)}) copy-start(bf16[128,256]{1,0:T(8,128)(2,1)} %constant.30.clone.refs_1_) | copy-start | bytes 196612
  37.0 15.3 %collective-permute-start.2 = (bf16[480,128]{1,0:T(8,128)(2,1)S(1)}, bf16[480,128]{1,0:T(8,128)(2,1)S(1)}, u32[]{:S(2)}, u32[]{:S(2)}) collective-permute-start(bf16[480,128]{1,0:T(8,128)(2,1)S(1)} %get-tuple-element.48), channel_id=1, source_target_pairs={{0,4},{4,8},{8,12},{12,16},{16,20},{20,24},{24,28},{28,32},{32,36}... | collective-permute-start | bytes 368648 | tf_op jit(solution)/shard_map/ppermute | solution.py:756
  38.0 14.4 %collective-permute-start.3 = (bf16[480,128]{1,0:T(8,128)(2,1)S(1)}, bf16[480,128]{1,0:T(8,128)(2,1)}, u32[]{:S(2)}, u32[]{:S(2)}) collective-permute-start(bf16[480,128]{1,0:T(8,128)(2,1)S(1)} %get-tuple-element.49), channel_id=1, source_target_pairs={{0,60},{4,0},{8,4},{12,8},{16,12},{20,16},{24,20},{28,24},{32,28},... | collective-permute-start | bytes 368648 | tf_op jit(solution)/shard_map/ppermute | solution.py:756
  44.1 13.1 %copy-start.9 = (bf16[128,256]{1,0:T(8,128)(2,1)S(1)}, bf16[128,256]{1,0:T(8,128)(2,1)}, u32[]{:S(2)}) copy-start(bf16[128,256]{1,0:T(8,128)(2,1)} %constant.32.clone.refs_2_) | copy-start | bytes 196612
  46.1 19.5 %copy-start = (bf16[512,512]{1,0:T(8,128)(2,1)S(1)}, bf16[512,512]{1,0:T(8,128)(2,1)}, u32[]{:S(2)}) copy-start(bf16[512,512]{1,0:T(8,128)(2,1)} %constant.33.clone.refs_1_.refs_2_) | copy-start | bytes 1572868
  46.2 19.5 %copy-start.2 = (bf16[2,128,512]{2,1,0:T(8,128)(2,1)S(1)}, bf16[2,128,512]{2,1,0:T(8,128)(2,1)}, u32[]{:S(2)}) copy-start(bf16[2,128,512]{2,1,0:T(8,128)(2,1)} %constant.34.clone.refs_2_) | copy-start | bytes 786436
  52.3 29.1 %copy-start.3 = (bf16[2,384,128]{2,1,0:T(8,128)(2,1)S(1)}, bf16[2,384,128]{2,1,0:T(8,128)(2,1)}, u32[]{:S(2)}) copy-start(bf16[2,384,128]{2,1,0:T(8,128)(2,1)} %constant.35.clone.refs_5_) | copy-start | bytes 589828
  52.4 13.3 %all-to-all-start.2 = ((bf16[16,96,128]{2,1,0:T(8,128)(2,1)}), bf16[16,96,128]{2,1,0:T(8,128)(2,1)S(1)}, u32[]{:S(2)}, u32[]{:S(2)}) async-start(bf16[16,96,128]{2,1,0:T(8,128)(2,1)} %get-tuple-element.54), calls=%async_computation.2 | async-start | bytes 786432 | tf_op jit(solution)/shard_map/all_to_all | solution.py:751
  57.2 40.2 %copy-start.6 = (bf16[2,128,128]{2,1,0:T(8,128)(2,1)S(1)}, bf16[2,128,128]{2,1,0:T(8,128)(2,1)}, u32[]{:S(2)}) copy-start(bf16[2,128,128]{2,1,0:T(8,128)(2,1)} %constant.37.clone.refs_1_) | copy-start | bytes 196612
  66.9 14.5 %all-to-all-start.3 = ((bf16[16,8,384]{2,1,0:T(8,128)(2,1)}), bf16[16,8,384]{2,1,0:T(8,128)(2,1)S(1)}, u32[]{:S(2)}, u32[]{:S(2)}) async-start(bf16[16,8,384]{2,1,0:T(8,128)(2,1)} %shard_map.201), calls=%async_computation.3 | async-start | bytes 196608 | tf_op jit(solution)/shard_map/all_to_all | solution.py:751
  71.9 4.4 %collective-permute-start.4 = (bf16[128,128]{1,0:T(8,128)(2,1)}, bf16[128,128]{1,0:T(8,128)(2,1)S(1)}, u32[]{:S(2)}, u32[]{:S(2)}) collective-permute-start(bf16[128,128]{1,0:T(8,128)(2,1)} %get-tuple-element.60), channel_id=1, source_target_pairs={{0,64},{64,128},{128,192},{192,0},{1,65},{65,129},{129,193},{193,1... | collective-permute-start | bytes 98312 | tf_op jit(solution)/shard_map/ppermute | solution.py:756
  72.2 4.6 %collective-permute-start.5 = (bf16[128,128]{1,0:T(8,128)(2,1)}, bf16[128,128]{1,0:T(8,128)(2,1)S(1)}, u32[]{:S(2)}, u32[]{:S(2)}) collective-permute-start(bf16[128,128]{1,0:T(8,128)(2,1)} %get-tuple-element.61), channel_id=1, source_target_pairs={{0,128},{64,192},{128,0},{192,64},{1,129},{65,193},{129,1},{193,65... | collective-permute-start | bytes 98312 | tf_op jit(solution)/shard_map/ppermute | solution.py:756
  73.9 3.7 %collective-permute-start.6 = (bf16[128,128]{1,0:T(8,128)(2,1)}, bf16[128,128]{1,0:T(8,128)(2,1)S(1)}, u32[]{:S(2)}, u32[]{:S(2)}) collective-permute-start(bf16[128,128]{1,0:T(8,128)(2,1)} %get-tuple-element.62), channel_id=1, source_target_pairs={{0,192},{64,0},{128,64},{192,128},{1,193},{65,1},{129,65},{193,129... | collective-permute-start | bytes 98312 | tf_op jit(solution)/shard_map/ppermute | solution.py:756
  99.5 19.2 %copy-start.5 = (bf16[256,256]{1,0:T(8,128)(2,1)S(1)}, bf16[256,256]{1,0:T(8,128)(2,1)}, u32[]{:S(2)}) copy-start(bf16[256,256]{1,0:T(8,128)(2,1)} %constant.38.clone.refs_1_) | copy-start | bytes 393220
  99.5 19.2 %all-to-all-start.5 = ((bf16[16,16,1152]{2,1,0:T(8,128)(2,1)}), bf16[16,16,1152]{2,1,0:T(8,128)(2,1)S(1)}, u32[]{:S(2)}, u32[]{:S(2)}) async-start(bf16[16,16,1152]{2,1,0:T(8,128)(2,1)} %shard_map.203), calls=%async_computation.5 | async-start | bytes 1179648 | tf_op jit(solution)/shard_map/all_to_all | solution.py:751
  (3 other events, 23.2 us)

commit v4 on v3

--- a/solution.py
+++ b/solution.py
@@ -302,7 +302,7 @@
         for y in range(2):
             rows[f * 48 : f * 48 + 48, y * 128 : y * 128 + 128] = pair_sums(state, f, y)
     result = table_dot3(table.get(), rows[...], ((1,), (1,)))
-    out[...] = result.reshape(16, 8, 256)
+    out[...] = result.reshape(16, 8, 256).astype(BF)
     emit_faces(state, slabs, faces, face)
 
 
@@ -327,8 +327,8 @@
     return [((g + a) % 4) * 4 + (c + b) % 4 for a, b in steps]
 
 
-def first_yz_kernel(got, ty, tz, out):
-    both = table_dot3(ty, got[...].reshape(128, 256))
+def first_yz_kernel(got, ty, tz, out, lows):
+    both = table_dot(ty, got[...].astype(F32).reshape(128, 256).astype(BF))
     high, low = split(both)
     parts = []
     for k in range(2):
@@ -336,21 +336,23 @@
     re = parts[0][:64] + parts[1][64:]
     im = parts[0][64:] - parts[1][:64]
     for k, part in enumerate((re, im)):
-        lanes = slice(k * 128, k * 128 + 128)
         high, low = split(part)
         for g in range(4):
             for c in range(4):
                 rows, cols = slice(c * 16, c * 16 + 16), slice(g * 128, g * 128 + 128)
-                out[g * 4 + c, 0:16, lanes] = high[rows, cols]
-                out[g * 4 + c, 16:32, lanes] = low[rows, cols]
-
-
-def add_faces_kernel(modes, below, above, zlo, zhi, xlo, xhi, out, kept, face):
+                out[g * 4 + c, :, k * 128 : k * 128 + 128] = high[rows, cols]
+                lows[g * 4 + c, 2 * k : 2 * k + 2, :] = low[c * 16 : c * 16 + 2, cols].astype(F32)
+    lows[:, 4:8, :] = jnp.zeros((16, 4, 128), F32)
+
+
+def add_faces_kernel(modes, lows, below, above, zlo, zhi, xlo, xhi, out, kept, face):
     kept.ref[0] = below[...]
     kept.ref[1] = above[...]
     kept.push(0)
-    out[:, 0:32, :] = modes[...]
-    out[:, 32:64, :] = jnp.zeros((16, 32, 256), BF)
+    out[:, 0:16, :] = modes[...]
+    out[:, 16:48, 0:128] = jnp.zeros((16, 32, 128), BF)
+    for dest in range(16):
+        out[dest, 16:48, 128:256] = with_lows(jnp.zeros((32, 128), F32), lows[dest])
     for k, ref in enumerate((zlo, zhi, xlo, xhi)):
         face[k] = ref[...].astype(F32)
     sides = [jnp.zeros((16, 96), F32)] * 2
@@ -366,19 +368,22 @@
         face[2, 25 * k : 25 * k + 5, 0:96] = side[0:5]
         face[3, 25 * k : 25 * k + 5, 0:96] = side[8:13]
     before, after, left, right, *corners = neighbours()
-    zlo_v, zhi_v, xlo_v, xhi_v = (face[k].astype(BF) for k in range(4))
-    for dest, value in (
-        (before, zlo_v),
-        (after, zhi_v),
-        (left, xlo_v),
-        (right, xhi_v),
-        (corners[0], zlo_v),
-        (corners[1], zhi_v),
-        (corners[2], zlo_v),
-        (corners[3], zhi_v),
+    for dest, k in (
+        (before, 0),
+        (after, 1),
+        (left, 2),
+        (right, 3),
+        (corners[0], 0),
+        (corners[1], 1),
+        (corners[2], 0),
+        (corners[3], 1),
     ):
-        out[dest, 32:64, 0:128] = value[0:32]
-        out[dest, 32:64, 128:256] = value[32:64]
+        out[dest, 16:48, 0:128] = face[k, 0:32].astype(BF)
+        out[dest, 16:48, 128:256] = with_lows(face[k, 32:64], lows[dest])
+
+
+def with_lows(face, lows):
+    return jnp.concatenate([face[:24], lows], axis=0).astype(BF)
 
 
 def dot3_table(x, table):
@@ -390,10 +395,12 @@
     kz = iota((16, 128), 1) % 16
     re_sum, im_sum = 0.0, 0.0
     for c in range(4):
-        total = 0.0
+        total, lows = 0.0, 0.0
         for src in range(4):
-            block = got[src * 4 + c, 0:32, :].astype(F32)
-            total = total + (block[:16] + block[16:])
+            total = total + got[src * 4 + c, 0:16, :].astype(F32)
+            lows = lows + got[src * 4 + c, 16:48, 128:256].astype(F32)[24:28]
+        lows = jnp.concatenate([lows[0:2], lows[2:4]], axis=1)
+        total = total + jnp.concatenate([lows, jnp.zeros((14, 256), F32)], axis=0)
         re, im = total[:, :128], total[:, 128:]
         turn = (kz * c) % 4
         re_sum += jnp.where(turn == 0, re, jnp.where(turn == 1, im, jnp.where(turn == 2, -re, -im)))
@@ -410,7 +417,7 @@
             spread_out.ref[q, half] = spread[q * 256 : q * 256 + 256, half * 128 : half * 128 + 128]
     spread_out.push(0)
     for k, source in enumerate(neighbours()):
-        block = got[source, 32:64, :]
+        block = got[source, 16:48, :]
         near.ref[k, 0:32, :] = block[:, :128]
         near.ref[k, 32:64, :] = block[:, 128:]
     near.push(0)
@@ -499,14 +506,14 @@
     for n in range(32):
         a = cells[pl.ds(n, 16, stride=32), :]
         columns.append(jnp.concatenate([a, pltpu.roll(a, 64, 1) * sign], axis=0))
-    stacked = jnp.concatenate(columns, axis=1)
-    result = stacked_dot3(tz.get(), stacked)
-    for g2 in range(4):
-        for c2 in range(4):
-            part = result[g2 * 16 : g2 * 16 + 16, c2 * 1024 : c2 * 1024 + 1024]
+    for c2 in range(4):
+        result = stacked_dot3(tz.get(), jnp.concatenate(columns[c2 * 8 : c2 * 8 + 8], axis=1))
+        for g2 in range(4):
+            part = result[g2 * 16 : g2 * 16 + 16]
             high = part.astype(BF)
-            out[g2 * 4 + c2, :, 0:1024] = high
-            out[g2 * 4 + c2, :, 1024:1152] = (part[:, :128] - high[:, :128].astype(F32)).astype(BF)
+            out.ref[g2 * 4 + c2, :, 0:1024] = high
+            out.ref[g2 * 4 + c2, :, 1024:1152] = (part[:, :128] - high[:, :128].astype(F32)).astype(BF)
+            out.push(g2 * 4 + c2)
 
 
 def grad_kernel(got, expand, spectrum, out, cells, wide):
@@ -768,7 +775,7 @@
 
     first, y0, y1, y2, y3, *faces = call(
         first_kernel,
-        [shape((16, 8, 256), F32)] + FACES,
+        [shape((16, 8, 256), BF)] + FACES,
         [],
         by_field + [(table_x_partial(), own_group)],
         [state_space, pltpu.VMEM((256, 256), F32), pltpu.VMEM((4, 64, 128), F32)],
@@ -776,27 +783,32 @@
     got = swap(first, "row")
     below, above = shift(y3, "row", 1), shift(y0, "row", -1)
     below2, above2 = shift(y2, "row", 1), shift(y1, "row", -1)
-    first = call(first_yz_kernel, shape((16, 32, 256), BF), [got, table_y_first(), table_z_first()])
-    first, kept = call(
-        add_faces_kernel,
-        [shape((16, 64, 256), BF), shape((2, 480, 128), BF)],
-        [first, below, above, *faces],
-        scratch=[pltpu.VMEM((4, 64, 128), F32)],
-        far={1: 1},
-    )
-    got = swap(first, owner)
+    first, lows = call(
+        first_yz_kernel,
+        [shape((16, 16, 256), BF), shape((16, 8, 128), F32)],
+        [got, table_y_first(), table_z_first()],
+    )
     mixer = call(
         mixer_kernel,
         shape((2, 256, 256), F32),
         [lift_weight],
         [(spectral_weight.reshape(2, 256, 1024), None)],
     )
+    first, mixer = tied(first, mixer)
+    first, kept = call(
+        add_faces_kernel,
+        [shape((16, 48, 256), BF), shape((2, 480, 128), BF)],
+        [first, lows, below, above, *faces],
+        scratch=[pltpu.VMEM((4, 64, 128), F32)],
+        far={1: 1},
+    )
+    got = swap(first, owner)
     maps = call(
         cell_maps_kernel,
         [shape((2, 128, 384), BF)] * 2,
         [lift_weight, mix_weight, project_weight],
     )
-    got, mixer, maps = tied(got, mixer, maps)
+    got, maps = tied(got, maps)
     modes, spread, near = call(
         mix_kernel,
         [shape((16, 96, 128), BF), shape((2, 2, 256, 128), F32), shape((8, 64, 128), BF)],
@@ -839,6 +851,7 @@
         [got, table_y_back(), np.ascontiguousarray(table_lanes().T)],
         [(table_z_back(), lambda: lax.axis_index("col") * 4 + own_group())],
         [pltpu.VMEM((512, 128), F32)],
+        far={0: 16},
     )
     got = swap(back, owner)
     spectrum = call(

time: 122 us -> 119 us (0.975)
  starting transfers between devices: 54.2 us -> 52.6 us
  waiting for transfers between devices: 24.9 us -> 23.4 us
    all_to_all x5, waiting for transfers between devices: 21.6 us -> 19.3 us  [swap(): return lax.all_to_all(x, axes, 0, 0, tiled=True)]
    all_to_all x5, starting transfers between devices: 39 us -> 37.4 us  [swap(): return lax.all_to_all(x, axes, 0, 0, tiled=True)]
  transfers between devices with their start and end apart: 12 -> 12, of which waited for: 10 -> 9; matrix products, arithmetic and copies ran while one was open for 1% -> 2% of each run, Pallas kernels for 11% -> 12%
where the time goes in v4:
time: 119 us; the launch traced here: 118 us
  starting transfers between devices  52.6 us (44%)
  Pallas kernels  24.9 us (21%)
  waiting for transfers between devices  23.4 us (20%)
  blocking collectives  14 us (12%)
  local copies, waits for them, and re-layouts  2.41 us (2%)
    all_to_all x5, starting transfers between devices, swap(): return lax.all_to_all(x, axes, 0, 0, tiled=True)  37.4 us
    pallas_call x12, Pallas kernels, call(): pl.pallas_call(kernel, out_shape=[pltpu.HBM(o.shape, o.dtype) if k in far...  24.9 us
    all_to_all x5, waiting for transfers between devices, swap(): return lax.all_to_all(x, axes, 0, 0, tiled=True)  19.3 us
    ppermute x7, starting transfers between devices, shift(): return lax.ppermute(x, axis, [(i, (i + step) % size) for i in range(size)])  15.2 us
    all_to_all x1, blocking collectives, swap(): return lax.all_to_all(x, axes, 0, 0, tiled=True)  14 us
    ppermute x7, waiting for transfers between devices, shift(): return lax.ppermute(x, axis, [(i, (i + step) % size) for i in range(size)])  4.15 us
  transfers between devices with their start and end apart: 12, of which 9 were waited for; matrix products, arithmetic and copies ran while one was open for 2% of the time, Pallas kernels for 12%

profile of v4, /device:TPU:1, one launch (start us, length us, event | category | flops | bytes accessed | tf_op | source)
XLA Modules:
  0.0 118.5 jit_solution(12545310874236878451)
XLA Ops:
  0.6 2.4 %shard_map.194 = (bf16[16,8,256]{2,1,0:T(8,128)(2,1)}, bf16[480,128]{1,0:T(8,128)(2,1)S(1)}, bf16[480,128]{1,0:T(8,128)(2,1)S(1)}, bf16[480,128]{1,0:T(8,128)(2,...) custom-call(f32[5,384,128]{2,1,0:T(8,128)} %bitcast.7, ...), custom_call_target="tpu_custom_call" | custom-call | tf_op jit(solution)/shard_map/pallas_call | solution.py:275
  3.1 11.9 %all-to-all-start = ((bf16[16,8,256]{2,1,0:T(8,128)(2,1)}), bf16[16,8,256]{2,1,0:T(8,128)(2,1)S(1)}, u32[]{:S(2)}, u32[]{:S(2)}) async-start(bf16[16,8,256]{2,1,0:T(8,128)(2,1)} %get-tuple-element.39), calls=%async_computation | async-start | bytes 131072 | tf_op jit(solution)/shard_map/all_to_all | solution.py:758
  15.0 2.3 %collective-permute-start = (bf16[480,128]{1,0:T(8,128)(2,1)S(1)}, bf16[480,128]{1,0:T(8,128)(2,1)S(1)}, u32[]{:S(2)}, u32[]{:S(2)}) collective-permute-start(bf16[480,128]{1,0:T(8,128)(2,1)S(1)} %get-tuple-element.43), channel_id=1, source_target_pairs={{0,4},{4,8},{8,12},{12,16},{16,20},{20,24},{24,28},{28,32},{32,36}... | collective-permute-start | bytes 368648 | tf_op jit(solution)/shard_map/ppermute | solution.py:763
  17.2 3.5 %collective-permute-start.1 = (bf16[480,128]{1,0:T(8,128)(2,1)S(1)}, bf16[480,128]{1,0:T(8,128)(2,1)S(1)}, u32[]{:S(2)}, u32[]{:S(2)}) collective-permute-start(bf16[480,128]{1,0:T(8,128)(2,1)S(1)} %get-tuple-element.44), channel_id=1, source_target_pairs={{0,60},{4,0},{8,4},{12,8},{16,12},{20,16},{24,20},{28,24},{32,28},... | collective-permute-start | bytes 368648 | tf_op jit(solution)/shard_map/ppermute | solution.py:763
  20.8 2.2 %reshape.20.refs_1_ = bf16[2,256,1024]{2,1,0:T(8,128)(2,1)} reshape(bf16[2,16,8,2,1024]{4,3,2,1,0:T(2,128)(2,1)} %param.23) | data formatting | bytes 2097152 | tf_op jit(solution)/shard_map/reshape | solution.py:795
  23.1 2.1 %shard_map.196.refs_3_ = f32[2,256,256]{2,1,0:T(8,128)S(1)} custom-call(f32[32,5]{1,0:T(8,128)S(1)} %copy.21.refs_0_, bf16[2,256,1024]{2,1,0:T(8,128)(2,1)} %reshape.20.refs_1_), custom_call_target="tpu_custom_call" | custom-call | tf_op jit(solution)/shard_map/pallas_call | solution.py:275
  28.3 7.1 %all-to-all-start.1 = ((bf16[16,48,256]{2,1,0:T(8,128)(2,1)}), bf16[16,48,256]{2,1,0:T(8,128)(2,1)S(1)}, u32[]{:S(2)}, u32[]{:S(2)}) async-start(bf16[16,48,256]{2,1,0:T(8,128)(2,1)} %get-tuple-element.47), calls=%async_computation.1 | async-start | bytes 786432 | tf_op jit(solution)/shard_map/all_to_all | solution.py:758
  37.1 4.2 %collective-permute-start.3 = (bf16[480,128]{1,0:T(8,128)(2,1)S(1)}, bf16[480,128]{1,0:T(8,128)(2,1)S(1)}, u32[]{:S(2)}, u32[]{:S(2)}) collective-permute-start(bf16[480,128]{1,0:T(8,128)(2,1)S(1)} %get-tuple-element.55), channel_id=1, source_target_pairs={{0,60},{4,0},{8,4},{12,8},{16,12},{20,16},{24,20},{28,24},{32,28},... | collective-permute-start | bytes 368648 | tf_op jit(solution)/shard_map/ppermute | solution.py:763
  42.0 4.4 %all-to-all-done.1.refs_0_ = bf16[16,48,256]{2,1,0:T(8,128)(2,1)S(1)} async-done(((bf16[16,48,256]{2,1,0:T(8,128)(2,1)}), bf16[16,48,256]{2,1,0:T(8,128)(2,1)S(1)}, u32[]{:S(2)}, u32[]{:S(2)}) %all-to-all-start.1) | async-done | bytes 393248 | tf_op jit(solution)/shard_map/all_to_all | solution.py:758
  46.4 2.6 %shard_map.199 = (bf16[16,96,128]{2,1,0:T(8,128)(2,1)}, f32[2,2,256,128]{3,2,1,0:T(8,128)}, bf16[8,64,128]{2,1,0:T(8,128)(2,1)}) custom-call(bf16[16,48,256]{2,1,0:T(8,128)(2,1)S(1)} %all-to-all-done.1.refs_0_, bf16[128,256]{1,0:T(8,128)(2,1)S(1)} %copy-done.7, bf16[512,128]{1,0:T(8,128)(2,1)S(1)} %copy-done.4, f32[2,256,256]{2,1,0:T(8,128)S(1)} %shard_map.196.refs_3_, ...), custom_call_target="tpu_custom_call" | custom-call | tf_op jit(solution)/shard_map/pallas_call | solution.py:275
  50.2 5.1 %all-to-all-start.2 = ((bf16[16,96,128]{2,1,0:T(8,128)(2,1)}), bf16[16,96,128]{2,1,0:T(8,128)(2,1)S(1)}, u32[]{:S(2)}, u32[]{:S(2)}) async-start(bf16[16,96,128]{2,1,0:T(8,128)(2,1)} %get-tuple-element.60), calls=%async_computation.2 | async-start | bytes 786432 | tf_op jit(solution)/shard_map/all_to_all | solution.py:758
  55.3 5.8 %shard_map.200 = (f32[5,384,128]{2,1,0:T(8,128)}, bf16[128,128]{1,0:T(8,128)(2,1)S(1)}, bf16[128,128]{1,0:T(8,128)(2,1)}, bf16[128,128]{1,0:T(8,128)(2,1)}, bf16[128,128]{1,0:T(8,128)(2,1)}) custom-call(bf16[64,128]{1,0:T(8,128)(2,1)S(1)} %get-tuple-element.37.refs_6_.refs_0_, bf16[64,128]{1,0:T(8,128)(2,1)S(1)} %get-tuple-element.38.refs_7_.refs_1_, ...), custom_call_target="tpu_custom_call" | custom-call | tf_op jit(solution)/shard_map/pallas_call | solution.py:275
  61.2 2.5 %all-to-all-done.2.refs_0_ = bf16[16,96,128]{2,1,0:T(8,128)(2,1)S(1)} async-done(((bf16[16,96,128]{2,1,0:T(8,128)(2,1)}), bf16[16,96,128]{2,1,0:T(8,128)(2,1)S(1)}, u32[]{:S(2)}, u32[]{:S(2)}) %all-to-all-start.2) | async-done | bytes 393248 | tf_op jit(solution)/shard_map/all_to_all | solution.py:758
  64.9 4.8 %all-to-all-start.3 = ((bf16[16,8,384]{2,1,0:T(8,128)(2,1)}), bf16[16,8,384]{2,1,0:T(8,128)(2,1)S(1)}, u32[]{:S(2)}, u32[]{:S(2)}) async-start(bf16[16,8,384]{2,1,0:T(8,128)(2,1)} %shard_map.201), calls=%async_computation.3 | async-start | bytes 196608 | tf_op jit(solution)/shard_map/all_to_all | solution.py:758
  70.0 1.7 %collective-permute-start.5 = (bf16[128,128]{1,0:T(8,128)(2,1)}, bf16[128,128]{1,0:T(8,128)(2,1)S(1)}, u32[]{:S(2)}, u32[]{:S(2)}) collective-permute-start(bf16[128,128]{1,0:T(8,128)(2,1)} %get-tuple-element.67), channel_id=1, source_target_pairs={{0,128},{64,192},{128,0},{192,64},{1,129},{65,193},{129,1},{193,65... | collective-permute-start | bytes 98312 | tf_op jit(solution)/shard_map/ppermute | solution.py:763
  71.7 1.7 %collective-permute-start.6 = (bf16[128,128]{1,0:T(8,128)(2,1)}, bf16[128,128]{1,0:T(8,128)(2,1)S(1)}, u32[]{:S(2)}, u32[]{:S(2)}) collective-permute-start(bf16[128,128]{1,0:T(8,128)(2,1)} %get-tuple-element.68), channel_id=1, source_target_pairs={{0,192},{64,0},{128,64},{192,128},{1,193},{65,1},{129,65},{193,129... | collective-permute-start | bytes 98312 | tf_op jit(solution)/shard_map/ppermute | solution.py:763
  75.4 3.9 %all-to-all-done.3.refs_0_ = bf16[16,8,384]{2,1,0:T(8,128)(2,1)S(1)} async-done(((bf16[16,8,384]{2,1,0:T(8,128)(2,1)}), bf16[16,8,384]{2,1,0:T(8,128)(2,1)S(1)}, u32[]{:S(2)}, u32[]{:S(2)}) %all-to-all-start.3) | async-done | bytes 98336 | tf_op jit(solution)/shard_map/all_to_all | solution.py:758
  79.3 2.0 %shard_map.202 = bf16[16,8,384]{2,1,0:T(8,128)(2,1)S(1)} custom-call(bf16[16,8,384]{2,1,0:T(8,128)(2,1)S(1)} %all-to-all-done.3.refs_0_, bf16[128,128]{1,0:T(8,128)(2,1)S(1)} %get-tuple-element.65.refs_1_, bf16[128,128]{1,0:T(8,128)(2,1)S(1)} %collective-permute-done.4.refs_2_, bf16[128,128]{1,0:T(8,128)(2,1)S(1)} %collective-permute-done.5.refs_3_, ...), custom_call_target="tpu_custom_call" | custom-call | tf_op jit(solution)/shard_map/pallas_call | solution.py:275
  81.2 14.0 %all_to_all.30.refs_0_ = bf16[16,8,384]{2,1,0:T(8,128)(2,1)S(1)} all-to-all(bf16[16,8,384]{2,1,0:T(8,128)(2,1)S(1)} %shard_map.202), channel_id=1, replica_groups=mesh['grp'=4,'row'=16,'col'=4] {'row'}, dimensions={0} | all-to-all | bytes 196608 | tf_op jit(solution)/shard_map/all_to_all | solution.py:758
  95.2 2.0 %shard_map.203 = bf16[16,16,1152]{2,1,0:T(8,128)(2,1)} custom-call(bf16[16,8,384]{2,1,0:T(8,128)(2,1)S(1)} %all_to_all.30.refs_0_, bf16[2,128,128]{2,1,0:T(8,128)(2,1)S(1)} %copy-done.6, bf16[512,512]{1,0:T(8,128)(2,1)S(1)} %copy-done, bf16[16,2,64,32]{3,2,1,0:T(8,128)(2,1)} %constant.36.clone.refs_3_), custom_call_target="tpu_custom_call" | custom-call | tf_op jit(solution)/shard_map/pallas_call | solution.py:275
  97.2 8.6 %all-to-all-start.5 = ((bf16[16,16,1152]{2,1,0:T(8,128)(2,1)}), bf16[16,16,1152]{2,1,0:T(8,128)(2,1)S(1)}, u32[]{:S(2)}, u32[]{:S(2)}) async-start(bf16[16,16,1152]{2,1,0:T(8,128)(2,1)} %shard_map.203), calls=%async_computation.5 | async-start | bytes 1179648 | tf_op jit(solution)/shard_map/all_to_all | solution.py:758
  105.8 2.0 %shard_map.204.refs_2_ = f32[4,128,1024]{2,1,0:T(8,128)S(1)} custom-call(f32[32,5]{1,0:T(8,128)S(1)} %copy.21.refs_0_, f32[2,2,256,128]{3,2,1,0:T(8,128)} %get-tuple-element.71.refs_1_), custom_call_target="tpu_custom_call" | custom-call | tf_op jit(solution)/shard_map/pallas_call | solution.py:275
  107.9 8.5 %all-to-all-done.5.refs_0_ = bf16[16,16,1152]{2,1,0:T(8,128)(2,1)S(1)} async-done(((bf16[16,16,1152]{2,1,0:T(8,128)(2,1)}), bf16[16,16,1152]{2,1,0:T(8,128)(2,1)S(1)}, u32[]{:S(2)}, u32[]{:S(2)}) %all-to-all-start.5) | async-done | bytes 589856 | tf_op jit(solution)/shard_map/all_to_all | solution.py:758
  116.4 1.9 %shard_map.205 = bf16[2,128,16,128]{3,2,1,0:T(8,128)(2,1)} custom-call(bf16[16,16,1152]{2,1,0:T(8,128)(2,1)S(1)} %all-to-all-done.5.refs_0_, bf16[256,256]{1,0:T(8,128)(2,1)S(1)} %copy-done.5, f32[4,128,1024]{2,1,0:T(8,128)S(1)} %shard_map.204.refs_2_), custom_call_target="tpu_custom_call" | custom-call | tf_op jit(solution)/shard_map/pallas_call | solution.py:275
  (45 shorter events, 10.4 us)
Async XLA Ops:
  0.6 20.1 %copy-start.14 = (f32[32,5]{0,1:T(8,128)S(1)}, f32[32,5]{0,1:T(8,128)}, u32[]{:S(2)}) copy-start(f32[32,5]{0,1:T(8,128)} %param.20) | copy-start | bytes 1924
  3.0 22.1 %copy-start.1 = (bf16[2,2,256,512]{3,2,1,0:T(8,128)(2,1)S(1)}, bf16[2,2,256,512]{3,2,1,0:T(8,128)(2,1)}, u32[]{:S(2)}) copy-start(bf16[2,2,256,512]{3,2,1,0:T(8,128)(2,1)} %constant.28.clone.refs_2_) | copy-start | bytes 3145732
  3.0 22.1 %copy-start.8 = (bf16[2,128,128]{2,1,0:T(8,128)(2,1)S(1)}, bf16[2,128,128]{2,1,0:T(8,128)(2,1)}, u32[]{:S(2)}) copy-start(bf16[2,128,128]{2,1,0:T(8,128)(2,1)} %constant.27.clone.refs_1_) | copy-start | bytes 196612
  3.1 22.1 %all-to-all-start = ((bf16[16,8,256]{2,1,0:T(8,128)(2,1)}), bf16[16,8,256]{2,1,0:T(8,128)(2,1)S(1)}, u32[]{:S(2)}, u32[]{:S(2)}) async-start(bf16[16,8,256]{2,1,0:T(8,128)(2,1)} %get-tuple-element.39), calls=%async_computation | async-start | bytes 131072 | tf_op jit(solution)/shard_map/all_to_all | solution.py:758
  15.0 10.8 %collective-permute-start = (bf16[480,128]{1,0:T(8,128)(2,1)S(1)}, bf16[480,128]{1,0:T(8,128)(2,1)S(1)}, u32[]{:S(2)}, u32[]{:S(2)}) collective-permute-start(bf16[480,128]{1,0:T(8,128)(2,1)S(1)} %get-tuple-element.43), channel_id=1, source_target_pairs={{0,4},{4,8},{8,12},{12,16},{16,20},{20,24},{24,28},{28,32},{32,36}... | collective-permute-start | bytes 368648 | tf_op jit(solution)/shard_map/ppermute | solution.py:763
  17.2 9.5 %collective-permute-start.1 = (bf16[480,128]{1,0:T(8,128)(2,1)S(1)}, bf16[480,128]{1,0:T(8,128)(2,1)S(1)}, u32[]{:S(2)}, u32[]{:S(2)}) collective-permute-start(bf16[480,128]{1,0:T(8,128)(2,1)S(1)} %get-tuple-element.44), channel_id=1, source_target_pairs={{0,60},{4,0},{8,4},{12,8},{16,12},{20,16},{24,20},{28,24},{32,28},... | collective-permute-start | bytes 368648 | tf_op jit(solution)/shard_map/ppermute | solution.py:763
  23.1 18.2 %copy-start.11 = (f32[5,32]{1,0:T(8,128)S(1)}, f32[5,32]{1,0:T(8,128)}, u32[]{:S(2)}) copy-start(f32[5,32]{1,0:T(8,128)} %refs_2_.6) | copy-start | bytes 1924
  23.1 23.4 %copy-start.4 = (bf16[512,128]{1,0:T(8,128)(2,1)S(1)}, bf16[512,128]{1,0:T(8,128)(2,1)}, u32[]{:S(2)}) copy-start(bf16[512,128]{1,0:T(8,128)(2,1)} %constant.31.clone.refs_2_) | copy-start | bytes 393220
  23.1 23.4 %copy-start.7 = (bf16[128,256]{1,0:T(8,128)(2,1)S(1)}, bf16[128,256]{1,0:T(8,128)(2,1)}, u32[]{:S(2)}) copy-start(bf16[128,256]{1,0:T(8,128)(2,1)} %constant.30.clone.refs_1_) | copy-start | bytes 196612
  25.7 29.6 %copy-start.9 = (bf16[128,256]{1,0:T(8,128)(2,1)S(1)}, bf16[128,256]{1,0:T(8,128)(2,1)}, u32[]{:S(2)}) copy-start(bf16[128,256]{1,0:T(8,128)(2,1)} %constant.32.clone.refs_2_) | copy-start | bytes 196612
  28.3 18.1 %all-to-all-start.1 = ((bf16[16,48,256]{2,1,0:T(8,128)(2,1)}), bf16[16,48,256]{2,1,0:T(8,128)(2,1)S(1)}, u32[]{:S(2)}, u32[]{:S(2)}) async-start(bf16[16,48,256]{2,1,0:T(8,128)(2,1)} %get-tuple-element.47), calls=%async_computation.1 | async-start | bytes 786432 | tf_op jit(solution)/shard_map/all_to_all | solution.py:758
  35.4 28.2 %copy-start = (bf16[512,512]{1,0:T(8,128)(2,1)S(1)}, bf16[512,512]{1,0:T(8,128)(2,1)}, u32[]{:S(2)}) copy-start(bf16[512,512]{1,0:T(8,128)(2,1)} %constant.33.clone.refs_1_.refs_2_) | copy-start | bytes 1572868
  35.4 28.2 %copy-start.2 = (bf16[2,128,512]{2,1,0:T(8,128)(2,1)S(1)}, bf16[2,128,512]{2,1,0:T(8,128)(2,1)}, u32[]{:S(2)}) copy-start(bf16[2,128,512]{2,1,0:T(8,128)(2,1)} %constant.34.clone.refs_2_) | copy-start | bytes 786436
  35.4 14.8 %collective-permute-start.2 = (bf16[480,128]{1,0:T(8,128)(2,1)S(1)}, bf16[480,128]{1,0:T(8,128)(2,1)S(1)}, u32[]{:S(2)}, u32[]{:S(2)}) collective-permute-start(bf16[480,128]{1,0:T(8,128)(2,1)S(1)} %get-tuple-element.54), channel_id=1, source_target_pairs={{0,4},{4,8},{8,12},{12,16},{16,20},{20,24},{24,28},{28,32},{32,36}... | collective-permute-start | bytes 368648 | tf_op jit(solution)/shard_map/ppermute | solution.py:763
  37.1 13.2 %collective-permute-start.3 = (bf16[480,128]{1,0:T(8,128)(2,1)S(1)}, bf16[480,128]{1,0:T(8,128)(2,1)S(1)}, u32[]{:S(2)}, u32[]{:S(2)}) collective-permute-start(bf16[480,128]{1,0:T(8,128)(2,1)S(1)} %get-tuple-element.55), channel_id=1, source_target_pairs={{0,60},{4,0},{8,4},{12,8},{16,12},{20,16},{24,20},{28,24},{32,28},... | collective-permute-start | bytes 368648 | tf_op jit(solution)/shard_map/ppermute | solution.py:763
  49.0 30.2 %copy-start.3 = (bf16[2,384,128]{2,1,0:T(8,128)(2,1)S(1)}, bf16[2,384,128]{2,1,0:T(8,128)(2,1)}, u32[]{:S(2)}) copy-start(bf16[2,384,128]{2,1,0:T(8,128)(2,1)} %constant.35.clone.refs_5_) | copy-start | bytes 589828
  50.2 13.4 %all-to-all-start.2 = ((bf16[16,96,128]{2,1,0:T(8,128)(2,1)}), bf16[16,96,128]{2,1,0:T(8,128)(2,1)S(1)}, u32[]{:S(2)}, u32[]{:S(2)}) async-start(bf16[16,96,128]{2,1,0:T(8,128)(2,1)} %get-tuple-element.60), calls=%async_computation.2 | async-start | bytes 786432 | tf_op jit(solution)/shard_map/all_to_all | solution.py:758
  55.3 39.9 %copy-start.6 = (bf16[2,128,128]{2,1,0:T(8,128)(2,1)S(1)}, bf16[2,128,128]{2,1,0:T(8,128)(2,1)}, u32[]{:S(2)}) copy-start(bf16[2,128,128]{2,1,0:T(8,128)(2,1)} %constant.37.clone.refs_1_) | copy-start | bytes 196612
  64.9 14.3 %all-to-all-start.3 = ((bf16[16,8,384]{2,1,0:T(8,128)(2,1)}), bf16[16,8,384]{2,1,0:T(8,128)(2,1)S(1)}, u32[]{:S(2)}, u32[]{:S(2)}) async-start(bf16[16,8,384]{2,1,0:T(8,128)(2,1)} %shard_map.201), calls=%async_computation.3 | async-start | bytes 196608 | tf_op jit(solution)/shard_map/all_to_all | solution.py:758
  69.7 4.4 %collective-permute-start.4 = (bf16[128,128]{1,0:T(8,128)(2,1)}, bf16[128,128]{1,0:T(8,128)(2,1)S(1)}, u32[]{:S(2)}, u32[]{:S(2)}) collective-permute-start(bf16[128,128]{1,0:T(8,128)(2,1)} %get-tuple-element.66), channel_id=1, source_target_pairs={{0,64},{64,128},{128,192},{192,0},{1,65},{65,129},{129,193},{193,1... | collective-permute-start | bytes 98312 | tf_op jit(solution)/shard_map/ppermute | solution.py:763
  70.0 4.6 %collective-permute-start.5 = (bf16[128,128]{1,0:T(8,128)(2,1)}, bf16[128,128]{1,0:T(8,128)(2,1)S(1)}, u32[]{:S(2)}, u32[]{:S(2)}) collective-permute-start(bf16[128,128]{1,0:T(8,128)(2,1)} %get-tuple-element.67), channel_id=1, source_target_pairs={{0,128},{64,192},{128,0},{192,64},{1,129},{65,193},{129,1},{193,65... | collective-permute-start | bytes 98312 | tf_op jit(solution)/shard_map/ppermute | solution.py:763
  71.7 3.7 %collective-permute-start.6 = (bf16[128,128]{1,0:T(8,128)(2,1)}, bf16[128,128]{1,0:T(8,128)(2,1)S(1)}, u32[]{:S(2)}, u32[]{:S(2)}) collective-permute-start(bf16[128,128]{1,0:T(8,128)(2,1)} %get-tuple-element.68), channel_id=1, source_target_pairs={{0,192},{64,0},{128,64},{192,128},{1,193},{65,1},{129,65},{193,129... | collective-permute-start | bytes 98312 | tf_op jit(solution)/shard_map/ppermute | solution.py:763
  97.2 19.2 %copy-start.5 = (bf16[256,256]{1,0:T(8,128)(2,1)S(1)}, bf16[256,256]{1,0:T(8,128)(2,1)}, u32[]{:S(2)}) copy-start(bf16[256,256]{1,0:T(8,128)(2,1)} %constant.38.clone.refs_1_) | copy-start | bytes 393220
  97.2 19.2 %all-to-all-start.5 = ((bf16[16,16,1152]{2,1,0:T(8,128)(2,1)}), bf16[16,16,1152]{2,1,0:T(8,128)(2,1)S(1)}, u32[]{:S(2)}, u32[]{:S(2)}) async-start(bf16[16,16,1152]{2,1,0:T(8,128)(2,1)} %shard_map.203), calls=%async_computation.5 | async-start | bytes 1179648 | tf_op jit(solution)/shard_map/all_to_all | solution.py:758
  (3 other events, 28.3 us)

commit v5 on v4

--- a/solution.py
+++ b/solution.py
@@ -243,7 +243,7 @@
             copy.wait()
 
 
-def call(body, outs, inputs, tables=(), scratch=(), far=None):
+def call(body, outs, inputs, tables=(), scratch=(), far=None, flops=None):
     far = far or {}
     single = not isinstance(outs, (list, tuple))
     shapes = [outs] if single else list(outs)
@@ -279,6 +279,7 @@
         out_specs=[hbm if k in far else vmem for k in range(m)],
         scratch_shapes=spaces + sems + list(scratch),
         compiler_params=pltpu.CompilerParams(vmem_limit_bytes=VMEM_LIMIT),
+        cost_estimate=flops and pl.CostEstimate(flops=flops, bytes_accessed=0, transcendentals=0),
     )(*inputs, *[pltpu.with_memory_space_constraint(a, pltpu.HBM) for a, _ in tables])
     return result[0] if single else result
 
@@ -461,26 +462,30 @@
     out[...] = table_dot(ty, stacked).reshape(16, 8, 384).astype(BF)
 
 
-def cell_kernel(got, snap0, snap1, snap2, snap3, tx, lift_mix, project_t, out, kept):
+def local_cells_kernel(snap0, snap1, snap2, snap3, lift_mix, local, gap, kept):
     g = own_group()
     for d, snap in enumerate((snap0, snap1, snap2, snap3)):
         kept[(g + 4 - d) % 4] = snap[...].astype(F32)
     snap = kept[0:3].reshape(384, 128)
-    high, low = split(snap)
-    preact = dot(high, lift_mix[0]) + dot(low, lift_mix[0]) + dot(high, lift_mix[1])
+    cells = snap.astype(BF)
+    local[...] = dot(cells, lift_mix[0]) + dot(cells, lift_mix[1])
+    lane = iota((384, 128), 1)
+    gap[...] = jnp.where(lane < 64, snap - pltpu.roll(snap, 64, 1), 0.0)
+
+
+def cell_kernel(got, local, gap, tx, project_t, out):
     rows = got[...].astype(F32).reshape(128, 384).astype(BF)
+    preact = local[...]
     preact = preact + table_dot(tx, rows)
     rate = math.sqrt(2.0 / math.pi)
     square = preact * preact
     bend = jnp.tanh(rate * preact * (1.0 + 0.044715 * square))
     activated = 0.5 * preact * (1.0 + bend)
     slope = 0.5 * (1.0 + bend) + 0.5 * preact * (1.0 - bend * bend) * rate * (1.0 + 3 * 0.044715 * square)
-    lane = iota((384, 128), 1)
-    gap = jnp.where(lane < 64, snap - pltpu.roll(snap, 64, 1), 0.0)
     turned = ((1,), (1,))
     high, low = split(activated)
     misfit = dot(high, project_t[0], turned) + dot(low, project_t[0], turned) + dot(high, project_t[1], turned)
-    misfit = misfit + gap
+    misfit = misfit + gap[...]
     back = dot3_table(misfit, project_t) * slope
     out[...] = table_dot3(tx, back, ((0,), (0,))).reshape(16, 8, 384).astype(BF)
 
@@ -647,16 +652,16 @@
     return dot(sides, one_hot((16, F * 128), put_at).astype(BF), ((0,), (0,)))
 
 
-def steps_kernel(xlo, xhi, pool, near, fields, below2, kept, above2, new, *refs):
+def steps_kernel(xlo, xhi, pool, fields, near, below2, kept, above2, new, *refs):
     snaps, (state, middle, stepped, around, rows) = refs[:4], refs[4:]
     g = own_group()
     outside = g == 3
-    fields, near = fields.get(), near.get()
-    kept = kept.get()
-    slabs = ((0, below2.get()), (1, kept.at[0]), (6, kept.at[1]), (7, above2.get()))
     for f in range(F):
         for y in range(4):
             state[f, y + 2] = fields[f, pl.ds(y, 96, stride=4), :]
+    near, kept = near.get(), kept.get()
+    slabs = ((0, below2.get()), (1, kept.at[0]), (6, kept.at[1]), (7, above2.get()))
+    for f in range(F):
         for k, slab in slabs:
             state[f, k] = slab[f * 96 : f * 96 + 96, :].astype(F32)
     for k in range(8):
@@ -822,8 +827,8 @@
     new_fields, *snaps = call(
         steps_kernel,
         [shape((F, 384, 128), F32)] + [shape((128, 128), BF)] * 4,
-        [*faces[2:], table_pool_x()],
-        [(v, None) for v in (near, flat, below2, kept, above2)],
+        [*faces[2:], table_pool_x(), flat],
+        [(v, None) for v in (near, below2, kept, above2)],
         [
             pltpu.VMEM((F, 8, 96, 128), F32),
             pltpu.VMEM((F, 6, 96, 128), F32),
@@ -833,17 +838,19 @@
         ],
         far={0: F, 2: 1, 3: 1, 4: 1},
     )
-    got, snaps[1:] = tied(got, snaps[1:])
+    got, _ = tied(got, snaps[1:])
     planes = call(inverse_y_kernel, shape((16, 8, 384), BF), [got, table_lanes(), table_y_inverse()])
     got = swap(planes, "row")
-    for d in range(1, 4):
+    for d in (2, 1, 3):
         snaps[d] = shift(snaps[d], "grp", d)
-    back = call(
-        cell_kernel,
-        shape((16, 8, 384), BF),
-        [got, *snaps, table_x_inverse(), *maps],
+    local, gap = call(
+        local_cells_kernel,
+        [shape((384, 384), F32), shape((384, 128), F32)],
+        [*snaps, maps[0]],
         scratch=[pltpu.VMEM((4, 128, 128), F32)],
-    )
+        flops=60_000_000_000,
+    )
+    back = call(cell_kernel, shape((16, 8, 384), BF), [got, local, gap, table_x_inverse(), maps[1]])
     got = swap(back, "row")
     back = call(
         back_yz_kernel,

time: 119 us -> 118 us (level)
  blocking collectives: 14 us -> 11.9 us
    all_to_all x5, waiting for transfers between devices: 19.3 us -> 22.2 us  [swap(): return lax.all_to_all(x, axes, 0, 0, tiled=True)]
    all_to_all x1, blocking collectives: 14 us -> 11.9 us  [swap(): return lax.all_to_all(x, axes, 0, 0, tiled=True)]
    ppermute x7, waiting for transfers between devices: 4.15 us -> 2.26 us  [shift(): return lax.ppermute(x, axis, [(i, (i + step) % size) for i in range(size)])]
    ppermute x7, starting transfers between devices: 15.2 us -> 16.6 us  [shift(): return lax.ppermute(x, axis, [(i, (i + step) % size) for i in range(size)])]
    all_to_all x5, starting transfers between devices: 37.4 us -> 36.2 us  [swap(): return lax.all_to_all(x, axes, 0, 0, tiled=True)]
    pallas_call x12 -> x13, Pallas kernels: 24.9 us -> 24.6 us  [call(): pl.pallas_call(kernel, out_shape=[pltpu.HBM(o.shape, o.dtype) if k in far...]
  transfers between devices with their start and end apart: 12 -> 12, of which waited for: 9 -> 5; matrix products, arithmetic and copies ran while one was open for 2% -> 2% of each run, Pallas kernels for 12% -> 13%
where the time goes in v5:
time: 118 us; the launch traced here: 117 us
  starting transfers between devices  52.7 us (45%)
  Pallas kernels  24.6 us (21%)
  waiting for transfers between devices  24.4 us (21%)
  blocking collectives  11.9 us (10%)
  local copies, waits for them, and re-layouts  2.42 us (2%)
    all_to_all x5, starting transfers between devices, swap(): return lax.all_to_all(x, axes, 0, 0, tiled=True)  36.2 us
    pallas_call x13, Pallas kernels, call(): pl.pallas_call(kernel, out_shape=[pltpu.HBM(o.shape, o.dtype) if k in far...  24.6 us
    all_to_all x5, waiting for transfers between devices, swap(): return lax.all_to_all(x, axes, 0, 0, tiled=True)  22.2 us
    ppermute x7, starting transfers between devices, shift(): return lax.ppermute(x, axis, [(i, (i + step) % size) for i in range(size)])  16.6 us
    all_to_all x1, blocking collectives, swap(): return lax.all_to_all(x, axes, 0, 0, tiled=True)  11.9 us
  transfers between devices with their start and end apart: 12, of which 5 were waited for; matrix products, arithmetic and copies ran while one was open for 2% of the time, Pallas kernels for 13%

profile of v5, /device:TPU:1, one launch (start us, length us, event | category | flops | bytes accessed | tf_op | source)
XLA Modules:
  0.0 117.2 jit_solution(493123672189126119)
XLA Ops:
  0.6 2.4 %shard_map.194 = (bf16[16,8,256]{2,1,0:T(8,128)(2,1)}, bf16[480,128]{1,0:T(8,128)(2,1)S(1)}, bf16[480,128]{1,0:T(8,128)(2,1)S(1)}, bf16[480,128]{1,0:T(8,128)(2,...) custom-call(f32[5,384,128]{2,1,0:T(8,128)} %bitcast.7, ...), custom_call_target="tpu_custom_call" | custom-call | tf_op jit(solution)/shard_map/pallas_call | solution.py:275
  3.1 11.9 %all-to-all-start = ((bf16[16,8,256]{2,1,0:T(8,128)(2,1)}), bf16[16,8,256]{2,1,0:T(8,128)(2,1)S(1)}, u32[]{:S(2)}, u32[]{:S(2)}) async-start(bf16[16,8,256]{2,1,0:T(8,128)(2,1)} %get-tuple-element.38), calls=%async_computation | async-start | bytes 131072 | tf_op jit(solution)/shard_map/all_to_all | solution.py:763
  15.0 2.3 %collective-permute-start = (bf16[480,128]{1,0:T(8,128)(2,1)S(1)}, bf16[480,128]{1,0:T(8,128)(2,1)S(1)}, u32[]{:S(2)}, u32[]{:S(2)}) collective-permute-start(bf16[480,128]{1,0:T(8,128)(2,1)S(1)} %get-tuple-element.42), channel_id=1, source_target_pairs={{0,4},{4,8},{8,12},{12,16},{16,20},{20,24},{24,28},{28,32},{32,36}... | collective-permute-start | bytes 368648 | tf_op jit(solution)/shard_map/ppermute | solution.py:768
  17.2 3.5 %collective-permute-start.1 = (bf16[480,128]{1,0:T(8,128)(2,1)S(1)}, bf16[480,128]{1,0:T(8,128)(2,1)S(1)}, u32[]{:S(2)}, u32[]{:S(2)}) collective-permute-start(bf16[480,128]{1,0:T(8,128)(2,1)S(1)} %get-tuple-element.43), channel_id=1, source_target_pairs={{0,60},{4,0},{8,4},{12,8},{16,12},{20,16},{24,20},{28,24},{32,28},... | collective-permute-start | bytes 368648 | tf_op jit(solution)/shard_map/ppermute | solution.py:768
  20.8 2.2 %reshape.20.refs_1_ = bf16[2,256,1024]{2,1,0:T(8,128)(2,1)} reshape(bf16[2,16,8,2,1024]{4,3,2,1,0:T(2,128)(2,1)} %param.23) | data formatting | bytes 2097152 | tf_op jit(solution)/shard_map/reshape | solution.py:800
  23.1 2.1 %shard_map.196.refs_3_ = f32[2,256,256]{2,1,0:T(8,128)S(1)} custom-call(f32[32,5]{1,0:T(8,128)S(1)} %copy.21.refs_0_, bf16[2,256,1024]{2,1,0:T(8,128)(2,1)} %reshape.20.refs_1_), custom_call_target="tpu_custom_call" | custom-call | tf_op jit(solution)/shard_map/pallas_call | solution.py:275
  26.8 1.6 %shard_map.197 = (bf16[16,48,256]{2,1,0:T(8,128)(2,1)}, bf16[2,480,128]{2,1,0:T(8,128)(2,1)}) custom-call(bf16[16,16,256]{2,1,0:T(8,128)(2,1)S(1)} %get-tuple-element.40.refs_0_, f32[16,8,128]{2,1,0:T(8,128)S(1)} %get-tuple-element.41.refs_1_, bf16[480,128]{1,0:T(8,128)(2,1)S(1)} %collective-permute-done.refs_2_, ...), custom_call_target="tpu_custom_call" | custom-call | tf_op jit(solution)/shard_map/pallas_call | solution.py:275
  28.3 7.1 %all-to-all-start.1 = ((bf16[16,48,256]{2,1,0:T(8,128)(2,1)}), bf16[16,48,256]{2,1,0:T(8,128)(2,1)S(1)}, u32[]{:S(2)}, u32[]{:S(2)}) async-start(bf16[16,48,256]{2,1,0:T(8,128)(2,1)} %get-tuple-element.46), calls=%async_computation.1 | async-start | bytes 786432 | tf_op jit(solution)/shard_map/all_to_all | solution.py:763
  35.4 1.6 %collective-permute-start.2 = (bf16[480,128]{1,0:T(8,128)(2,1)}, bf16[480,128]{1,0:T(8,128)(2,1)}, u32[]{:S(2)}, u32[]{:S(2)}) collective-permute-start(bf16[480,128]{1,0:T(8,128)(2,1)} %copy-done.13), channel_id=1, source_target_pairs={{0,4},{4,8},{8,12},{12,16},{16,20},{20,24},{24,28},{28,32},{32,36}... | collective-permute-start | bytes 368648 | tf_op jit(solution)/shard_map/ppermute | solution.py:768
  37.1 4.2 %collective-permute-start.3 = (bf16[480,128]{1,0:T(8,128)(2,1)S(1)}, bf16[480,128]{1,0:T(8,128)(2,1)}, u32[]{:S(2)}, u32[]{:S(2)}) collective-permute-start(bf16[480,128]{1,0:T(8,128)(2,1)S(1)} %get-tuple-element.54), channel_id=1, source_target_pairs={{0,60},{4,0},{8,4},{12,8},{16,12},{20,16},{24,20},{28,24},{32,28},... | collective-permute-start | bytes 368648 | tf_op jit(solution)/shard_map/ppermute | solution.py:768
  42.0 4.4 %all-to-all-done.1.refs_0_ = bf16[16,48,256]{2,1,0:T(8,128)(2,1)S(1)} async-done(((bf16[16,48,256]{2,1,0:T(8,128)(2,1)}), bf16[16,48,256]{2,1,0:T(8,128)(2,1)S(1)}, u32[]{:S(2)}, u32[]{:S(2)}) %all-to-all-start.1) | async-done | bytes 393248 | tf_op jit(solution)/shard_map/all_to_all | solution.py:763
  46.5 2.6 %shard_map.199 = (bf16[16,96,128]{2,1,0:T(8,128)(2,1)}, f32[2,2,256,128]{3,2,1,0:T(8,128)}, bf16[8,64,128]{2,1,0:T(8,128)(2,1)}) custom-call(bf16[16,48,256]{2,1,0:T(8,128)(2,1)S(1)} %all-to-all-done.1.refs_0_, bf16[128,256]{1,0:T(8,128)(2,1)S(1)} %copy-done.8, bf16[512,128]{1,0:T(8,128)(2,1)S(1)} %copy-done.5, f32[2,256,256]{2,1,0:T(8,128)S(1)} %shard_map.196.refs_3_, ...), custom_call_target="tpu_custom_call" | custom-call | tf_op jit(solution)/shard_map/pallas_call | solution.py:275
  50.3 5.0 %all-to-all-start.2 = ((bf16[16,96,128]{2,1,0:T(8,128)(2,1)}), bf16[16,96,128]{2,1,0:T(8,128)(2,1)S(1)}, u32[]{:S(2)}, u32[]{:S(2)}) async-start(bf16[16,96,128]{2,1,0:T(8,128)(2,1)} %get-tuple-element.59), calls=%async_computation.2 | async-start | bytes 786432 | tf_op jit(solution)/shard_map/all_to_all | solution.py:763
  55.4 5.6 %shard_map.200 = (f32[5,384,128]{2,1,0:T(8,128)}, bf16[128,128]{1,0:T(8,128)(2,1)S(1)}, bf16[128,128]{1,0:T(8,128)(2,1)}, bf16[128,128]{1,0:T(8,128)(2,1)}, bf16[128,128]{1,0:T(8,128)(2,1)}) custom-call(bf16[64,128]{1,0:T(8,128)(2,1)S(1)} %get-tuple-element.36.refs_6_.refs_0_, bf16[64,128]{1,0:T(8,128)(2,1)S(1)} %get-tuple-element.37.refs_7_.refs_1_, ...), custom_call_target="tpu_custom_call" | custom-call | tf_op jit(solution)/shard_map/pallas_call | solution.py:275
  62.4 2.4 %collective-permute-start.5 = (bf16[128,128]{1,0:T(8,128)(2,1)}, bf16[128,128]{1,0:T(8,128)(2,1)S(1)}, u32[]{:S(2)}, u32[]{:S(2)}) collective-permute-start(bf16[128,128]{1,0:T(8,128)(2,1)} %get-tuple-element.61), channel_id=1, source_target_pairs={{0,128},{64,192},{128,0},{192,64},{1,129},{65,193},{129,1},{193,65... | collective-permute-start | bytes 98312 | tf_op jit(solution)/shard_map/ppermute | solution.py:768
  67.3 4.8 %all-to-all-start.3 = ((bf16[16,8,384]{2,1,0:T(8,128)(2,1)}), bf16[16,8,384]{2,1,0:T(8,128)(2,1)S(1)}, u32[]{:S(2)}, u32[]{:S(2)}) async-start(bf16[16,8,384]{2,1,0:T(8,128)(2,1)} %shard_map.201), calls=%async_computation.3 | async-start | bytes 196608 | tf_op jit(solution)/shard_map/all_to_all | solution.py:763
  72.5 9.2 %all-to-all-done.3.refs_0_ = bf16[16,8,384]{2,1,0:T(8,128)(2,1)S(1)} async-done(((bf16[16,8,384]{2,1,0:T(8,128)(2,1)}), bf16[16,8,384]{2,1,0:T(8,128)(2,1)S(1)}, u32[]{:S(2)}, u32[]{:S(2)}) %all-to-all-start.3) | async-done | bytes 98336 | tf_op jit(solution)/shard_map/all_to_all | solution.py:763
  81.7 1.6 %shard_map.203 = bf16[16,8,384]{2,1,0:T(8,128)(2,1)S(1)} custom-call(bf16[16,8,384]{2,1,0:T(8,128)(2,1)S(1)} %all-to-all-done.3.refs_0_, f32[384,384]{1,0:T(8,128)S(1)} %get-tuple-element.66.refs_1_, f32[384,128]{1,0:T(8,128)S(1)} %get-tuple-element.67.refs_2_, bf16[2,384,128]{2,1,0:T(8,128)(2,1)S(1)} %copy-done.4, ...), custom_call_target="tpu_custom_call" | custom-call | tf_op jit(solution)/shard_map/pallas_call | solution.py:275
  83.2 11.9 %all_to_all.30.refs_0_ = bf16[16,8,384]{2,1,0:T(8,128)(2,1)S(1)} all-to-all(bf16[16,8,384]{2,1,0:T(8,128)(2,1)S(1)} %shard_map.203), channel_id=1, replica_groups=mesh['grp'=4,'row'=16,'col'=4] {'row'}, dimensions={0} | all-to-all | bytes 196608 | tf_op jit(solution)/shard_map/all_to_all | solution.py:763
  95.2 2.0 %shard_map.204 = bf16[16,16,1152]{2,1,0:T(8,128)(2,1)} custom-call(bf16[16,8,384]{2,1,0:T(8,128)(2,1)S(1)} %all_to_all.30.refs_0_, bf16[2,128,128]{2,1,0:T(8,128)(2,1)S(1)} %copy-done.7, bf16[512,512]{1,0:T(8,128)(2,1)S(1)} %copy-done.1, bf16[16,2,64,32]{3,2,1,0:T(8,128)(2,1)} %constant.36.clone.refs_3_), custom_call_target="tpu_custom_call" | custom-call | tf_op jit(solution)/shard_map/pallas_call | solution.py:275
  97.2 7.4 %all-to-all-start.5 = ((bf16[16,16,1152]{2,1,0:T(8,128)(2,1)}), bf16[16,16,1152]{2,1,0:T(8,128)(2,1)S(1)}, u32[]{:S(2)}, u32[]{:S(2)}) async-start(bf16[16,16,1152]{2,1,0:T(8,128)(2,1)} %shard_map.204), calls=%async_computation.5 | async-start | bytes 1179648 | tf_op jit(solution)/shard_map/all_to_all | solution.py:763
  104.5 2.0 %shard_map.205.refs_2_ = f32[4,128,1024]{2,1,0:T(8,128)S(1)} custom-call(f32[32,5]{1,0:T(8,128)S(1)} %copy.21.refs_0_, f32[2,2,256,128]{3,2,1,0:T(8,128)} %get-tuple-element.69.refs_1_), custom_call_target="tpu_custom_call" | custom-call | tf_op jit(solution)/shard_map/pallas_call | solution.py:275
  106.6 8.6 %all-to-all-done.5.refs_0_ = bf16[16,16,1152]{2,1,0:T(8,128)(2,1)S(1)} async-done(((bf16[16,16,1152]{2,1,0:T(8,128)(2,1)}), bf16[16,16,1152]{2,1,0:T(8,128)(2,1)S(1)}, u32[]{:S(2)}, u32[]{:S(2)}) %all-to-all-start.5) | async-done | bytes 589856 | tf_op jit(solution)/shard_map/all_to_all | solution.py:763
  115.1 1.9 %shard_map.206 = bf16[2,128,16,128]{3,2,1,0:T(8,128)(2,1)} custom-call(bf16[16,16,1152]{2,1,0:T(8,128)(2,1)S(1)} %all-to-all-done.5.refs_0_, bf16[256,256]{1,0:T(8,128)(2,1)S(1)} %copy-done.6, f32[4,128,1024]{2,1,0:T(8,128)S(1)} %shard_map.205.refs_2_), custom_call_target="tpu_custom_call" | custom-call | tf_op jit(solution)/shard_map/pallas_call | solution.py:275
  (46 shorter events, 8.0 us)
Async XLA Ops:
  0.6 20.1 %copy-start.14 = (f32[32,5]{0,1:T(8,128)S(1)}, f32[32,5]{0,1:T(8,128)}, u32[]{:S(2)}) copy-start(f32[32,5]{0,1:T(8,128)} %param.20) | copy-start | bytes 1924
  3.0 22.7 %copy-start.13 = (bf16[480,128]{1,0:T(8,128)(2,1)}, bf16[480,128]{1,0:T(8,128)(2,1)S(1)}, u32[]{:S(2)}) copy-start(bf16[480,128]{1,0:T(8,128)(2,1)S(1)} %get-tuple-element.53) | copy-start | bytes 368644
  3.0 22.1 %copy-start.2 = (bf16[2,2,256,512]{3,2,1,0:T(8,128)(2,1)S(1)}, bf16[2,2,256,512]{3,2,1,0:T(8,128)(2,1)}, u32[]{:S(2)}) copy-start(bf16[2,2,256,512]{3,2,1,0:T(8,128)(2,1)} %constant.28.clone.refs_2_) | copy-start | bytes 3145732
  3.0 22.1 %copy-start.9 = (bf16[2,128,128]{2,1,0:T(8,128)(2,1)S(1)}, bf16[2,128,128]{2,1,0:T(8,128)(2,1)}, u32[]{:S(2)}) copy-start(bf16[2,128,128]{2,1,0:T(8,128)(2,1)} %constant.27.clone.refs_1_) | copy-start | bytes 196612
  3.1 22.1 %all-to-all-start = ((bf16[16,8,256]{2,1,0:T(8,128)(2,1)}), bf16[16,8,256]{2,1,0:T(8,128)(2,1)S(1)}, u32[]{:S(2)}, u32[]{:S(2)}) async-start(bf16[16,8,256]{2,1,0:T(8,128)(2,1)} %get-tuple-element.38), calls=%async_computation | async-start | bytes 131072 | tf_op jit(solution)/shard_map/all_to_all | solution.py:763
  15.0 10.8 %collective-permute-start = (bf16[480,128]{1,0:T(8,128)(2,1)S(1)}, bf16[480,128]{1,0:T(8,128)(2,1)S(1)}, u32[]{:S(2)}, u32[]{:S(2)}) collective-permute-start(bf16[480,128]{1,0:T(8,128)(2,1)S(1)} %get-tuple-element.42), channel_id=1, source_target_pairs={{0,4},{4,8},{8,12},{12,16},{16,20},{20,24},{24,28},{28,32},{32,36}... | collective-permute-start | bytes 368648 | tf_op jit(solution)/shard_map/ppermute | solution.py:768
  17.2 9.5 %collective-permute-start.1 = (bf16[480,128]{1,0:T(8,128)(2,1)S(1)}, bf16[480,128]{1,0:T(8,128)(2,1)S(1)}, u32[]{:S(2)}, u32[]{:S(2)}) collective-permute-start(bf16[480,128]{1,0:T(8,128)(2,1)S(1)} %get-tuple-element.43), channel_id=1, source_target_pairs={{0,60},{4,0},{8,4},{12,8},{16,12},{20,16},{24,20},{28,24},{32,28},... | collective-permute-start | bytes 368648 | tf_op jit(solution)/shard_map/ppermute | solution.py:768
  23.1 18.2 %copy-start.12 = (f32[5,32]{1,0:T(8,128)S(1)}, f32[5,32]{1,0:T(8,128)}, u32[]{:S(2)}) copy-start(f32[5,32]{1,0:T(8,128)} %refs_2_.6) | copy-start | bytes 1924
  23.1 23.4 %copy-start.5 = (bf16[512,128]{1,0:T(8,128)(2,1)S(1)}, bf16[512,128]{1,0:T(8,128)(2,1)}, u32[]{:S(2)}) copy-start(bf16[512,128]{1,0:T(8,128)(2,1)} %constant.31.clone.refs_2_) | copy-start | bytes 393220
  23.1 23.4 %copy-start.8 = (bf16[128,256]{1,0:T(8,128)(2,1)S(1)}, bf16[128,256]{1,0:T(8,128)(2,1)}, u32[]{:S(2)}) copy-start(bf16[128,256]{1,0:T(8,128)(2,1)} %constant.30.clone.refs_1_) | copy-start | bytes 196612
  25.7 29.6 %copy-start = (f32[5,96,4,128]{3,2,1,0:T(4,128)S(1)}, f32[5,96,4,128]{3,2,1,0:T(4,128)}, u32[]{:S(2)}) copy-start(f32[5,96,4,128]{3,2,1,0:T(4,128)} %param.19) | copy-start | bytes 2949124
  25.8 29.6 %copy-start.10 = (bf16[128,256]{1,0:T(8,128)(2,1)S(1)}, bf16[128,256]{1,0:T(8,128)(2,1)}, u32[]{:S(2)}) copy-start(bf16[128,256]{1,0:T(8,128)(2,1)} %constant.32.clone.refs_2_) | copy-start | bytes 196612
  28.3 18.1 %all-to-all-start.1 = ((bf16[16,48,256]{2,1,0:T(8,128)(2,1)}), bf16[16,48,256]{2,1,0:T(8,128)(2,1)S(1)}, u32[]{:S(2)}, u32[]{:S(2)}) async-start(bf16[16,48,256]{2,1,0:T(8,128)(2,1)} %get-tuple-element.46), calls=%async_computation.1 | async-start | bytes 786432 | tf_op jit(solution)/shard_map/all_to_all | solution.py:763
  35.4 30.6 %copy-start.1 = (bf16[512,512]{1,0:T(8,128)(2,1)S(1)}, bf16[512,512]{1,0:T(8,128)(2,1)}, u32[]{:S(2)}) copy-start(bf16[512,512]{1,0:T(8,128)(2,1)} %constant.33.clone.refs_1_.refs_2_) | copy-start | bytes 1572868
  35.4 30.6 %copy-start.3 = (bf16[2,128,512]{2,1,0:T(8,128)(2,1)S(1)}, bf16[2,128,512]{2,1,0:T(8,128)(2,1)}, u32[]{:S(2)}) copy-start(bf16[2,128,512]{2,1,0:T(8,128)(2,1)} %constant.34.clone.refs_2_) | copy-start | bytes 786436
  35.4 14.9 %collective-permute-start.2 = (bf16[480,128]{1,0:T(8,128)(2,1)}, bf16[480,128]{1,0:T(8,128)(2,1)}, u32[]{:S(2)}, u32[]{:S(2)}) collective-permute-start(bf16[480,128]{1,0:T(8,128)(2,1)} %copy-done.13), channel_id=1, source_target_pairs={{0,4},{4,8},{8,12},{12,16},{16,20},{20,24},{24,28},{28,32},{32,36}... | collective-permute-start | bytes 368648 | tf_op jit(solution)/shard_map/ppermute | solution.py:768
  37.1 13.3 %collective-permute-start.3 = (bf16[480,128]{1,0:T(8,128)(2,1)S(1)}, bf16[480,128]{1,0:T(8,128)(2,1)}, u32[]{:S(2)}, u32[]{:S(2)}) collective-permute-start(bf16[480,128]{1,0:T(8,128)(2,1)S(1)} %get-tuple-element.54), channel_id=1, source_target_pairs={{0,60},{4,0},{8,4},{12,8},{16,12},{20,16},{24,20},{28,24},{32,28},... | collective-permute-start | bytes 368648 | tf_op jit(solution)/shard_map/ppermute | solution.py:768
  50.3 15.7 %all-to-all-start.2 = ((bf16[16,96,128]{2,1,0:T(8,128)(2,1)}), bf16[16,96,128]{2,1,0:T(8,128)(2,1)S(1)}, u32[]{:S(2)}, u32[]{:S(2)}) async-start(bf16[16,96,128]{2,1,0:T(8,128)(2,1)} %get-tuple-element.59), calls=%async_computation.2 | async-start | bytes 786432 | tf_op jit(solution)/shard_map/all_to_all | solution.py:763
  61.0 11.1 %collective-permute-start.4 = (bf16[128,128]{1,0:T(8,128)(2,1)}, bf16[128,128]{1,0:T(8,128)(2,1)S(1)}, u32[]{:S(2)}, u32[]{:S(2)}) collective-permute-start(bf16[128,128]{1,0:T(8,128)(2,1)} %get-tuple-element.60), channel_id=1, source_target_pairs={{0,64},{64,128},{128,192},{192,0},{1,65},{65,129},{129,193},{193,1... | collective-permute-start | bytes 98312 | tf_op jit(solution)/shard_map/ppermute | solution.py:768
  62.4 9.6 %collective-permute-start.5 = (bf16[128,128]{1,0:T(8,128)(2,1)}, bf16[128,128]{1,0:T(8,128)(2,1)S(1)}, u32[]{:S(2)}, u32[]{:S(2)}) collective-permute-start(bf16[128,128]{1,0:T(8,128)(2,1)} %get-tuple-element.61), channel_id=1, source_target_pairs={{0,128},{64,192},{128,0},{192,64},{1,129},{65,193},{129,1},{193,65... | collective-permute-start | bytes 98312 | tf_op jit(solution)/shard_map/ppermute | solution.py:768
  64.8 7.3 %collective-permute-start.6 = (bf16[128,128]{1,0:T(8,128)(2,1)}, bf16[128,128]{1,0:T(8,128)(2,1)S(1)}, u32[]{:S(2)}, u32[]{:S(2)}) collective-permute-start(bf16[128,128]{1,0:T(8,128)(2,1)} %get-tuple-element.62), channel_id=1, source_target_pairs={{0,192},{64,0},{128,64},{192,128},{1,193},{65,1},{129,65},{193,129... | collective-permute-start | bytes 98312 | tf_op jit(solution)/shard_map/ppermute | solution.py:768
  67.3 14.4 %all-to-all-start.3 = ((bf16[16,8,384]{2,1,0:T(8,128)(2,1)}), bf16[16,8,384]{2,1,0:T(8,128)(2,1)S(1)}, u32[]{:S(2)}, u32[]{:S(2)}) async-start(bf16[16,8,384]{2,1,0:T(8,128)(2,1)} %shard_map.201), calls=%async_computation.3 | async-start | bytes 196608 | tf_op jit(solution)/shard_map/all_to_all | solution.py:763
  72.1 23.0 %copy-start.7 = (bf16[2,128,128]{2,1,0:T(8,128)(2,1)S(1)}, bf16[2,128,128]{2,1,0:T(8,128)(2,1)}, u32[]{:S(2)}) copy-start(bf16[2,128,128]{2,1,0:T(8,128)(2,1)} %constant.37.clone.refs_1_) | copy-start | bytes 196612
  97.2 18.0 %all-to-all-start.5 = ((bf16[16,16,1152]{2,1,0:T(8,128)(2,1)}), bf16[16,16,1152]{2,1,0:T(8,128)(2,1)S(1)}, u32[]{:S(2)}, u32[]{:S(2)}) async-start(bf16[16,16,1152]{2,1,0:T(8,128)(2,1)} %shard_map.204), calls=%async_computation.5 | async-start | bytes 1179648 | tf_op jit(solution)/shard_map/all_to_all | solution.py:763
  (3 other events, 45.7 us)

commit v6 on v5

--- a/solution.py
+++ b/solution.py
@@ -516,9 +516,8 @@
         for g2 in range(4):
             part = result[g2 * 16 : g2 * 16 + 16]
             high = part.astype(BF)
-            out.ref[g2 * 4 + c2, :, 0:1024] = high
-            out.ref[g2 * 4 + c2, :, 1024:1152] = (part[:, :128] - high[:, :128].astype(F32)).astype(BF)
-            out.push(g2 * 4 + c2)
+            out[g2 * 4 + c2, :, 0:1024] = high
+            out[g2 * 4 + c2, :, 1024:1152] = (part[:, :128] - high[:, :128].astype(F32)).astype(BF)
 
 
 def grad_kernel(got, expand, spectrum, out, cells, wide):
@@ -585,7 +584,8 @@
     for q in range(2):
         for kx in range(2):
             rows = jnp.concatenate([spread_v[q, half, pl.ds(kx, 128, stride=2), :] for half in range(2)], axis=1)
-            out[2 * q + kx] = dot3_table(rows, tables)
+            out.ref[2 * q + kx] = dot3_table(rows, tables)
+            out.push(2 * q + kx)
 
 
 def emit_faces(state, slabs, faces, face):
@@ -850,6 +850,16 @@
         scratch=[pltpu.VMEM((4, 128, 128), F32)],
         flops=60_000_000_000,
     )
+    spread, local = tied(spread, local)
+    spectrum = call(
+        spectrum_kernel,
+        shape((4, 128, 1024), F32),
+        [lift_weight],
+        [(spread, None)],
+        [pltpu.VMEM((256, 1024), F32)],
+        far={0: 4},
+    )
+    got, spectrum = tied(got, spectrum)
     back = call(cell_kernel, shape((16, 8, 384), BF), [got, local, gap, table_x_inverse(), maps[1]])
     got = swap(back, "row")
     back = call(
@@ -858,16 +868,8 @@
         [got, table_y_back(), np.ascontiguousarray(table_lanes().T)],
         [(table_z_back(), lambda: lax.axis_index("col") * 4 + own_group())],
         [pltpu.VMEM((512, 128), F32)],
-        far={0: 16},
     )
     got = swap(back, owner)
-    spectrum = call(
-        spectrum_kernel,
-        shape((4, 128, 1024), F32),
-        [lift_weight],
-        [(spread, None)],
-        [pltpu.VMEM((256, 1024), F32)],
-    )
     grad = call(
         grad_kernel,
         shape((2, 128, 16, 128), BF),

time: 118 us -> 117 us (level)
  blocking collectives: 11.9 us -> 29.5 us
  waiting for transfers between devices: 24.4 us -> 14 us
  starting transfers between devices: 52.7 us -> 45.4 us
    all_to_all x1 -> x2, blocking collectives: 11.9 us -> 29.5 us  [swap(): return lax.all_to_all(x, axes, 0, 0, tiled=True)]
    all_to_all x5 -> x4, waiting for transfers between devices: 22.2 us -> 10.7 us  [swap(): return lax.all_to_all(x, axes, 0, 0, tiled=True)]
    all_to_all x5 -> x4, starting transfers between devices: 36.2 us -> 28.8 us  [swap(): return lax.all_to_all(x, axes, 0, 0, tiled=True)]
  transfers between devices with their start and end apart: 12 -> 11, of which waited for: 5 -> 4; matrix products, arithmetic and copies ran while one was open for 2% -> 1% of each run, Pallas kernels for 13% -> 14%
where the time goes in v6:
time: 117 us; the launch traced here: 116 us
  starting transfers between devices  45.4 us (39%)
  blocking collectives  29.5 us (25%)
  Pallas kernels  24.8 us (21%)
  waiting for transfers between devices  14 us (12%)
  local copies, waits for them, and re-layouts  1.37 us (1%)
    all_to_all x2, blocking collectives, swap(): return lax.all_to_all(x, axes, 0, 0, tiled=True)  29.5 us
    all_to_all x4, starting transfers between devices, swap(): return lax.all_to_all(x, axes, 0, 0, tiled=True)  28.8 us
    pallas_call x13, Pallas kernels, call(): pl.pallas_call(kernel, out_shape=[pltpu.HBM(o.shape, o.dtype) if k in far...  24.8 us
    ppermute x7, starting transfers between devices, shift(): return lax.ppermute(x, axis, [(i, (i + step) % size) for i in range(size)])  16.6 us
    all_to_all x4, waiting for transfers between devices, swap(): return lax.all_to_all(x, axes, 0, 0, tiled=True)  10.7 us
    ppermute x7, waiting for transfers between devices, shift(): return lax.ppermute(x, axis, [(i, (i + step) % size) for i in range(size)])  3.31 us
  transfers between devices with their start and end apart: 11, of which 4 were waited for; matrix products, arithmetic and copies ran while one was open for 1% of the time, Pallas kernels for 14%

profile of v6, /device:TPU:1, one launch (start us, length us, event | category | flops | bytes accessed | tf_op | source)
XLA Modules:
  0.0 116.2 jit_solution(15442566905115691093)
XLA Ops:
  0.6 2.6 %shard_map.194 = (bf16[16,8,256]{2,1,0:T(8,128)(2,1)}, bf16[480,128]{1,0:T(8,128)(2,1)S(1)}, bf16[480,128]{1,0:T(8,128)(2,1)}, bf16[480,128]{1,0:T(8,128)(2,1)},...) custom-call(f32[5,384,128]{2,1,0:T(8,128)} %bitcast.7, ...), custom_call_target="tpu_custom_call" | custom-call | tf_op jit(solution)/shard_map/pallas_call | solution.py:275
  3.2 11.9 %all-to-all-start = ((bf16[16,8,256]{2,1,0:T(8,128)(2,1)}), bf16[16,8,256]{2,1,0:T(8,128)(2,1)S(1)}, u32[]{:S(2)}, u32[]{:S(2)}) async-start(bf16[16,8,256]{2,1,0:T(8,128)(2,1)} %get-tuple-element.42), calls=%async_computation | async-start | bytes 131072 | tf_op jit(solution)/shard_map/all_to_all | solution.py:763
  15.1 2.3 %collective-permute-start = (bf16[480,128]{1,0:T(8,128)(2,1)S(1)}, bf16[480,128]{1,0:T(8,128)(2,1)S(1)}, u32[]{:S(2)}, u32[]{:S(2)}) collective-permute-start(bf16[480,128]{1,0:T(8,128)(2,1)S(1)} %get-tuple-element.46), channel_id=1, source_target_pairs={{0,4},{4,8},{8,12},{12,16},{16,20},{20,24},{24,28},{28,32},{32,36}... | collective-permute-start | bytes 368648 | tf_op jit(solution)/shard_map/ppermute | solution.py:768
  17.4 3.5 %collective-permute-start.1 = (bf16[480,128]{1,0:T(8,128)(2,1)S(1)}, bf16[480,128]{1,0:T(8,128)(2,1)S(1)}, u32[]{:S(2)}, u32[]{:S(2)}) collective-permute-start(bf16[480,128]{1,0:T(8,128)(2,1)S(1)} %get-tuple-element.47), channel_id=1, source_target_pairs={{0,60},{4,0},{8,4},{12,8},{16,12},{20,16},{24,20},{28,24},{32,28},... | collective-permute-start | bytes 368648 | tf_op jit(solution)/shard_map/ppermute | solution.py:768
  22.2 2.1 %shard_map.196.refs_3_ = f32[2,256,256]{2,1,0:T(8,128)S(1)} custom-call(f32[32,5]{1,0:T(8,128)S(1)} %copy.21.refs_0_, bf16[2,256,1024]{2,1,0:T(8,128)(2,1)} %reshape.20.refs_1_), custom_call_target="tpu_custom_call" | custom-call | tf_op jit(solution)/shard_map/pallas_call | solution.py:275
  24.9 2.0 %collective-permute-done.1.refs_3_ = bf16[480,128]{1,0:T(8,128)(2,1)S(1)} collective-permute-done((bf16[480,128]{1,0:T(8,128)(2,1)S(1)}, bf16[480,128]{1,0:T(8,128)(2,1)S(1)}, u32[]{:S(2)}, u32[]{:S(2)}) %collective-permute-start.1) | collective-permute-done | bytes 122912 | tf_op jit(solution)/shard_map/ppermute | solution.py:768
  26.9 1.6 %shard_map.197 = (bf16[16,48,256]{2,1,0:T(8,128)(2,1)}, bf16[2,480,128]{2,1,0:T(8,128)(2,1)}) custom-call(bf16[16,16,256]{2,1,0:T(8,128)(2,1)S(1)} %get-tuple-element.44.refs_0_, f32[16,8,128]{2,1,0:T(8,128)S(1)} %get-tuple-element.45.refs_1_, bf16[480,128]{1,0:T(8,128)(2,1)S(1)} %collective-permute-done.refs_2_, ...), custom_call_target="tpu_custom_call" | custom-call | tf_op jit(solution)/shard_map/pallas_call | solution.py:275
  28.5 7.1 %all-to-all-start.1 = ((bf16[16,48,256]{2,1,0:T(8,128)(2,1)}), bf16[16,48,256]{2,1,0:T(8,128)(2,1)S(1)}, u32[]{:S(2)}, u32[]{:S(2)}) async-start(bf16[16,48,256]{2,1,0:T(8,128)(2,1)} %get-tuple-element.50), calls=%async_computation.1 | async-start | bytes 786432 | tf_op jit(solution)/shard_map/all_to_all | solution.py:763
  35.6 1.6 %collective-permute-start.2 = (bf16[480,128]{1,0:T(8,128)(2,1)}, bf16[480,128]{1,0:T(8,128)(2,1)}, u32[]{:S(2)}, u32[]{:S(2)}) collective-permute-start(bf16[480,128]{1,0:T(8,128)(2,1)} %get-tuple-element.57), channel_id=1, source_target_pairs={{0,4},{4,8},{8,12},{12,16},{16,20},{20,24},{24,28},{28,32},{32,36}... | collective-permute-start | bytes 368648 | tf_op jit(solution)/shard_map/ppermute | solution.py:768
  37.3 4.2 %collective-permute-start.3 = (bf16[480,128]{1,0:T(8,128)(2,1)}, bf16[480,128]{1,0:T(8,128)(2,1)}, u32[]{:S(2)}, u32[]{:S(2)}) collective-permute-start(bf16[480,128]{1,0:T(8,128)(2,1)} %get-tuple-element.58), channel_id=1, source_target_pairs={{0,60},{4,0},{8,4},{12,8},{16,12},{20,16},{24,20},{28,24},{32,28},... | collective-permute-start | bytes 368648 | tf_op jit(solution)/shard_map/ppermute | solution.py:768
  42.2 4.4 %all-to-all-done.1.refs_0_ = bf16[16,48,256]{2,1,0:T(8,128)(2,1)S(1)} async-done(((bf16[16,48,256]{2,1,0:T(8,128)(2,1)}), bf16[16,48,256]{2,1,0:T(8,128)(2,1)S(1)}, u32[]{:S(2)}, u32[]{:S(2)}) %all-to-all-start.1) | async-done | bytes 393248 | tf_op jit(solution)/shard_map/all_to_all | solution.py:763
  46.6 2.6 %shard_map.199 = (bf16[16,96,128]{2,1,0:T(8,128)(2,1)}, f32[2,2,256,128]{3,2,1,0:T(8,128)}, bf16[8,64,128]{2,1,0:T(8,128)(2,1)}) custom-call(bf16[16,48,256]{2,1,0:T(8,128)(2,1)S(1)} %all-to-all-done.1.refs_0_, bf16[128,256]{1,0:T(8,128)(2,1)S(1)} %copy-done.9, bf16[512,128]{1,0:T(8,128)(2,1)S(1)} %copy-done.6, f32[2,256,256]{2,1,0:T(8,128)S(1)} %shard_map.196.refs_3_, ...), custom_call_target="tpu_custom_call" | custom-call | tf_op jit(solution)/shard_map/pallas_call | solution.py:275
  49.2 1.3 %collective-permute-done.2.refs_5_ = bf16[480,128]{1,0:T(8,128)(2,1)} collective-permute-done((bf16[480,128]{1,0:T(8,128)(2,1)}, bf16[480,128]{1,0:T(8,128)(2,1)}, u32[]{:S(2)}, u32[]{:S(2)}) %collective-permute-start.2) | collective-permute-done | bytes 122912 | tf_op jit(solution)/shard_map/ppermute | solution.py:768
  50.5 5.0 %all-to-all-start.2 = ((bf16[16,96,128]{2,1,0:T(8,128)(2,1)}), bf16[16,96,128]{2,1,0:T(8,128)(2,1)S(1)}, u32[]{:S(2)}, u32[]{:S(2)}) async-start(bf16[16,96,128]{2,1,0:T(8,128)(2,1)} %get-tuple-element.63), calls=%async_computation.2 | async-start | bytes 786432 | tf_op jit(solution)/shard_map/all_to_all | solution.py:763
  55.6 5.6 %shard_map.200 = (f32[5,384,128]{2,1,0:T(8,128)}, bf16[128,128]{1,0:T(8,128)(2,1)S(1)}, bf16[128,128]{1,0:T(8,128)(2,1)}, bf16[128,128]{1,0:T(8,128)(2,1)}, bf16[128,128]{1,0:T(8,128)(2,1)}) custom-call(bf16[64,128]{1,0:T(8,128)(2,1)S(1)} %get-tuple-element.40.refs_6_.refs_0_, bf16[64,128]{1,0:T(8,128)(2,1)S(1)} %get-tuple-element.41.refs_7_.refs_1_, ...), custom_call_target="tpu_custom_call" | custom-call | tf_op jit(solution)/shard_map/pallas_call | solution.py:275
  61.2 1.5 %collective-permute-start.4 = (bf16[128,128]{1,0:T(8,128)(2,1)}, bf16[128,128]{1,0:T(8,128)(2,1)S(1)}, u32[]{:S(2)}, u32[]{:S(2)}) collective-permute-start(bf16[128,128]{1,0:T(8,128)(2,1)} %get-tuple-element.64), channel_id=1, source_target_pairs={{0,64},{64,128},{128,192},{192,0},{1,65},{65,129},{129,193},{193,1... | collective-permute-start | bytes 98312 | tf_op jit(solution)/shard_map/ppermute | solution.py:768
  62.7 2.4 %collective-permute-start.5 = (bf16[128,128]{1,0:T(8,128)(2,1)}, bf16[128,128]{1,0:T(8,128)(2,1)S(1)}, u32[]{:S(2)}, u32[]{:S(2)}) collective-permute-start(bf16[128,128]{1,0:T(8,128)(2,1)} %get-tuple-element.65), channel_id=1, source_target_pairs={{0,128},{64,192},{128,0},{192,64},{1,129},{65,193},{129,1},{193,65... | collective-permute-start | bytes 98312 | tf_op jit(solution)/shard_map/ppermute | solution.py:768
  67.5 4.8 %all-to-all-start.3 = ((bf16[16,8,384]{2,1,0:T(8,128)(2,1)}), bf16[16,8,384]{2,1,0:T(8,128)(2,1)S(1)}, u32[]{:S(2)}, u32[]{:S(2)}) async-start(bf16[16,8,384]{2,1,0:T(8,128)(2,1)} %shard_map.201), calls=%async_computation.3 | async-start | bytes 196608 | tf_op jit(solution)/shard_map/all_to_all | solution.py:763
  72.7 2.9 %shard_map.203.refs_2_ = f32[4,128,1024]{2,1,0:T(8,128)} custom-call(f32[32,5]{1,0:T(8,128)S(1)} %copy.21.refs_0_, f32[2,2,256,128]{3,2,1,0:T(8,128)} %get-tuple-element.72.refs_1_), custom_call_target="tpu_custom_call" | custom-call | tf_op jit(solution)/shard_map/pallas_call | solution.py:275
  75.6 6.3 %all-to-all-done.3.refs_0_ = bf16[16,8,384]{2,1,0:T(8,128)(2,1)S(1)} async-done(((bf16[16,8,384]{2,1,0:T(8,128)(2,1)}), bf16[16,8,384]{2,1,0:T(8,128)(2,1)S(1)}, u32[]{:S(2)}, u32[]{:S(2)}) %all-to-all-start.3) | async-done | bytes 98336 | tf_op jit(solution)/shard_map/all_to_all | solution.py:763
  81.9 1.5 %shard_map.204 = bf16[16,8,384]{2,1,0:T(8,128)(2,1)S(1)} custom-call(bf16[16,8,384]{2,1,0:T(8,128)(2,1)S(1)} %all-to-all-done.3.refs_0_, f32[384,384]{1,0:T(8,128)S(1)} %get-tuple-element.74.refs_1_, f32[384,128]{1,0:T(8,128)S(1)} %get-tuple-element.75.refs_2_, bf16[2,384,128]{2,1,0:T(8,128)(2,1)S(1)} %copy-done.5, ...), custom_call_target="tpu_custom_call" | custom-call | tf_op jit(solution)/shard_map/pallas_call | solution.py:275
  83.4 12.2 %all_to_all.30.refs_0_ = bf16[16,8,384]{2,1,0:T(8,128)(2,1)S(1)} all-to-all(bf16[16,8,384]{2,1,0:T(8,128)(2,1)S(1)} %shard_map.204), channel_id=1, replica_groups=mesh['grp'=4,'row'=16,'col'=4] {'row'}, dimensions={0} | all-to-all | bytes 196608 | tf_op jit(solution)/shard_map/all_to_all | solution.py:763
  96.7 17.3 %all_to_all.31.refs_0_ = bf16[16,16,1152]{2,1,0:T(8,128)(2,1)S(1)} all-to-all(bf16[16,16,1152]{2,1,0:T(8,128)(2,1)S(1)} %shard_map.205), channel_id=1, replica_groups=mesh['grp'=4,'row'=16,'col'=4] {'grp','col'}, dimensions={0} | all-to-all | bytes 1179648 | tf_op jit(solution)/shard_map/all_to_all | solution.py:763
  114.1 1.9 %shard_map.206 = bf16[2,128,16,128]{3,2,1,0:T(8,128)(2,1)} custom-call(bf16[16,16,1152]{2,1,0:T(8,128)(2,1)S(1)} %all_to_all.31.refs_0_, bf16[256,256]{1,0:T(8,128)(2,1)S(1)} %copy-done.7, f32[4,128,1024]{2,1,0:T(8,128)S(1)} %copy-done.1), custom_call_target="tpu_custom_call" | custom-call | tf_op jit(solution)/shard_map/pallas_call | solution.py:275
  (47 shorter events, 6.6 us)
Async XLA Ops:
  0.6 20.3 %copy-start.15 = (f32[32,5]{0,1:T(8,128)S(1)}, f32[32,5]{0,1:T(8,128)}, u32[]{:S(2)}) copy-start(f32[32,5]{0,1:T(8,128)} %param.20) | copy-start | bytes 1924
  0.6 20.4 %copy-start.14 = (bf16[2,16,8,2,1024]{4,3,2,1,0:T(2,128)(2,1)S(1)}, bf16[2,16,8,2,1024]{4,3,2,1,0:T(2,128)(2,1)}, u32[]{:S(2)}) copy-start(bf16[2,16,8,2,1024]{4,3,2,1,0:T(2,128)(2,1)} %param.23) | copy-start | bytes 3145732
  3.2 21.1 %copy-start.3 = (bf16[2,2,256,512]{3,2,1,0:T(8,128)(2,1)S(1)}, bf16[2,2,256,512]{3,2,1,0:T(8,128)(2,1)}, u32[]{:S(2)}) copy-start(bf16[2,2,256,512]{3,2,1,0:T(8,128)(2,1)} %constant.28.clone.refs_2_) | copy-start | bytes 3145732
  3.2 21.1 %copy-start.10 = (bf16[2,128,128]{2,1,0:T(8,128)(2,1)S(1)}, bf16[2,128,128]{2,1,0:T(8,128)(2,1)}, u32[]{:S(2)}) copy-start(bf16[2,128,128]{2,1,0:T(8,128)(2,1)} %constant.27.clone.refs_1_) | copy-start | bytes 196612
  3.2 21.1 %all-to-all-start = ((bf16[16,8,256]{2,1,0:T(8,128)(2,1)}), bf16[16,8,256]{2,1,0:T(8,128)(2,1)S(1)}, u32[]{:S(2)}, u32[]{:S(2)}) async-start(bf16[16,8,256]{2,1,0:T(8,128)(2,1)} %get-tuple-element.42), calls=%async_computation | async-start | bytes 131072 | tf_op jit(solution)/shard_map/all_to_all | solution.py:763
  15.1 9.8 %collective-permute-start = (bf16[480,128]{1,0:T(8,128)(2,1)S(1)}, bf16[480,128]{1,0:T(8,128)(2,1)S(1)}, u32[]{:S(2)}, u32[]{:S(2)}) collective-permute-start(bf16[480,128]{1,0:T(8,128)(2,1)S(1)} %get-tuple-element.46), channel_id=1, source_target_pairs={{0,4},{4,8},{8,12},{12,16},{16,20},{20,24},{24,28},{28,32},{32,36}... | collective-permute-start | bytes 368648 | tf_op jit(solution)/shard_map/ppermute | solution.py:768
  17.4 9.5 %collective-permute-start.1 = (bf16[480,128]{1,0:T(8,128)(2,1)S(1)}, bf16[480,128]{1,0:T(8,128)(2,1)S(1)}, u32[]{:S(2)}, u32[]{:S(2)}) collective-permute-start(bf16[480,128]{1,0:T(8,128)(2,1)S(1)} %get-tuple-element.47), channel_id=1, source_target_pairs={{0,60},{4,0},{8,4},{12,8},{16,12},{20,16},{24,20},{28,24},{32,28},... | collective-permute-start | bytes 368648 | tf_op jit(solution)/shard_map/ppermute | solution.py:768
  22.2 24.4 %copy-start.6 = (bf16[512,128]{1,0:T(8,128)(2,1)S(1)}, bf16[512,128]{1,0:T(8,128)(2,1)}, u32[]{:S(2)}) copy-start(bf16[512,128]{1,0:T(8,128)(2,1)} %constant.31.clone.refs_2_) | copy-start | bytes 393220
  22.2 24.4 %copy-start.9 = (bf16[128,256]{1,0:T(8,128)(2,1)S(1)}, bf16[128,256]{1,0:T(8,128)(2,1)}, u32[]{:S(2)}) copy-start(bf16[128,256]{1,0:T(8,128)(2,1)} %constant.30.clone.refs_1_) | copy-start | bytes 196612
  24.9 30.7 %copy-start = (f32[5,96,4,128]{3,2,1,0:T(4,128)S(1)}, f32[5,96,4,128]{3,2,1,0:T(4,128)}, u32[]{:S(2)}) copy-start(f32[5,96,4,128]{3,2,1,0:T(4,128)} %param.19) | copy-start | bytes 2949124
  24.9 30.7 %copy-start.11 = (bf16[128,256]{1,0:T(8,128)(2,1)S(1)}, bf16[128,256]{1,0:T(8,128)(2,1)}, u32[]{:S(2)}) copy-start(bf16[128,256]{1,0:T(8,128)(2,1)} %constant.32.clone.refs_2_) | copy-start | bytes 196612
  28.5 18.1 %all-to-all-start.1 = ((bf16[16,48,256]{2,1,0:T(8,128)(2,1)}), bf16[16,48,256]{2,1,0:T(8,128)(2,1)S(1)}, u32[]{:S(2)}, u32[]{:S(2)}) async-start(bf16[16,48,256]{2,1,0:T(8,128)(2,1)} %get-tuple-element.50), calls=%async_computation.1 | async-start | bytes 786432 | tf_op jit(solution)/shard_map/all_to_all | solution.py:763
  35.6 30.6 %copy-start.2 = (bf16[512,512]{1,0:T(8,128)(2,1)S(1)}, bf16[512,512]{1,0:T(8,128)(2,1)}, u32[]{:S(2)}) copy-start(bf16[512,512]{1,0:T(8,128)(2,1)} %constant.33.clone.refs_1_.refs_2_) | copy-start | bytes 1572868
  35.6 30.6 %copy-start.4 = (bf16[2,128,512]{2,1,0:T(8,128)(2,1)S(1)}, bf16[2,128,512]{2,1,0:T(8,128)(2,1)}, u32[]{:S(2)}) copy-start(bf16[2,128,512]{2,1,0:T(8,128)(2,1)} %constant.34.clone.refs_2_) | copy-start | bytes 786436
  35.6 14.9 %collective-permute-start.2 = (bf16[480,128]{1,0:T(8,128)(2,1)}, bf16[480,128]{1,0:T(8,128)(2,1)}, u32[]{:S(2)}, u32[]{:S(2)}) collective-permute-start(bf16[480,128]{1,0:T(8,128)(2,1)} %get-tuple-element.57), channel_id=1, source_target_pairs={{0,4},{4,8},{8,12},{12,16},{16,20},{20,24},{24,28},{28,32},{32,36}... | collective-permute-start | bytes 368648 | tf_op jit(solution)/shard_map/ppermute | solution.py:768
  37.3 13.3 %collective-permute-start.3 = (bf16[480,128]{1,0:T(8,128)(2,1)}, bf16[480,128]{1,0:T(8,128)(2,1)}, u32[]{:S(2)}, u32[]{:S(2)}) collective-permute-start(bf16[480,128]{1,0:T(8,128)(2,1)} %get-tuple-element.58), channel_id=1, source_target_pairs={{0,60},{4,0},{8,4},{12,8},{16,12},{20,16},{24,20},{28,24},{32,28},... | collective-permute-start | bytes 368648 | tf_op jit(solution)/shard_map/ppermute | solution.py:768
  50.5 15.7 %all-to-all-start.2 = ((bf16[16,96,128]{2,1,0:T(8,128)(2,1)}), bf16[16,96,128]{2,1,0:T(8,128)(2,1)S(1)}, u32[]{:S(2)}, u32[]{:S(2)}) async-start(bf16[16,96,128]{2,1,0:T(8,128)(2,1)} %get-tuple-element.63), calls=%async_computation.2 | async-start | bytes 786432 | tf_op jit(solution)/shard_map/all_to_all | solution.py:763
  61.2 11.1 %collective-permute-start.4 = (bf16[128,128]{1,0:T(8,128)(2,1)}, bf16[128,128]{1,0:T(8,128)(2,1)S(1)}, u32[]{:S(2)}, u32[]{:S(2)}) collective-permute-start(bf16[128,128]{1,0:T(8,128)(2,1)} %get-tuple-element.64), channel_id=1, source_target_pairs={{0,64},{64,128},{128,192},{192,0},{1,65},{65,129},{129,193},{193,1... | collective-permute-start | bytes 98312 | tf_op jit(solution)/shard_map/ppermute | solution.py:768
  62.7 9.6 %collective-permute-start.5 = (bf16[128,128]{1,0:T(8,128)(2,1)}, bf16[128,128]{1,0:T(8,128)(2,1)S(1)}, u32[]{:S(2)}, u32[]{:S(2)}) collective-permute-start(bf16[128,128]{1,0:T(8,128)(2,1)} %get-tuple-element.65), channel_id=1, source_target_pairs={{0,128},{64,192},{128,0},{192,64},{1,129},{65,193},{129,1},{193,65... | collective-permute-start | bytes 98312 | tf_op jit(solution)/shard_map/ppermute | solution.py:768
  65.0 7.3 %collective-permute-start.6 = (bf16[128,128]{1,0:T(8,128)(2,1)}, bf16[128,128]{1,0:T(8,128)(2,1)S(1)}, u32[]{:S(2)}, u32[]{:S(2)}) collective-permute-start(bf16[128,128]{1,0:T(8,128)(2,1)} %get-tuple-element.66), channel_id=1, source_target_pairs={{0,192},{64,0},{128,64},{192,128},{1,193},{65,1},{129,65},{193,129... | collective-permute-start | bytes 98312 | tf_op jit(solution)/shard_map/ppermute | solution.py:768
  67.5 14.3 %all-to-all-start.3 = ((bf16[16,8,384]{2,1,0:T(8,128)(2,1)}), bf16[16,8,384]{2,1,0:T(8,128)(2,1)S(1)}, u32[]{:S(2)}, u32[]{:S(2)}) async-start(bf16[16,8,384]{2,1,0:T(8,128)(2,1)} %shard_map.201), calls=%async_computation.3 | async-start | bytes 196608 | tf_op jit(solution)/shard_map/all_to_all | solution.py:763
  72.7 22.9 %copy-start.8 = (bf16[2,128,128]{2,1,0:T(8,128)(2,1)S(1)}, bf16[2,128,128]{2,1,0:T(8,128)(2,1)}, u32[]{:S(2)}) copy-start(bf16[2,128,128]{2,1,0:T(8,128)(2,1)} %constant.37.clone.refs_1_) | copy-start | bytes 196612
  81.9 32.2 %copy-start.1 = (f32[4,128,1024]{2,1,0:T(8,128)S(1)}, f32[4,128,1024]{2,1,0:T(8,128)}, u32[]{:S(2)}) copy-start(f32[4,128,1024]{2,1,0:T(8,128)} %shard_map.203.refs_2_) | copy-start | bytes 6291460
  81.9 32.2 %copy-start.7 = (bf16[256,256]{1,0:T(8,128)(2,1)S(1)}, bf16[256,256]{1,0:T(8,128)(2,1)}, u32[]{:S(2)}) copy-start(bf16[256,256]{1,0:T(8,128)(2,1)} %constant.38.clone.refs_1_) | copy-start | bytes 393220
  (3 other events, 47.7 us)

commit v7 on v6

--- a/solution.py
+++ b/solution.py
@@ -822,7 +822,6 @@
         [pltpu.VMEM((1536, 128), F32)],
         far={1: 1, 2: 1},
     )
-    modes, below2, above2 = tied(modes, below2, above2)
     got = swap(modes, owner)
     new_fields, *snaps = call(
         steps_kernel,
@@ -837,6 +836,7 @@
             pltpu.VMEM((512, 256), F32),
         ],
         far={0: F, 2: 1, 3: 1, 4: 1},
+        flops=60_000_000_000,
     )
     got, _ = tied(got, snaps[1:])
     planes = call(inverse_y_kernel, shape((16, 8, 384), BF), [got, table_lanes(), table_y_inverse()])

time: 117 us -> 117 us (level)
  waiting for transfers between devices: 14 us -> 12.8 us
    ppermute x7, waiting for transfers between devices: 3.31 us -> 2.05 us  [shift(): return lax.ppermute(x, axis, [(i, (i + step) % size) for i in range(size)])]
  transfers between devices with their start and end apart: 11 -> 11, of which waited for: 4 -> 3; matrix products, arithmetic and copies ran while one was open for 1% -> 1% of each run, Pallas kernels for 14% -> 14%
where the time goes in v7:
time: 117 us; the launch traced here: 116 us
  starting transfers between devices  46.1 us (39%)
  blocking collectives  29.5 us (25%)
  Pallas kernels  24.8 us (21%)
  waiting for transfers between devices  12.8 us (11%)
  local copies, waits for them, and re-layouts  2.02 us (2%)
    all_to_all x2, blocking collectives, swap(): return lax.all_to_all(x, axes, 0, 0, tiled=True)  29.5 us
    all_to_all x4, starting transfers between devices, swap(): return lax.all_to_all(x, axes, 0, 0, tiled=True)  29.5 us
    pallas_call x13, Pallas kernels, call(): pl.pallas_call(kernel, out_shape=[pltpu.HBM(o.shape, o.dtype) if k in far...  24.8 us
    ppermute x7, starting transfers between devices, shift(): return lax.ppermute(x, axis, [(i, (i + step) % size) for i in range(size)])  16.5 us
    all_to_all x4, waiting for transfers between devices, swap(): return lax.all_to_all(x, axes, 0, 0, tiled=True)  10.8 us
  transfers between devices with their start and end apart: 11, of which 3 were waited for; matrix products, arithmetic and copies ran while one was open for 1% of the time, Pallas kernels for 14%

profile of v7, /device:TPU:1, one launch (start us, length us, event | category | flops | bytes accessed | tf_op | source)
XLA Modules:
  0.0 116.3 jit_solution(11076205772730500134)
XLA Ops:
  0.6 2.5 %shard_map.194 = (bf16[16,8,256]{2,1,0:T(8,128)(2,1)}, bf16[480,128]{1,0:T(8,128)(2,1)S(1)}, bf16[480,128]{1,0:T(8,128)(2,1)S(1)}, bf16[480,128]{1,0:T(8,128)(2,...) custom-call(f32[5,384,128]{2,1,0:T(8,128)} %bitcast.7, ...), custom_call_target="tpu_custom_call" | custom-call | tf_op jit(solution)/shard_map/pallas_call | solution.py:275
  3.1 11.9 %all-to-all-start = ((bf16[16,8,256]{2,1,0:T(8,128)(2,1)}), bf16[16,8,256]{2,1,0:T(8,128)(2,1)S(1)}, u32[]{:S(2)}, u32[]{:S(2)}) async-start(bf16[16,8,256]{2,1,0:T(8,128)(2,1)} %get-tuple-element.39), calls=%async_computation | async-start | bytes 131072 | tf_op jit(solution)/shard_map/all_to_all | solution.py:763
  15.0 2.3 %collective-permute-start = (bf16[480,128]{1,0:T(8,128)(2,1)}, bf16[480,128]{1,0:T(8,128)(2,1)S(1)}, u32[]{:S(2)}, u32[]{:S(2)}) collective-permute-start(bf16[480,128]{1,0:T(8,128)(2,1)} %get-tuple-element.43), channel_id=1, source_target_pairs={{0,4},{4,8},{8,12},{12,16},{16,20},{20,24},{24,28},{28,32},{32,36}... | collective-permute-start | bytes 368648 | tf_op jit(solution)/shard_map/ppermute | solution.py:768
  17.3 3.5 %collective-permute-start.1 = (bf16[480,128]{1,0:T(8,128)(2,1)S(1)}, bf16[480,128]{1,0:T(8,128)(2,1)S(1)}, u32[]{:S(2)}, u32[]{:S(2)}) collective-permute-start(bf16[480,128]{1,0:T(8,128)(2,1)S(1)} %get-tuple-element.44), channel_id=1, source_target_pairs={{0,60},{4,0},{8,4},{12,8},{16,12},{20,16},{24,20},{28,24},{32,28},... | collective-permute-start | bytes 368648 | tf_op jit(solution)/shard_map/ppermute | solution.py:768
  22.1 2.1 %shard_map.196.refs_3_ = f32[2,256,256]{2,1,0:T(8,128)S(1)} custom-call(f32[32,5]{1,0:T(8,128)S(1)} %copy.21.refs_0_, bf16[2,256,1024]{2,1,0:T(8,128)(2,1)} %reshape.20.refs_1_), custom_call_target="tpu_custom_call" | custom-call | tf_op jit(solution)/shard_map/pallas_call | solution.py:275
  24.8 2.0 %collective-permute-done.1.refs_3_ = bf16[480,128]{1,0:T(8,128)(2,1)S(1)} collective-permute-done((bf16[480,128]{1,0:T(8,128)(2,1)S(1)}, bf16[480,128]{1,0:T(8,128)(2,1)S(1)}, u32[]{:S(2)}, u32[]{:S(2)}) %collective-permute-start.1) | collective-permute-done | bytes 122912 | tf_op jit(solution)/shard_map/ppermute | solution.py:768
  26.8 1.6 %shard_map.197 = (bf16[16,48,256]{2,1,0:T(8,128)(2,1)}, bf16[2,480,128]{2,1,0:T(8,128)(2,1)}) custom-call(bf16[16,16,256]{2,1,0:T(8,128)(2,1)S(1)} %get-tuple-element.41.refs_0_, f32[16,8,128]{2,1,0:T(8,128)S(1)} %get-tuple-element.42.refs_1_, bf16[480,128]{1,0:T(8,128)(2,1)S(1)} %collective-permute-done.refs_2_, ...), custom_call_target="tpu_custom_call" | custom-call | tf_op jit(solution)/shard_map/pallas_call | solution.py:275
  28.4 7.1 %all-to-all-start.1 = ((bf16[16,48,256]{2,1,0:T(8,128)(2,1)}), bf16[16,48,256]{2,1,0:T(8,128)(2,1)S(1)}, u32[]{:S(2)}, u32[]{:S(2)}) async-start(bf16[16,48,256]{2,1,0:T(8,128)(2,1)} %get-tuple-element.47), calls=%async_computation.1 | async-start | bytes 786432 | tf_op jit(solution)/shard_map/all_to_all | solution.py:763
  35.5 1.5 %collective-permute-start.2 = (bf16[480,128]{1,0:T(8,128)(2,1)S(1)}, bf16[480,128]{1,0:T(8,128)(2,1)S(1)}, u32[]{:S(2)}, u32[]{:S(2)}) collective-permute-start(bf16[480,128]{1,0:T(8,128)(2,1)S(1)} %get-tuple-element.53), channel_id=1, source_target_pairs={{0,4},{4,8},{8,12},{12,16},{16,20},{20,24},{24,28},{28,32},{32,36}... | collective-permute-start | bytes 368648 | tf_op jit(solution)/shard_map/ppermute | solution.py:768
  37.1 4.2 %collective-permute-start.3 = (bf16[480,128]{1,0:T(8,128)(2,1)S(1)}, bf16[480,128]{1,0:T(8,128)(2,1)S(1)}, u32[]{:S(2)}, u32[]{:S(2)}) collective-permute-start(bf16[480,128]{1,0:T(8,128)(2,1)S(1)} %get-tuple-element.55), channel_id=1, source_target_pairs={{0,60},{4,0},{8,4},{12,8},{16,12},{20,16},{24,20},{28,24},{32,28},... | collective-permute-start | bytes 368648 | tf_op jit(solution)/shard_map/ppermute | solution.py:768
  42.0 4.5 %all-to-all-done.1.refs_0_ = bf16[16,48,256]{2,1,0:T(8,128)(2,1)S(1)} async-done(((bf16[16,48,256]{2,1,0:T(8,128)(2,1)}), bf16[16,48,256]{2,1,0:T(8,128)(2,1)S(1)}, u32[]{:S(2)}, u32[]{:S(2)}) %all-to-all-start.1) | async-done | bytes 393248 | tf_op jit(solution)/shard_map/all_to_all | solution.py:763
  46.6 2.6 %shard_map.199 = (bf16[16,96,128]{2,1,0:T(8,128)(2,1)}, f32[2,2,256,128]{3,2,1,0:T(8,128)}, bf16[8,64,128]{2,1,0:T(8,128)(2,1)}) custom-call(bf16[16,48,256]{2,1,0:T(8,128)(2,1)S(1)} %all-to-all-done.1.refs_0_, bf16[128,256]{1,0:T(8,128)(2,1)S(1)} %copy-done.9, bf16[512,128]{1,0:T(8,128)(2,1)S(1)} %copy-done.6, f32[2,256,256]{2,1,0:T(8,128)S(1)} %shard_map.196.refs_3_, ...), custom_call_target="tpu_custom_call" | custom-call | tf_op jit(solution)/shard_map/pallas_call | solution.py:275
  49.2 5.0 %all-to-all-start.2 = ((bf16[16,96,128]{2,1,0:T(8,128)(2,1)}), bf16[16,96,128]{2,1,0:T(8,128)(2,1)S(1)}, u32[]{:S(2)}, u32[]{:S(2)}) async-start(bf16[16,96,128]{2,1,0:T(8,128)(2,1)} %get-tuple-element.57), calls=%async_computation.2 | async-start | bytes 786432 | tf_op jit(solution)/shard_map/all_to_all | solution.py:763
  54.9 5.7 %shard_map.200 = (f32[5,384,128]{2,1,0:T(8,128)}, bf16[128,128]{1,0:T(8,128)(2,1)S(1)}, bf16[128,128]{1,0:T(8,128)(2,1)}, bf16[128,128]{1,0:T(8,128)(2,1)}, bf16[128,128]{1,0:T(8,128)(2,1)}) custom-call(bf16[64,128]{1,0:T(8,128)(2,1)S(1)} %get-tuple-element.37.refs_6_.refs_0_, bf16[64,128]{1,0:T(8,128)(2,1)S(1)} %get-tuple-element.38.refs_7_.refs_1_, ...), custom_call_target="tpu_custom_call" | custom-call | flops 60000002048 | tf_op jit(solution)/shard_map/pallas_call | solution.py:275
  60.5 1.5 %collective-permute-start.4 = (bf16[128,128]{1,0:T(8,128)(2,1)}, bf16[128,128]{1,0:T(8,128)(2,1)S(1)}, u32[]{:S(2)}, u32[]{:S(2)}) collective-permute-start(bf16[128,128]{1,0:T(8,128)(2,1)} %get-tuple-element.58), channel_id=1, source_target_pairs={{0,64},{64,128},{128,192},{192,0},{1,65},{65,129},{129,193},{193,1... | collective-permute-start | bytes 98312 | tf_op jit(solution)/shard_map/ppermute | solution.py:768
  62.0 2.5 %collective-permute-start.5 = (bf16[128,128]{1,0:T(8,128)(2,1)}, bf16[128,128]{1,0:T(8,128)(2,1)S(1)}, u32[]{:S(2)}, u32[]{:S(2)}) collective-permute-start(bf16[128,128]{1,0:T(8,128)(2,1)} %get-tuple-element.59), channel_id=1, source_target_pairs={{0,128},{64,192},{128,0},{192,64},{1,129},{65,193},{129,1},{193,65... | collective-permute-start | bytes 98312 | tf_op jit(solution)/shard_map/ppermute | solution.py:768
  65.6 1.3 %shard_map.201 = bf16[16,8,384]{2,1,0:T(8,128)(2,1)} custom-call(bf16[16,96,128]{2,1,0:T(8,128)(2,1)S(1)} %all-to-all-done.2.refs_0_, bf16[512,512]{1,0:T(8,128)(2,1)S(1)} %copy-done.2, bf16[2,128,512]{2,1,0:T(8,128)(2,1)S(1)} %copy-done.4), custom_call_target="tpu_custom_call" | custom-call | tf_op jit(solution)/shard_map/pallas_call | solution.py:275
  66.9 5.5 %all-to-all-start.3 = ((bf16[16,8,384]{2,1,0:T(8,128)(2,1)}), bf16[16,8,384]{2,1,0:T(8,128)(2,1)S(1)}, u32[]{:S(2)}, u32[]{:S(2)}) async-start(bf16[16,8,384]{2,1,0:T(8,128)(2,1)} %shard_map.201), calls=%async_computation.3 | async-start | bytes 196608 | tf_op jit(solution)/shard_map/all_to_all | solution.py:763
  72.8 2.9 %shard_map.203.refs_2_ = f32[4,128,1024]{2,1,0:T(8,128)} custom-call(f32[32,5]{1,0:T(8,128)S(1)} %copy.21.refs_0_, f32[2,2,256,128]{3,2,1,0:T(8,128)} %get-tuple-element.66.refs_1_), custom_call_target="tpu_custom_call" | custom-call | tf_op jit(solution)/shard_map/pallas_call | solution.py:275
  75.7 6.2 %all-to-all-done.3.refs_0_ = bf16[16,8,384]{2,1,0:T(8,128)(2,1)S(1)} async-done(((bf16[16,8,384]{2,1,0:T(8,128)(2,1)}), bf16[16,8,384]{2,1,0:T(8,128)(2,1)S(1)}, u32[]{:S(2)}, u32[]{:S(2)}) %all-to-all-start.3) | async-done | bytes 98336 | tf_op jit(solution)/shard_map/all_to_all | solution.py:763
  82.0 1.5 %shard_map.204 = bf16[16,8,384]{2,1,0:T(8,128)(2,1)S(1)} custom-call(bf16[16,8,384]{2,1,0:T(8,128)(2,1)S(1)} %all-to-all-done.3.refs_0_, f32[384,384]{1,0:T(8,128)S(1)} %get-tuple-element.68.refs_1_, f32[384,128]{1,0:T(8,128)S(1)} %get-tuple-element.69.refs_2_, bf16[2,384,128]{2,1,0:T(8,128)(2,1)S(1)} %copy-done.5, ...), custom_call_target="tpu_custom_call" | custom-call | tf_op jit(solution)/shard_map/pallas_call | solution.py:275
  83.5 12.2 %all_to_all.30.refs_0_ = bf16[16,8,384]{2,1,0:T(8,128)(2,1)S(1)} all-to-all(bf16[16,8,384]{2,1,0:T(8,128)(2,1)S(1)} %shard_map.204), channel_id=1, replica_groups=mesh['grp'=4,'row'=16,'col'=4] {'row'}, dimensions={0} | all-to-all | bytes 196608 | tf_op jit(solution)/shard_map/all_to_all | solution.py:763
  96.9 17.3 %all_to_all.31.refs_0_ = bf16[16,16,1152]{2,1,0:T(8,128)(2,1)S(1)} all-to-all(bf16[16,16,1152]{2,1,0:T(8,128)(2,1)S(1)} %shard_map.205), channel_id=1, replica_groups=mesh['grp'=4,'row'=16,'col'=4] {'grp','col'}, dimensions={0} | all-to-all | bytes 1179648 | tf_op jit(solution)/shard_map/all_to_all | solution.py:763
  114.2 1.9 %shard_map.206 = bf16[2,128,16,128]{3,2,1,0:T(8,128)(2,1)} custom-call(bf16[16,16,1152]{2,1,0:T(8,128)(2,1)S(1)} %all_to_all.31.refs_0_, bf16[256,256]{1,0:T(8,128)(2,1)S(1)} %copy-done.7, f32[4,128,1024]{2,1,0:T(8,128)S(1)} %copy-done.1), custom_call_target="tpu_custom_call" | custom-call | tf_op jit(solution)/shard_map/pallas_call | solution.py:275
  (51 shorter events, 6.0 us)
Async XLA Ops:
  0.6 20.2 %copy-start.15 = (f32[32,5]{0,1:T(8,128)S(1)}, f32[32,5]{0,1:T(8,128)}, u32[]{:S(2)}) copy-start(f32[32,5]{0,1:T(8,128)} %param.20) | copy-start | bytes 1924
  0.6 20.3 %copy-start.14 = (bf16[2,16,8,2,1024]{4,3,2,1,0:T(2,128)(2,1)S(1)}, bf16[2,16,8,2,1024]{4,3,2,1,0:T(2,128)(2,1)}, u32[]{:S(2)}) copy-start(bf16[2,16,8,2,1024]{4,3,2,1,0:T(2,128)(2,1)} %param.23) | copy-start | bytes 3145732
  3.1 21.1 %copy-start.3 = (bf16[2,2,256,512]{3,2,1,0:T(8,128)(2,1)S(1)}, bf16[2,2,256,512]{3,2,1,0:T(8,128)(2,1)}, u32[]{:S(2)}) copy-start(bf16[2,2,256,512]{3,2,1,0:T(8,128)(2,1)} %constant.28.clone.refs_2_) | copy-start | bytes 3145732
  3.1 21.1 %copy-start.10 = (bf16[2,128,128]{2,1,0:T(8,128)(2,1)S(1)}, bf16[2,128,128]{2,1,0:T(8,128)(2,1)}, u32[]{:S(2)}) copy-start(bf16[2,128,128]{2,1,0:T(8,128)(2,1)} %constant.27.clone.refs_1_) | copy-start | bytes 196612
  3.1 21.1 %all-to-all-start = ((bf16[16,8,256]{2,1,0:T(8,128)(2,1)}), bf16[16,8,256]{2,1,0:T(8,128)(2,1)S(1)}, u32[]{:S(2)}, u32[]{:S(2)}) async-start(bf16[16,8,256]{2,1,0:T(8,128)(2,1)} %get-tuple-element.39), calls=%async_computation | async-start | bytes 131072 | tf_op jit(solution)/shard_map/all_to_all | solution.py:763
  15.0 9.8 %collective-permute-start = (bf16[480,128]{1,0:T(8,128)(2,1)}, bf16[480,128]{1,0:T(8,128)(2,1)S(1)}, u32[]{:S(2)}, u32[]{:S(2)}) collective-permute-start(bf16[480,128]{1,0:T(8,128)(2,1)} %get-tuple-element.43), channel_id=1, source_target_pairs={{0,4},{4,8},{8,12},{12,16},{16,20},{20,24},{24,28},{28,32},{32,36}... | collective-permute-start | bytes 368648 | tf_op jit(solution)/shard_map/ppermute | solution.py:768
  17.3 9.5 %collective-permute-start.1 = (bf16[480,128]{1,0:T(8,128)(2,1)S(1)}, bf16[480,128]{1,0:T(8,128)(2,1)S(1)}, u32[]{:S(2)}, u32[]{:S(2)}) collective-permute-start(bf16[480,128]{1,0:T(8,128)(2,1)S(1)} %get-tuple-element.44), channel_id=1, source_target_pairs={{0,60},{4,0},{8,4},{12,8},{16,12},{20,16},{24,20},{28,24},{32,28},... | collective-permute-start | bytes 368648 | tf_op jit(solution)/shard_map/ppermute | solution.py:768
  22.1 19.1 %copy-start.11 = (f32[32,32]{1,0:T(8,128)S(1)}, f32[32,32]{1,0:T(8,128)}, u32[]{:S(2)}) copy-start(f32[32,32]{1,0:T(8,128)} %refs_1_.6) | copy-start | bytes 12292
  22.1 19.1 %copy-start.12 = (f32[5,32]{1,0:T(8,128)S(1)}, f32[5,32]{1,0:T(8,128)}, u32[]{:S(2)}) copy-start(f32[5,32]{1,0:T(8,128)} %refs_2_.6) | copy-start | bytes 1924
  22.1 24.5 %copy-start.6 = (bf16[512,128]{1,0:T(8,128)(2,1)S(1)}, bf16[512,128]{1,0:T(8,128)(2,1)}, u32[]{:S(2)}) copy-start(bf16[512,128]{1,0:T(8,128)(2,1)} %constant.31.clone.refs_2_) | copy-start | bytes 393220
  22.1 24.5 %copy-start.9 = (bf16[128,256]{1,0:T(8,128)(2,1)S(1)}, bf16[128,256]{1,0:T(8,128)(2,1)}, u32[]{:S(2)}) copy-start(bf16[128,256]{1,0:T(8,128)(2,1)} %constant.30.clone.refs_1_) | copy-start | bytes 196612
  24.8 30.1 %copy-start = (f32[5,96,4,128]{3,2,1,0:T(4,128)S(1)}, f32[5,96,4,128]{3,2,1,0:T(4,128)}, u32[]{:S(2)}) copy-start(f32[5,96,4,128]{3,2,1,0:T(4,128)} %param.19) | copy-start | bytes 2949124
  24.8 30.1 %copy-start.13 = (bf16[128,256]{1,0:T(8,128)(2,1)S(1)}, bf16[128,256]{1,0:T(8,128)(2,1)}, u32[]{:S(2)}) copy-start(bf16[128,256]{1,0:T(8,128)(2,1)} %constant.32.clone.refs_2_) | copy-start | bytes 196612
  28.4 18.1 %all-to-all-start.1 = ((bf16[16,48,256]{2,1,0:T(8,128)(2,1)}), bf16[16,48,256]{2,1,0:T(8,128)(2,1)S(1)}, u32[]{:S(2)}, u32[]{:S(2)}) async-start(bf16[16,48,256]{2,1,0:T(8,128)(2,1)} %get-tuple-element.47), calls=%async_computation.1 | async-start | bytes 786432 | tf_op jit(solution)/shard_map/all_to_all | solution.py:763
  35.5 18.6 %collective-permute-start.2 = (bf16[480,128]{1,0:T(8,128)(2,1)S(1)}, bf16[480,128]{1,0:T(8,128)(2,1)S(1)}, u32[]{:S(2)}, u32[]{:S(2)}) collective-permute-start(bf16[480,128]{1,0:T(8,128)(2,1)S(1)} %get-tuple-element.53), channel_id=1, source_target_pairs={{0,4},{4,8},{8,12},{12,16},{16,20},{20,24},{24,28},{28,32},{32,36}... | collective-permute-start | bytes 368648 | tf_op jit(solution)/shard_map/ppermute | solution.py:768
  37.1 17.1 %collective-permute-start.3 = (bf16[480,128]{1,0:T(8,128)(2,1)S(1)}, bf16[480,128]{1,0:T(8,128)(2,1)S(1)}, u32[]{:S(2)}, u32[]{:S(2)}) collective-permute-start(bf16[480,128]{1,0:T(8,128)(2,1)S(1)} %get-tuple-element.55), channel_id=1, source_target_pairs={{0,60},{4,0},{8,4},{12,8},{16,12},{20,16},{24,20},{28,24},{32,28},... | collective-permute-start | bytes 368648 | tf_op jit(solution)/shard_map/ppermute | solution.py:768
  49.2 16.4 %all-to-all-start.2 = ((bf16[16,96,128]{2,1,0:T(8,128)(2,1)}), bf16[16,96,128]{2,1,0:T(8,128)(2,1)S(1)}, u32[]{:S(2)}, u32[]{:S(2)}) async-start(bf16[16,96,128]{2,1,0:T(8,128)(2,1)} %get-tuple-element.57), calls=%async_computation.2 | async-start | bytes 786432 | tf_op jit(solution)/shard_map/all_to_all | solution.py:763
  60.5 11.9 %collective-permute-start.4 = (bf16[128,128]{1,0:T(8,128)(2,1)}, bf16[128,128]{1,0:T(8,128)(2,1)S(1)}, u32[]{:S(2)}, u32[]{:S(2)}) collective-permute-start(bf16[128,128]{1,0:T(8,128)(2,1)} %get-tuple-element.58), channel_id=1, source_target_pairs={{0,64},{64,128},{128,192},{192,0},{1,65},{65,129},{129,193},{193,1... | collective-permute-start | bytes 98312 | tf_op jit(solution)/shard_map/ppermute | solution.py:768
  62.0 10.5 %collective-permute-start.5 = (bf16[128,128]{1,0:T(8,128)(2,1)}, bf16[128,128]{1,0:T(8,128)(2,1)S(1)}, u32[]{:S(2)}, u32[]{:S(2)}) collective-permute-start(bf16[128,128]{1,0:T(8,128)(2,1)} %get-tuple-element.59), channel_id=1, source_target_pairs={{0,128},{64,192},{128,0},{192,64},{1,129},{65,193},{129,1},{193,65... | collective-permute-start | bytes 98312 | tf_op jit(solution)/shard_map/ppermute | solution.py:768
  64.5 8.0 %collective-permute-start.6 = (bf16[128,128]{1,0:T(8,128)(2,1)}, bf16[128,128]{1,0:T(8,128)(2,1)S(1)}, u32[]{:S(2)}, u32[]{:S(2)}) collective-permute-start(bf16[128,128]{1,0:T(8,128)(2,1)} %get-tuple-element.60), channel_id=1, source_target_pairs={{0,192},{64,0},{128,64},{192,128},{1,193},{65,1},{129,65},{193,129... | collective-permute-start | bytes 98312 | tf_op jit(solution)/shard_map/ppermute | solution.py:768
  66.9 15.1 %all-to-all-start.3 = ((bf16[16,8,384]{2,1,0:T(8,128)(2,1)}), bf16[16,8,384]{2,1,0:T(8,128)(2,1)S(1)}, u32[]{:S(2)}, u32[]{:S(2)}) async-start(bf16[16,8,384]{2,1,0:T(8,128)(2,1)} %shard_map.201), calls=%async_computation.3 | async-start | bytes 196608 | tf_op jit(solution)/shard_map/all_to_all | solution.py:763
  72.8 22.9 %copy-start.8 = (bf16[2,128,128]{2,1,0:T(8,128)(2,1)S(1)}, bf16[2,128,128]{2,1,0:T(8,128)(2,1)}, u32[]{:S(2)}) copy-start(bf16[2,128,128]{2,1,0:T(8,128)(2,1)} %constant.37.clone.refs_1_) | copy-start | bytes 196612
  82.0 32.3 %copy-start.1 = (f32[4,128,1024]{2,1,0:T(8,128)S(1)}, f32[4,128,1024]{2,1,0:T(8,128)}, u32[]{:S(2)}) copy-start(f32[4,128,1024]{2,1,0:T(8,128)} %shard_map.203.refs_2_) | copy-start | bytes 6291460
  82.0 32.3 %copy-start.7 = (bf16[256,256]{1,0:T(8,128)(2,1)S(1)}, bf16[256,256]{1,0:T(8,128)(2,1)}, u32[]{:S(2)}) copy-start(bf16[256,256]{1,0:T(8,128)(2,1)} %constant.38.clone.refs_1_) | copy-start | bytes 393220
  (5 other events, 32.0 us)
